TPU v7x, 256 devices: a whole 4x4x8 slice. The times are simulated.
256 devices in a mesh: sub: 64 (over z, x, core), loc: 4 (over y).
Axes of the slice: x: 4, y: 4, z: 8, core: 2. Of those that a mesh axis runs over, the one named last changes fastest.
Arguments:
- interface_load: float32 [256, 16, 2048], P(('sub', 'loc')), may hold values from -60 to 60
- flexibility: bfloat16 [256, 2048, 2048], P(('sub', 'loc')), may hold values from -2 to 4, as said below
- corner_coupling: float32 [256, 24, 2048], P(('sub', 'loc')), may hold values from -0.125 to 0.125
- coarse_factor: float32 [2048, 2048], P('loc'), may hold values from -3 to 3, as said below
- face_slots: int32 [256, 4, 4], P(('sub', 'loc')), may hold values from -1 to 15, as said below
- corner_map: int32 [256, 24], P(('sub', 'loc')), may hold values from 0 to 2047, as said below
Outputs:
- multipliers: float32 [256, 16, 2048], P(('sub', 'loc'))
- residual: float32 [256, 16, 2048], P(('sub', 'loc'))
Inputs may be any that keep to these rules, and one draw needn't show every extreme that they name: `face_slots`: slots of a face are filled from slot 0; slot c of face d of s is filled exactly when slot c of face d XOR 1 of the neighbour of face d is; a block stands in at most one slot of its subdomain; faces toward no subdomain of the grid are empty (-1); some face has all 4 slots filled. `corner_map`: the 24 entries of a subdomain are distinct. `flexibility`: each subdomain's matrix is symmetric positive definite. `coarse_factor`: lower triangular with a positive diagonal.
All inputs are finite; a program needn't handle non-finite values.
Results may differ from a plain program's by a relative error of at most 0.0038.
Values sent between devices are 32-bit elements; how exact they have to be, the bound alone decides.
No kernel may reach another device: no remote copies, remote signals or barrier semaphores. Data moves between devices by JAX's collectives and lax.ppermute only.
A program may use at most 128 MiB of HBM per device.

v0:
```python
import jax
import jax.numpy as jnp
from jax import lax
from jax.sharding import PartitionSpec as P

BLOCK_ROWS = 128
ITERATIONS = 2


def extended(array, sides, width):
    for axis, dim in sides:
        count, length = (lax.axis_size(axis), array.shape[dim])
        up = [(i, (i + 1) % count) for i in range(count - 1)]
        down = [(j, i) for i, j in up]
        last = lax.slice_in_dim(array, length - width, length, axis=dim)
        leading = lax.slice_in_dim(array, 0, width, axis=dim)
        before = lax.ppermute(last, axis, up)
        after = lax.ppermute(leading, axis, down)
        array = jnp.concatenate([before, array, after], axis=dim)
    return array


def per_device(interface_load, flexibility, corner_coupling, coarse_factor, face_slots, corner_map):
    highest = lax.Precision.HIGHEST
    applied = interface_load[0]
    matrix_local = flexibility[0]
    coupling = corner_coupling[0]
    slots_local = face_slots[0]
    corners_local = corner_map[0]
    case_count, dof_count = applied.shape
    blocks = dof_count // BLOCK_ROWS
    coarse_count = coarse_factor.shape[1]
    slot_table = (slots_local[:, :, None] == jnp.arange(blocks, dtype=jnp.int32)).astype(
        jnp.float32
    )
    paired = jnp.sum(slot_table, axis=(0, 1)) > 0.5
    dof_weight = jnp.repeat(jnp.where(paired, 0.5, 1.0).astype(jnp.float32), BLOCK_ROWS)
    corner_table = (corners_local[:, None] == jnp.arange(coarse_count, dtype=jnp.int32)).astype(
        jnp.float32
    )
    contract_last = (((1,), (1,)), ((), ()))

    def jump_field(values):
        shaped = values.reshape(case_count, blocks, BLOCK_ROWS)
        outgoing = jnp.einsum("fcb,kbx->fkcx", slot_table, shaped, precision=highest)
        from_sub = extended(outgoing[0:2], (("sub", 0),), 1)
        from_loc = extended(outgoing[2:4], (("loc", 0),), 1)
        incoming = jnp.concatenate(
            [from_sub[0:1], from_sub[3:4], from_loc[0:1], from_loc[3:4]], axis=0
        )
        partner = jnp.einsum("fcb,fkcx->kbx", slot_table, incoming, precision=highest)
        return (shaped - partner).reshape(case_count, dof_count)

    def weighted_dot(left_part, right_part):
        return jnp.sum(left_part * right_part * dof_weight[None, :], axis=1)

    def corner_sum(values):
        terms = lax.dot_general(values, coupling, contract_last, precision=highest)
        return jnp.dot(terms, corner_table, precision=highest)

    def residual_stats(residual):
        return (lax.psum(weighted_dot(residual, residual), ("sub", "loc")), None)

    def direction_totals(direction):
        return lax.psum(corner_sum(direction), ("sub", "loc"))

    driven = jump_field(applied)
    multipliers = jnp.zeros_like(driven)
    residual = driven
    direction = driven
    norm_now, res_totals = residual_stats(residual)
    totals = direction_totals(direction)
    for iteration in range(ITERATIONS):
        local_part = jnp.dot(
            direction.astype(jnp.bfloat16), matrix_local, preferred_element_type=jnp.float32
        )
        middle = lax.dot_general(totals, coarse_factor, contract_last, precision=highest)
        solved = lax.psum(jnp.dot(middle, coarse_factor, precision=highest), "loc")
        picked = lax.dot_general(solved, corner_table, contract_last, precision=highest)
        spread = jnp.dot(picked, coupling, precision=highest)
        mapped = jump_field(local_part + spread)
        curvature = lax.psum(weighted_dot(direction, mapped), ("sub", "loc"))
        step_size = norm_now / curvature
        multipliers = multipliers + step_size[:, None] * direction
        residual = residual - step_size[:, None] * mapped
        if iteration + 1 < ITERATIONS:
            norm_next, res_totals = residual_stats(residual)
            beta_ratio = norm_next / norm_now
            direction = residual + beta_ratio[:, None] * direction
            totals = direction_totals(direction)
            norm_now = norm_next
    return (multipliers[None], residual[None])


def solution(mesh):
    in_specs = (
        P(("sub", "loc"), None, None),
        P(("sub", "loc"), None, None),
        P(("sub", "loc"), None, None),
        P("loc", None),
        P(("sub", "loc"), None, None),
        P(("sub", "loc"), None),
    )
    out_specs = (P(("sub", "loc"), None, None), P(("sub", "loc"), None, None))
    return jax.shard_map(
        per_device, mesh=mesh, in_specs=in_specs, out_specs=out_specs, check_vma=False
    )
```

profile of v0, /device:TPU:32, one launch (start us, length us, event | category | flops | bytes accessed | tf_op | source)
XLA Modules:
  0.0 885.7 jit_solution(12954689517485190528)
XLA Ops:
  9.3 1.9 collective-permute-start
  11.2 1.3 collective-permute-start.3
  12.5 4.5 collective-permute-start.2
  17.1 5.2 collective-permute-start.1
  22.3 1.5 collective-permute-done.1
  24.4 1.6 fusion.18
  26.1 244.1 %all-reduce.6.cloned.1.call-done = f32[16,2048]{1,0:T(8,128)} async-done(((f32[16,2048]{1,0:T(8,128)}), f32[16,2048]{1,0:T(8,128)}) %all-reduce.6.cloned.1.call-update) | async-done | bytes 131088 | tf_op jit(solution)/shard_map/psum | solution.py:65
  270.2 5.9 fusion.70
  276.1 2.7 fusion.71
  279.0 4.6 fusion.2
  283.5 39.8 %all-reduce.8.cloned.1.call-done = f32[16,2048]{1,0:T(8,128)} async-done(((f32[16,2048]{1,0:T(8,128)}), f32[16,2048]{1,0:T(8,128)}) %all-reduce.8.cloned.1.call-update) | async-done | bytes 131088 | tf_op jit(solution)/shard_map/psum | solution.py:78
  323.4 1.1 fusion.17
  325.2 1.9 collective-permute-start.4
  327.1 1.3 collective-permute-start.7
  328.4 4.5 collective-permute-start.6
  332.9 5.2 collective-permute-start.5
  338.2 1.5 collective-permute-done.5
  340.2 76.2 %all-reduce = (f32[16]{0:T(128)S(1)}, f32[16]{0:T(128)S(1)}) all-reduce(f32[16]{0:T(128)S(1)} %get-tuple-element.3, f32[16]{0:T(128)S(1)} %get-tuple-element.2), channel_id=1, replica_groups=mesh['sub'=64,'loc'=4] {'sub','loc'}, use_global_device_ids=true, to_apply=%region_2.3 | all-reduce | flops 32 | bytes 256 | tf_op jit(solution)/shard_map/psum | solution.py:62
  416.7 76.8 %psum.60 = f32[16]{0:T(128)S(1)} all-reduce(f32[16]{0:T(128)S(1)} %multiply_reduce_fusion.1), channel_id=1, replica_groups=mesh['sub'=64,'loc'=4] {'sub','loc'}, use_global_device_ids=true, to_apply=%region_8.9 | all-reduce | flops 16 | bytes 128 | tf_op jit(solution)/shard_map/psum | solution.py:62
  493.9 1.0 fusion.16
  495.2 237.1 %all-reduce.10.cloned.1.call-done = f32[16,2048]{1,0:T(8,128)} async-done(((f32[16,2048]{1,0:T(8,128)}), f32[16,2048]{1,0:T(8,128)}) %all-reduce.10.cloned.1.call-update) | async-done | bytes 131088 | tf_op jit(solution)/shard_map/psum | solution.py:65
  732.2 5.9 fusion.72
  738.1 2.7 fusion.73
  740.9 4.6 fusion
  745.4 39.9 %all-reduce.12.cloned.1.call-done = f32[16,2048]{1,0:T(8,128)} async-done(((f32[16,2048]{1,0:T(8,128)}), f32[16,2048]{1,0:T(8,128)}) %all-reduce.12.cloned.1.call-update) | async-done | bytes 131088 | tf_op jit(solution)/shard_map/psum | solution.py:78
  785.3 1.1 fusion.15
  787.1 1.9 collective-permute-start.8
  789.0 1.3 collective-permute-start.11
  790.3 4.5 collective-permute-start.10
  794.9 5.2 collective-permute-start.9
  800.2 1.5 collective-permute-done.9
  802.1 76.2 %psum.63 = f32[16]{0:T(128)S(1)} all-reduce(f32[16]{0:T(128)S(1)} %get-tuple-element.27), channel_id=1, replica_groups=mesh['sub'=64,'loc'=4] {'sub','loc'}, use_global_device_ids=true, to_apply=%region_12.13 | all-reduce | flops 16 | bytes 128 | tf_op jit(solution)/shard_map/psum | solution.py:82
  (53 shorter events, 6.8 us)
Async XLA Ops:
  7.2 17.0 %copy-start = (f32[1,24,2048]{2,1,0:T(8,128)S(1)}, f32[1,24,2048]{2,1,0:T(8,128)}, u32[]{:S(2)}) copy-start(f32[1,24,2048]{2,1,0:T(8,128)} %param.8) | copy-start | bytes 589828
  7.2 263.1 %all-reduce.6.cloned.1.call-start = ((), (), s32[]{:S(2)}) async-start(), calls=%async_computation | async-start | bytes 262144 | tf_op jit(solution)/shard_map/psum | solution.py:65
  9.3 13.0 %collective-permute-start = (f32[1,16,4,128]{3,2,1,0:T(4,128)S(1)}, f32[1,16,4,128]{3,2,1,0:T(4,128)S(1)}, u32[]{:S(2)}, u32[]{:S(2)}) collective-permute-start(f32[1,16,4,128]{3,2,1,0:T(4,128)S(1)} %get-tuple-element.20), channel_id=1, source_target_pairs={{0,4},{4,8},{8,12},{12,16},{16,20},{20,24},{24,28},{28,32},{32,36}... | collective-permute-start | bytes 98312 | tf_op jit(solution)/shard_map/ppermute | solution.py:17
  11.2 11.1 %collective-permute-start.3 = (f32[1,16,4,128]{3,2,1,0:T(4,128)S(1)}, f32[1,16,4,128]{3,2,1,0:T(4,128)S(1)}, u32[]{:S(2)}, u32[]{:S(2)}) collective-permute-start(f32[1,16,4,128]{3,2,1,0:T(4,128)S(1)} %get-tuple-element.21), channel_id=1, source_target_pairs={{1,0},{2,1},{3,2},{5,4},{6,5},{7,6},{9,8},{10,9},{11,10},{13,12},{... | collective-permute-start | bytes 98312 | tf_op jit(solution)/shard_map/ppermute | solution.py:18
  12.5 9.8 %collective-permute-start.2 = (f32[1,16,4,128]{3,2,1,0:T(4,128)S(1)}, f32[1,16,4,128]{3,2,1,0:T(4,128)S(1)}, u32[]{:S(2)}, u32[]{:S(2)}) collective-permute-start(f32[1,16,4,128]{3,2,1,0:T(4,128)S(1)} %get-tuple-element.22), channel_id=1, source_target_pairs={{0,1},{1,2},{2,3},{4,5},{5,6},{6,7},{8,9},{9,10},{10,11},{12,13},{... | collective-permute-start | bytes 98312 | tf_op jit(solution)/shard_map/ppermute | solution.py:17
  17.1 6.8 collective-permute-start.1
  26.1 297.3 %all-reduce.8.cloned.1.call-start = ((), (), s32[]{:S(2)}) async-start(), calls=%async_computation.1 | async-start | bytes 262144 | tf_op jit(solution)/shard_map/psum | solution.py:78
  270.2 5.9 copy-start.1
  278.9 453.3 %all-reduce.10.cloned.1.call-start = ((), (), s32[]{:S(2)}) async-start(), calls=%async_computation.2 | async-start | bytes 262144 | tf_op jit(solution)/shard_map/psum | solution.py:65
  278.9 44.4 %copy-start.3 = (s32[1,24]{1,0:T(1,128)S(1)}, s32[1,24]{1,0:T(1,128)}, u32[]{:S(2)}) copy-start(s32[1,24]{1,0:T(1,128)} %param.11) | copy-start | bytes 292
  325.2 13.0 %collective-permute-start.4 = (f32[1,16,4,128]{3,2,0,1:T(4,128)S(1)}, f32[1,16,4,128]{3,2,0,1:T(4,128)S(1)}, u32[]{:S(2)}, u32[]{:S(2)}) collective-permute-start(f32[1,16,4,128]{3,2,0,1:T(4,128)S(1)} %get-tuple-element.16), channel_id=1, source_target_pairs={{0,4},{4,8},{8,12},{12,16},{16,20},{20,24},{24,28},{28,32},{32,36}... | collective-permute-start | bytes 98312 | tf_op jit(solution)/shard_map/ppermute | solution.py:17
  327.1 11.1 %collective-permute-start.7 = (f32[1,16,4,128]{3,2,0,1:T(4,128)S(1)}, f32[1,16,4,128]{3,2,0,1:T(4,128)S(1)}, u32[]{:S(2)}, u32[]{:S(2)}) collective-permute-start(f32[1,16,4,128]{3,2,0,1:T(4,128)S(1)} %get-tuple-element.17), channel_id=1, source_target_pairs={{1,0},{2,1},{3,2},{5,4},{6,5},{7,6},{9,8},{10,9},{11,10},{13,12},{... | collective-permute-start | bytes 98312 | tf_op jit(solution)/shard_map/ppermute | solution.py:18
  328.4 9.8 %collective-permute-start.6 = (f32[1,16,4,128]{3,2,0,1:T(4,128)S(1)}, f32[1,16,4,128]{3,2,0,1:T(4,128)S(1)}, u32[]{:S(2)}, u32[]{:S(2)}) collective-permute-start(f32[1,16,4,128]{3,2,0,1:T(4,128)S(1)} %get-tuple-element.18), channel_id=1, source_target_pairs={{0,1},{1,2},{2,3},{4,5},{5,6},{6,7},{8,9},{9,10},{10,11},{12,13},{... | collective-permute-start | bytes 98312 | tf_op jit(solution)/shard_map/ppermute | solution.py:17
  332.9 6.8 collective-permute-start.5
  494.9 290.4 %all-reduce.12.cloned.1.call-start = ((), (), s32[]{:S(2)}) async-start(), calls=%async_computation.3 | async-start | bytes 262144 | tf_op jit(solution)/shard_map/psum | solution.py:78
  732.2 5.9 copy-start.2
  787.1 13.1 %collective-permute-start.8 = (f32[1,16,4,128]{3,2,0,1:T(4,128)S(1)}, f32[1,16,4,128]{3,2,0,1:T(4,128)S(1)}, u32[]{:S(2)}, u32[]{:S(2)}) collective-permute-start(f32[1,16,4,128]{3,2,0,1:T(4,128)S(1)} %get-tuple-element.12), channel_id=1, source_target_pairs={{0,4},{4,8},{8,12},{12,16},{16,20},{20,24},{24,28},{28,32},{32,36}... | collective-permute-start | bytes 98312 | tf_op jit(solution)/shard_map/ppermute | solution.py:17
  789.0 11.1 %collective-permute-start.11 = (f32[1,16,4,128]{3,2,0,1:T(4,128)S(1)}, f32[1,16,4,128]{3,2,0,1:T(4,128)S(1)}, u32[]{:S(2)}, u32[]{:S(2)}) collective-permute-start(f32[1,16,4,128]{3,2,0,1:T(4,128)S(1)} %get-tuple-element.13), channel_id=1, source_target_pairs={{1,0},{2,1},{3,2},{5,4},{6,5},{7,6},{9,8},{10,9},{11,10},{13,12},{... | collective-permute-start | bytes 98312 | tf_op jit(solution)/shard_map/ppermute | solution.py:18
  790.3 9.8 %collective-permute-start.10 = (f32[1,16,4,128]{3,2,0,1:T(4,128)S(1)}, f32[1,16,4,128]{3,2,0,1:T(4,128)S(1)}, u32[]{:S(2)}, u32[]{:S(2)}) collective-permute-start(f32[1,16,4,128]{3,2,0,1:T(4,128)S(1)} %get-tuple-element.14), channel_id=1, source_target_pairs={{0,1},{1,2},{2,3},{4,5},{5,6},{6,7},{8,9},{9,10},{10,11},{12,13},{... | collective-permute-start | bytes 98312 | tf_op jit(solution)/shard_map/ppermute | solution.py:17
  794.9 6.8 collective-permute-start.9
Sparse Core Ops, SparseCore 0:
  26.2 244.0 all-reduce.5
  279.0 44.2 all-reduce.7
  495.0 237.1 all-reduce.9
  741.0 44.2 all-reduce.11
where the time goes:
time: 891 us; the launch traced here: 886 us
  waiting for transfers between devices  565 us (63%)
  blocking collectives  229 us (26%)
  starting transfers between devices  39.2 us (4%)
  matrix products  34.3 us (4%)
  between operations  14.1 us (2%)
    psum x2, waiting for transfers between devices, direction_totals(): return lax.psum(corner_sum(direction), ('sub', 'loc'))  481 us
    psum x2, blocking collectives, residual_stats(): return (lax.psum(weighted_dot(residual, residual), ('sub', 'loc')), None)  153 us
    psum x2, waiting for transfers between devices, per_device(): solved = lax.psum(jnp.dot(middle, coarse_factor, precision=highest), 'loc')  79.7 us
    psum x1, blocking collectives, per_device(): curvature = lax.psum(weighted_dot(direction, mapped), ('sub', 'loc'))  76.2 us
    ppermute x6, starting transfers between devices, extended(): after = lax.ppermute(leading, axis, down)  19.5 us
    ppermute x6, starting transfers between devices, extended(): before = lax.ppermute(last, axis, up)  19.4 us
  transfers between devices with their start and end apart: 16, of which 7 were waited for; matrix products, arithmetic and copies ran while one was open for 1% of the time, Pallas kernels for 0%

commit v1 on v0

v1 whole, which is shorter than its diff:
```python
import functools

import jax
import jax.numpy as jnp
from jax import lax
from jax.experimental import pallas as pl
from jax.experimental.pallas import tpu as pltpu
from jax.sharding import Mesh, PartitionSpec as P

BW = 128
LANES = 32
NORM, CROSS, SQUARE, LOCAL = 24, 25, 26, 27
RADIX = 256
F32, BF16 = jnp.float32, jnp.bfloat16
ALL = ("z", "x", "c", "y")
SUB = ("z", "x", "c")

NN = (((1,), (0,)), ((), ()))
NT = (((1,), (1,)), ((), ()))

VMEM = pl.BlockSpec(memory_space=pltpu.VMEM)
SMEM = pl.BlockSpec(memory_space=pltpu.SMEM)


def params(mib):
    return pltpu.CompilerParams(vmem_limit_bytes=mib * 1024 * 1024)


def split(x):
    hi = x.astype(BF16)
    return hi, (x - hi.astype(F32)).astype(BF16)


def dot(a, b, dims):
    return lax.dot_general(a, b, dims, preferred_element_type=F32)


def dot3(a, b_hi, b_lo, dims):
    rows = a.shape[0]
    a_hi, a_lo = split(a)
    both = dot(jnp.concatenate([a_hi, a_lo], axis=0), b_hi, dims)
    return both[:rows] + both[rows:] + dot(a_hi, b_lo, dims)


def block_at(b):
    return pl.ds(pl.multiple_of(jnp.maximum(b, 0) * BW, BW), BW)


def subtract_faces(ref, slots, incoming):
    for f in range(4):
        for c in range(4):
            b = slots[f, c]
            at = block_at(b)
            held = ref[:, at]
            got = incoming[f][0:16, c * BW : (c + 1) * BW]
            ref[:, at] = jnp.where(b >= 0, held - got, held)


def pack_faces(values, slots, outs, row0):
    rows = values.shape[0]
    for f in range(4):
        for c in range(4):
            outs[f][row0 : row0 + rows, c * BW : (c + 1) * BW] = values[:, block_at(slots[f, c])]


def lane_sum(x):
    return jnp.sum(x, axis=1, keepdims=True)


def place(lane, y, slot, column):
    return jnp.where(lane == y * LANES + slot, column, 0.0)


def first_pack(slots, corners, y_ref, load, o0, o1, o2, o3, cm_row):
    pack_faces(load, slots, (o0, o1, o2, o3), 0)
    lane = lax.broadcasted_iota(jnp.int32, (8, BW), 1)
    base = y_ref[0] * LANES
    row = jnp.zeros((8, BW), jnp.int32)
    for j in range(corners.shape[1]):
        row = jnp.where(lane == base + j, corners[0, j], row)
    row = row.astype(F32)
    cm_row[...] = row
    for o in (o0, o1):
        o[16:24, 0:BW] = row
        o[16:24, BW:] = jnp.zeros((8, 3 * BW), F32)


def prepare(slots, y_ref, coupling, factor, bx_hi, bx_lo, weight, f_hi, f_lo, bx):
    bx[...] = jnp.zeros_like(bx)
    bx[pl.ds(pl.multiple_of(y_ref[0] * LANES, LANES), 24), :] = coupling[...]
    hi, lo = split(bx[...])
    bx_hi[...] = hi
    bx_lo[...] = lo
    weight[...] = jnp.ones_like(weight)
    for f in range(4):
        for c in range(4):
            b = slots[f, c]
            at = block_at(b)
            weight[:, at] = jnp.where(b >= 0, jnp.full((8, BW), 0.5, F32), weight[:, at])
    hi, lo = split(factor[...])
    f_hi[...] = hi
    f_lo[...] = lo


def first_vector(slots, y_ref, load, i0, i1, i2, i3, bx_hi, bx_lo, weight, cm_row, v0, pay):
    v0[...] = load[...]
    subtract_faces(v0, slots, (i0, i1, i2, i3))
    v = v0[...]
    norm = lane_sum(v * v * weight[0:1, :])
    lane = lax.broadcasted_iota(jnp.int32, (16, BW), 1)
    pay[0:16, :] = dot3(v, bx_hi[...], bx_lo[...], NT) + place(lane, y_ref[0], NORM, norm)
    row = lax.broadcasted_iota(jnp.int32, (8, BW), 0)
    own, up, down = (cm_row[0:1, :], i0[16:17, 0:BW], i1[16:17, 0:BW])
    pay[16:24, :] = jnp.where(
        row == 0, own, jnp.where(row == 1, up, jnp.where(row == 2, down, 0.0))
    )


def local_product(first, slots, y_ref, v, mat, *rest):
    if first:
        coupling, z, o0, o1, o2, o3, pieces = rest
    else:
        z, o0, o1, o2, o3, dot_out, pieces = rest
    step = pl.program_id(0)
    width = mat.shape[1]

    @pl.when(step == 0)
    def _():
        hi, lo = split(v[...])
        pieces[0:16, :] = hi
        pieces[16:32, :] = lo

    both = dot(pieces[...], mat[...], NN)
    z[:, pl.ds(pl.multiple_of(step * width, width), width)] = both[:16] + both[16:]

    @pl.when(step == pl.num_programs(0) - 1)
    def _():
        pack_faces(z, slots, (o0, o1, o2, o3), 0)
        if first:
            pack_faces(coupling, slots, (o0, o1, o2, o3), 16)
        else:
            lane = lax.broadcasted_iota(jnp.int32, (16, BW), 1)
            dot_out[...] = place(lane, y_ref[0], LOCAL, lane_sum(v[...] * z[...]))


def jumped_coupling(slots, y_ref, coupling, i0, i1, i2, i3, b_hi, b_lo, full):
    y = y_ref[0]
    full[...] = jnp.zeros_like(full)

    def rows(group, col):
        return pl.ds(pl.multiple_of(group * BW + col * LANES, LANES), 24)

    full[rows(0, y), :] = coupling[...]
    places = (rows(1, y), rows(2, y), rows(0, jnp.maximum(y - 1, 0)), rows(0, jnp.minimum(y + 1, 3)))
    for f, got in enumerate((i0, i1, i2, i3)):
        for c in range(4):
            b = slots[f, c]
            at = block_at(b)
            held = full[places[f], at]
            full[places[f], at] = jnp.where(b >= 0, -got[16:40, c * BW : (c + 1) * BW], held)
    hi, lo = split(full[...])
    b_hi[...] = hi
    b_lo[...] = lo


def picked_columns(pay, f_hi, f_lo, c_hi, c_lo):
    dofs = f_hi.shape[1]
    wanted = jnp.concatenate([pay[16:17, :], pay[17:18, :], pay[18:19, :]], axis=1)
    row = lax.broadcasted_iota(jnp.int32, (dofs, 3 * BW), 0)
    hot = (row == wanted.astype(jnp.int32)).astype(F32).astype(BF16)
    c_hi[...] = dot(f_hi[...], hot, NN).astype(BF16)
    c_lo[...] = dot(f_lo[...], hot, NN).astype(BF16)


def coarse(final, y_ref, ta, tb, ma, mb, f_hi, f_lo, c_hi, c_lo, part, scal, spread_rows, hot):
    groups = ta.shape[0]
    digits = f_hi.shape[1] // RADIX
    half = digits * 16
    lane = lax.broadcasted_iota(jnp.int32, (16, BW), 1)
    slot = lane % LANES
    low = lax.broadcasted_iota(jnp.int32, (RADIX, BW), 0)
    total = jnp.zeros((16, BW), F32)
    for n, (t, m) in enumerate(((ta, ma), (tb, mb))):

        def body(j, acc):
            terms = t[j, 0:16, :]
            dof = m[j, 16:17, :].astype(jnp.int32)
            top = jnp.where(slot < 24, jnp.broadcast_to(dof // RADIX, (16, BW)), -1)
            hi = terms.astype(BF16).astype(F32)
            lo = terms - hi
            at = pl.ds(pl.multiple_of((n * groups + j) * BW, BW), BW)
            for d in range(digits):
                mine = top == d
                spread_rows[d * 16 : d * 16 + 16, at] = jnp.where(mine, hi, 0.0).astype(BF16)
                spread_rows[half + d * 16 : half + d * 16 + 16, at] = jnp.where(
                    mine, lo, 0.0
                ).astype(BF16)
            hot[:, at] = (low == dof % RADIX).astype(F32).astype(BF16)
            return acc + terms

        total = lax.fori_loop(0, groups, body, total, unroll=4)
    sums = dot(spread_rows[...], hot[...], NT)
    sums = sums[:half] + sums[half:]
    rhs = jnp.concatenate([sums[d * 16 : d * 16 + 16, :] for d in range(digits)], axis=1)
    mid = dot3(rhs, f_hi[...], f_lo[...], NT)
    picked = dot3(mid, c_hi[...], c_lo[...], NN)

    def over(which):
        return lane_sum(jnp.where(which, total, 0.0))

    if final:
        own = lane == y_ref[0] * LANES + LOCAL
        energy = over(own) + lane_sum(mid * mid)
        wide = lax.broadcasted_iota(jnp.int32, picked.shape, 1)
        picked = jnp.where(wide == NORM, energy, picked)
        scal[...] = jnp.where(lane == 0, over(slot == CROSS), over(slot == SQUARE))
    else:
        scal[...] = jnp.broadcast_to(over(slot == NORM), (16, BW))
    part[...] = picked


def next_vector(
    slots, y_ref, z0, i0, i1, i2, i3, p0, p1, p2, p3, b_hi, b_lo, v0, bx_hi, bx_lo, weight, v1, pay
):
    picked = (p0[...] + p1[...]) + (p2[...] + p3[...])
    v1[...] = z0[...] + dot3(picked, b_hi[...], b_lo[...], NN)
    subtract_faces(v1, slots, (i0, i1, i2, i3))
    v = v1[...]
    w = v * weight[0:1, :]
    lane = lax.broadcasted_iota(jnp.int32, (16, BW), 1)
    y = y_ref[0]
    pay[...] = (
        dot3(v, bx_hi[...], bx_lo[...], NT)
        + place(lane, y, CROSS, lane_sum(v0[...] * w))
        + place(lane, y, SQUARE, lane_sum(v * w))
    )


def finish(slots, z1, i0, i1, i2, i3, p0, p1, p2, p3, b_hi, b_lo, v0, v1, s0, s1, mult, resid):
    picked = (p0[...] + p1[...]) + (p2[...] + p3[...])
    resid[...] = z1[...] + dot3(picked, b_hi[...], b_lo[...], NN)
    subtract_faces(resid, slots, (i0, i1, i2, i3))
    norm, cross, square = (s0[:, 0:1], s1[:, 0:1], s1[:, 1:2])
    energy = picked[:, NORM : NORM + 1]
    step1 = norm / cross
    fresh = norm - 2.0 * step1 * cross + step1 * step1 * square
    c = 1.0 + fresh / norm
    curvature = c * c * cross - 2.0 * c * step1 * square + step1 * step1 * energy
    step2 = fresh / curvature
    first, second = (v0[...], v1[...])
    mult[...] = (step1 + step2 * c) * first - (step2 * step1) * second
    resid[...] = first - (step1 + step2 * c) * second + (step2 * step1) * resid[...]


def call(kernel, name, ins, outs, scratch=(), mib=32, specs=None):
    return pl.pallas_call(
        kernel,
        out_shape=[jax.ShapeDtypeStruct(s, d) for s, d in outs],
        in_specs=specs,
        out_specs=[VMEM] * len(outs),
        scratch_shapes=[pltpu.VMEM(s, d) for s, d in scratch],
        compiler_params=params(mib),
        name=name,
    )(*ins)


def per_device(interface_load, flexibility, corner_coupling, coarse_factor, face_slots, corner_map):
    load = interface_load[0]
    matrix = flexibility[0]
    coupling = corner_coupling[0]
    slots = face_slots[0]
    cases, dofs = load.shape
    owned, coarse_dofs = coarse_factor.shape
    corners = coupling.shape[0]
    zs, xs = (lax.axis_size("z"), lax.axis_size("x"))
    subs = zs * xs * lax.axis_size("c")
    ys = lax.axis_size("y")
    face = 4 * BW
    y = lax.axis_index("y").astype(jnp.int32).reshape(1)

    def neighbours(o0, o1, o2, o3):
        back = [(i + 1, i) for i in range(subs - 1)]
        ahead = [(i, i + 1) for i in range(subs - 1)]
        left = [(j + 1, j) for j in range(ys - 1)]
        right = [(j, j + 1) for j in range(ys - 1)]
        return (
            lax.ppermute(o1, SUB, ahead),
            lax.ppermute(o0, SUB, back),
            lax.ppermute(o3, "y", right),
            lax.ppermute(o2, "y", left),
        )

    def others(p):
        return [lax.ppermute(p, "y", [(j, (j + k) % ys) for j in range(ys)]) for k in range(1, ys)]

    def gather_sub(p):
        every = jnp.broadcast_to(p[None], (zs * xs,) + p.shape)
        mine = lax.all_to_all(every, ("z", "x"), 0, 0)
        return mine, lax.ppermute(mine, "c", [(0, 1), (1, 0)])

    *faces, cm_row = call(
        first_pack,
        "first_pack",
        (slots, corner_map, y, load),
        [((24, face), F32)] * 2 + [((16, face), F32)] * 2 + [((8, BW), F32)],
        specs=[SMEM, SMEM, SMEM, VMEM],
    )
    got = neighbours(*faces)
    bx_hi, bx_lo, weight, f_hi, f_lo = call(
        prepare,
        "prepare",
        (slots, y, coupling, coarse_factor),
        [((BW, dofs), BF16)] * 2 + [((8, dofs), F32)] + [((owned, coarse_dofs), BF16)] * 2,
        [((BW, dofs), F32)],
        specs=[SMEM, SMEM, VMEM, VMEM],
    )
    v0, pay = call(
        first_vector,
        "first_vector",
        (slots, y, load, *got, bx_hi, bx_lo, weight, cm_row),
        [((cases, dofs), F32), ((24, BW), F32)],
        specs=[SMEM, SMEM] + [VMEM] * 9,
    )

    def product(first, v):
        width = 256
        rows = 40 if first else 16
        whole = pl.BlockSpec((cases, dofs), lambda j: (0, 0))
        outs = [((cases, dofs), F32)] + [((rows, face), F32)] * 4
        if not first:
            outs = outs + [((cases, BW), F32)]
        ins = (slots, y, v, matrix) + ((coupling,) if first else ())
        in_specs = [SMEM, SMEM, whole, pl.BlockSpec((dofs, width), lambda j: (0, j))]
        if first:
            in_specs = in_specs + [pl.BlockSpec((corners, dofs), lambda j: (0, 0))]
        return pl.pallas_call(
            functools.partial(local_product, first),
            grid=(dofs // width,),
            out_shape=[jax.ShapeDtypeStruct(s, d) for s, d in outs],
            in_specs=in_specs,
            out_specs=[pl.BlockSpec(s, lambda j: (0, 0)) for s, _ in outs],
            scratch_shapes=[pltpu.VMEM((2 * cases, dofs), BF16)],
            compiler_params=params(32),
            name="local_product",
        )(*ins)

    def solve(final, t, m):
        groups = 2 * t[0].shape[0]
        return call(
            functools.partial(coarse, final),
            "coarse",
            (y, *t, *m, f_hi, f_lo, c_hi, c_lo),
            [((cases, 3 * BW), F32), ((cases, BW), F32)],
            [
                ((2 * cases * (coarse_dofs // RADIX), groups * BW), BF16),
                ((RADIX, groups * BW), BF16),
            ],
            specs=[SMEM] + [VMEM] * 8,
        )

    row = sum(others(pay), pay)
    gathered = gather_sub(row)
    z0, *faces = product(True, v0)
    c_hi, c_lo = call(
        picked_columns,
        "picked_columns",
        (row, f_hi, f_lo),
        [((owned, 3 * BW), BF16)] * 2,
        specs=[VMEM] * 3,
    )
    got = neighbours(*faces)
    b_hi, b_lo = call(
        jumped_coupling,
        "jumped_coupling",
        (slots, y, coupling, *got),
        [((3 * BW, dofs), BF16)] * 2,
        [((3 * BW, dofs), F32)],
        specs=[SMEM, SMEM] + [VMEM] * 5,
    )
    part, scal0 = solve(False, gathered, gathered)
    v1, pay = call(
        next_vector,
        "next_vector",
        (slots, y, z0, *got, part, *others(part), b_hi, b_lo, v0, bx_hi, bx_lo, weight),
        [((cases, dofs), F32), ((cases, BW), F32)],
        specs=[SMEM, SMEM] + [VMEM] * 15,
    )
    z1, *faces, local_dot = product(False, v1)
    row = sum(others(pay), pay) + local_dot
    later = gather_sub(row)
    got = neighbours(*faces)
    part, scal1 = solve(True, later, gathered)
    mult, resid = call(
        finish,
        "finish",
        (slots, z1, *got, part, *others(part), b_hi, b_lo, v0, v1, scal0, scal1),
        [((cases, dofs), F32)] * 2,
        specs=[SMEM] + [VMEM] * 15,
    )
    return mult[None], resid[None]


def solution(mesh):
    fine = Mesh(mesh.devices.reshape(8, 4, 2, 4), ALL)
    in_specs = (
        P(ALL, None, None),
        P(ALL, None, None),
        P(ALL, None, None),
        P("y", None),
        P(ALL, None, None),
        P(ALL, None),
    )
    out_specs = (P(ALL, None, None), P(ALL, None, None))
    return jax.shard_map(
        per_device, mesh=fine, in_specs=in_specs, out_specs=out_specs, check_vma=False
    )
```

time: 891 us -> 148 us (0.17)
  waiting for transfers between devices: 565 us -> 10.4 us
  blocking collectives: 229 us -> 37.7 us
  matrix products: 34.3 us -> 0 us
  Pallas kernels: 0 us -> 34.2 us
  starting transfers between devices: 39.2 us -> 55.3 us
  between operations: 14.1 us -> 0.92 us
    psum x4 -> x0, waiting for transfers between devices: 561 us -> none  [the longest x2 481 us: direction_totals(): return lax.psum(corner_sum(direction), ('sub', 'loc'))]
    psum x3 -> x0, blocking collectives: 229 us -> none  [the longest x2 153 us: residual_stats(): return (lax.psum(weighted_dot(residual, residual), ('sub', 'loc')), None)]
    all_to_all x0 -> x2, blocking collectives: none -> 37.7 us  [gather_sub(): mine = lax.all_to_all(every, ('z', 'x'), 0, 0)]
    dot_general x20 -> x0, matrix products: 34.3 us -> none  [the longest x2 11.7 us: per_device(): lax.dot_general(totals, coarse_factor, contract_last, precision=highest)]
    pallas_call x0 -> x11, Pallas kernels: none -> 34.2 us  [the longest x9 26.1 us: call(): pl.pallas_call(kernel, out_shape=[jax.ShapeDtypeStruct(s, d) for s, d in...]
    ppermute x12 -> x26, starting transfers between devices: 38.9 us -> 55.3 us  [the longest x12 20.2 us: others(): lax.ppermute(p, 'y', [(j, (j + k) % ys) for j in range(ys)])]
  transfers between devices with their start and end apart: 16 -> 26, of which waited for: 7 -> 7; matrix products, arithmetic and copies ran while one was open for 1% -> 0% of each run, Pallas kernels for 0% -> 20%
where the time goes in v1:
time: 148 us; the launch traced here: 147 us
  starting transfers between devices  55.3 us (37%)
  blocking collectives  37.7 us (25%)
  Pallas kernels  34.2 us (23%)
  waiting for transfers between devices  10.4 us (7%)
  local copies, waits for them, and re-layouts  8.81 us (6%)
    all_to_all x2, blocking collectives, gather_sub(): mine = lax.all_to_all(every, ('z', 'x'), 0, 0)  37.7 us
    pallas_call x9, Pallas kernels, call(): pl.pallas_call(kernel, out_shape=[jax.ShapeDtypeStruct(s, d) for s, d in...  26.1 us
    ppermute x12, starting transfers between devices, others(): lax.ppermute(p, 'y', [(j, (j + k) % ys) for j in range(ys)])  20.2 us
    ppermute x3, starting transfers between devices, neighbours(): lax.ppermute(o0, SUB, back)  16.3 us
    ppermute x12, waiting for transfers between devices, others(): lax.ppermute(p, 'y', [(j, (j + k) % ys) for j in range(ys)])  10.3 us
    unnamed x22, local copies, waits for them, and re-layouts  8.76 us
    ppermute x3, starting transfers between devices, neighbours(): lax.ppermute(o3, 'y', right)  8.24 us
    pallas_call x2, Pallas kernels, product(): pl.pallas_call(functools.partial(local_product, first), grid=(dofs // wid...  8.14 us
  transfers between devices with their start and end apart: 26, of which 7 were waited for; matrix products, arithmetic and copies ran while one was open for 0% of the time, Pallas kernels for 20%

profile of v1, /device:TPU:32, one launch (start us, length us, event | category | flops | bytes accessed | tf_op | source)
XLA Modules:
  0.0 147.4 jit_solution(3769644978020915102)
XLA Ops:
  3.5 1.9 %collective-permute-start = (f32[24,512]{1,0:T(8,128)S(1)}, f32[24,512]{1,0:T(8,128)S(1)}, u32[]{:S(2)}, u32[]{:S(2)}) collective-permute-start(f32[24,512]{1,0:T(8,128)S(1)} %get-tuple-element.37), channel_id=1, source_target_pairs={{0,4},{4,8},{8,12},{12,16},{16,20},{20,24},{24,28},{28,32},{32,36}... | collective-permute-start | bytes 147464 | tf_op jit(solution)/shard_map/ppermute | solution.py:287
  5.4 5.8 %collective-permute-start.1 = (f32[24,512]{1,0:T(8,128)S(1)}, f32[24,512]{1,0:T(8,128)S(1)}, u32[]{:S(2)}, u32[]{:S(2)}) collective-permute-start(f32[24,512]{1,0:T(8,128)S(1)} %get-tuple-element.38), channel_id=1, source_target_pairs={{4,0},{8,4},{12,8},{16,12},{20,16},{24,20},{28,24},{32,28},{36,32}... | collective-permute-start | bytes 147464 | tf_op jit(solution)/shard_map/ppermute | solution.py:288
  11.2 3.5 %collective-permute-start.2 = (f32[16,512]{1,0:T(8,128)S(1)}, f32[16,512]{1,0:T(8,128)S(1)}, u32[]{:S(2)}, u32[]{:S(2)}) collective-permute-start(f32[16,512]{1,0:T(8,128)S(1)} %get-tuple-element.39), channel_id=1, source_target_pairs={{0,1},{1,2},{2,3},{4,5},{5,6},{6,7},{8,9},{9,10},{10,11},{12,13},{... | collective-permute-start | bytes 98312 | tf_op jit(solution)/shard_map/ppermute | solution.py:289
  14.7 1.3 collective-permute-start.3
  16.0 2.2 %copy-done.1 = f32[512,2048]{1,0:T(8,128)S(1)} copy-done((f32[512,2048]{1,0:T(8,128)S(1)}, f32[512,2048]{1,0:T(8,128)}, u32[]{:S(2)}) %copy-start.1) | copy-done | bytes 4194328
  19.1 2.1 %prepare.1 = (bf16[128,2048]{1,0:T(8,128)(2,1)S(1)}, bf16[128,2048]{1,0:T(8,128)(2,1)S(1)}, f32[8,2048]{1,0:T(8,128)S(1)}, bf16[512,2048]{1,0:T(8,128)(2,1)S(1)}, bf16[512,2048]{1,0:T(8,128)(2,1)S(1)}) custom-call(s32[4,4]{1,0:T(4,128)S(1)} %bitcast.17, s32[1]{0:T(128)} %bitcast.1.y_ref, f32[24,2048]{1,0:T(8,128)S(1)} %bitcast.11, f32[512,2048]{1,0:T(8,128)S(1)} %copy-done.1), custom_call_target="tpu_custom_call" | custom-call | tf_op jit(solution)/shard_map/prepare/pallas_call | solution.py:256
  22.3 4.1 %collective-permute-start.10 = (f32[24,128]{1,0:T(8,128)S(1)}, f32[24,128]{1,0:T(8,128)S(1)}, u32[]{:S(2)}, u32[]{:S(2)}) collective-permute-start(f32[24,128]{1,0:T(8,128)S(1)} %get-tuple-element.51), channel_id=1, source_target_pairs={{0,3},{1,0},{2,1},{3,2},{4,7},{5,4},{6,5},{7,6},{8,11},{9,8},{10,9... | collective-permute-start | bytes 36872 | tf_op jit(solution)/shard_map/ppermute | solution.py:294
  28.1 3.6 %collective-permute-done.9 = f32[24,128]{1,0:T(8,128)S(1)} collective-permute-done((f32[24,128]{1,0:T(8,128)S(1)}, f32[24,128]{1,0:T(8,128)S(1)}, u32[]{:S(2)}, u32[]{:S(2)}) %collective-permute-start.9) | collective-permute-done | bytes 12320 | tf_op jit(solution)/shard_map/ppermute | solution.py:294
  32.0 21.7 %all_to_all.10.ta.ma = f32[32,24,128]{2,1,0:T(8,128)S(1)} all-to-all(f32[32,24,128]{2,1,0:T(8,128)S(1)} %broadcast_in_dim.8), channel_id=1, replica_groups=mesh['z'=8,'x'=4,'c'=2,'y'=4] {'z','x'}, dimensions={0} | all-to-all | bytes 786432 | tf_op jit(solution)/shard_map/all_to_all | solution.py:298
  53.7 3.4 %copy-done = bf16[1,2048,2048]{2,1,0:T(8,128)(2,1)S(1)} copy-done((bf16[1,2048,2048]{2,1,0:T(8,128)(2,1)S(1)}, bf16[1,2048,2048]{2,1,0:T(8,128)(2,1)}, u32[]{:S(2)}) %copy-start) | copy-done | bytes 8388632
  57.1 4.1 %local_product.2 = (f32[16,2048]{1,0:T(8,128)S(1)}, f32[40,512]{1,0:T(8,128)S(1)}, f32[40,512]{1,0:T(8,128)S(1)}, f32[40,512]{1,0:T(8,128)S(1)}, f32[40,512]{1,0:T(8,128)S(1)}) custom-call(s32[4,4]{1,0:T(4,128)S(1)} %bitcast.19, s32[1]{0:T(128)} %bitcast.1.y_ref, f32[16,2048]{1,0:T(8,128)S(1)} %get-tuple-element.45.v.v0, bf16[2048,2048]{1,0:T(8,128)(2,1)S(1)} %bitcast.7, ...), custom_call_target="tpu_custom_call" | custom-call | tf_op jit(solution)/shard_map/local_product/pallas_call | solution.py:336
  61.1 2.4 %collective-permute-start.4 = (f32[40,512]{1,0:T(8,128)S(1)}, f32[40,512]{1,0:T(8,128)S(1)}, u32[]{:S(2)}, u32[]{:S(2)}) collective-permute-start(f32[40,512]{1,0:T(8,128)S(1)} %get-tuple-element.47), channel_id=1, source_target_pairs={{0,4},{4,8},{8,12},{12,16},{16,20},{20,24},{24,28},{28,32},{32,36}... | collective-permute-start | bytes 245768 | tf_op jit(solution)/shard_map/ppermute | solution.py:287
  63.6 5.3 %collective-permute-start.5 = (f32[40,512]{1,0:T(8,128)S(1)}, f32[40,512]{1,0:T(8,128)S(1)}, u32[]{:S(2)}, u32[]{:S(2)}) collective-permute-start(f32[40,512]{1,0:T(8,128)S(1)} %get-tuple-element.48), channel_id=1, source_target_pairs={{4,0},{8,4},{12,8},{16,12},{20,16},{24,20},{28,24},{32,28},{36,32}... | collective-permute-start | bytes 245768 | tf_op jit(solution)/shard_map/ppermute | solution.py:288
  68.8 1.7 %collective-permute-start.6 = (f32[40,512]{1,0:T(8,128)S(1)}, f32[40,512]{1,0:T(8,128)S(1)}, u32[]{:S(2)}, u32[]{:S(2)}) collective-permute-start(f32[40,512]{1,0:T(8,128)S(1)} %get-tuple-element.49), channel_id=1, source_target_pairs={{0,1},{1,2},{2,3},{4,5},{5,6},{6,7},{8,9},{9,10},{10,11},{12,13},{... | collective-permute-start | bytes 245768 | tf_op jit(solution)/shard_map/ppermute | solution.py:289
  70.5 1.3 collective-permute-start.7
  71.8 2.4 %picked_columns.1 = (bf16[512,384]{1,0:T(8,128)(2,1)S(1)}, bf16[512,384]{1,0:T(8,128)(2,1)S(1)}) custom-call(f32[24,128]{1,0:T(8,128)S(1)} %add_add_fusion.pay, bf16[512,2048]{1,0:T(8,128)(2,1)S(1)} %get-tuple-element.52.f_hi, bf16[512,2048]{1,0:T(8,128)(2,1)S(1)} %get-tuple-element.53.f_lo), custom_call_target="tpu_custom_call" | custom-call | tf_op jit(solution)/shard_map/picked_columns/pallas_call | solution.py:256
  74.2 7.4 %coarse.2 = (f32[16,384]{1,0:T(8,128)S(1)}, f32[16,128]{1,0:T(8,128)S(1)}) custom-call(s32[1]{0:T(128)} %bitcast.1.y_ref, f32[32,24,128]{2,1,0:T(8,128)S(1)} %all_to_all.10.ta.ma, f32[32,24,128]{2,1,0:T(8,128)S(1)} %collective-permute-done.11.tb.mb, f32[32,24,128]{2,1,0:T(8,128)S(1)} %all_to_all.10.ta.ma, f32[32,24,128]{2,1,0:T(8,128)S(1)} %collective-permute-done.11.tb.mb, ...), custom_call_target="tpu_custom_call" | custom-call | tf_op jit(solution)/shard_map/coarse/pallas_call | solution.py:256
  81.6 3.4 %collective-permute-start.14 = (f32[16,384]{1,0:T(8,128)S(1)}, f32[16,384]{1,0:T(8,128)S(1)}, u32[]{:S(2)}, u32[]{:S(2)}) collective-permute-start(f32[16,384]{1,0:T(8,128)S(1)} %get-tuple-element.56.p0), channel_id=1, source_target_pairs={{0,3},{1,0},{2,1},{3,2},{4,7},{5,4},{6,5},{7,6},{8,11},{9,8},{10,9... | collective-permute-start | bytes 73736 | tf_op jit(solution)/shard_map/ppermute | solution.py:294
  85.0 1.4 collective-permute-start.13
  86.4 1.3 collective-permute-start.12
  87.7 1.6 %jumped_coupling.1 = (bf16[384,2048]{1,0:T(8,128)(2,1)S(1)}, bf16[384,2048]{1,0:T(8,128)(2,1)S(1)}) custom-call(s32[4,4]{1,0:T(4,128)S(1)} %bitcast.20, s32[1]{0:T(128)} %bitcast.1.y_ref, f32[24,2048]{1,0:T(8,128)S(1)} %bitcast.13, f32[40,512]{1,0:T(8,128)S(1)} %collective-permute-done.4.i0, f32[40,512]{1,0:T(8,128)S(1)} %collective-permute-done.5.i1, ...), custom_call_target="tpu_custom_call" | custom-call | tf_op jit(solution)/shard_map/jumped_coupling/pallas_call | solution.py:256
  91.4 1.6 %next_vector.1 = (f32[16,2048]{1,0:T(8,128)S(1)}, f32[16,128]{1,0:T(8,128)S(1)}) custom-call(s32[4,4]{1,0:T(4,128)S(1)} %bitcast.21, s32[1]{0:T(128)} %bitcast.1.y_ref, f32[16,2048]{1,0:T(8,128)S(1)} %get-tuple-element.46.z0, f32[40,512]{1,0:T(8,128)S(1)} %collective-permute-done.4.i0, f32[40,512]{1,0:T(8,128)S(1)} %collective-permute-done.5.i1, ...), custom_call_target="tpu_custom_call" | custom-call | tf_op jit(solution)/shard_map/next_vector/pallas_call | solution.py:256
  93.8 1.4 collective-permute-start.20
  95.4 4.1 %local_product.3 = (f32[16,2048]{1,0:T(8,128)S(1)}, f32[16,512]{1,0:T(8,128)S(1)}, f32[16,512]{1,0:T(8,128)S(1)}, f32[16,512]{1,0:T(8,128)S(1)}, f32[16,512]{1,0:T(8,128)S(1)}, /*index=5*/f32[16,128]{1,0:T(8,128)S(1)}) custom-call(s32[4,4]{1,0:T(4,128)S(1)} %bitcast.22, s32[1]{0:T(128)} %bitcast.1.y_ref, f32[16,2048]{1,0:T(8,128)S(1)} %get-tuple-element.59.v.v1, ...), custom_call_target="tpu_custom_call" | custom-call | tf_op jit(solution)/shard_map/local_product/pallas_call | solution.py:336
  100.1 16.1 %all_to_all.11.ta = f32[32,16,128]{2,1,0:T(8,128)S(1)} all-to-all(f32[32,16,128]{2,1,0:T(8,128)S(1)} %broadcast_in_dim.9), channel_id=1, replica_groups=mesh['z'=8,'x'=4,'c'=2,'y'=4] {'z','x'}, dimensions={0} | all-to-all | bytes 524288 | tf_op jit(solution)/shard_map/all_to_all | solution.py:298
  116.2 2.4 %collective-permute-start.15 = (f32[16,512]{1,0:T(8,128)S(1)}, f32[16,512]{1,0:T(8,128)S(1)}, u32[]{:S(2)}, u32[]{:S(2)}) collective-permute-start(f32[16,512]{1,0:T(8,128)S(1)} %get-tuple-element.61), channel_id=1, source_target_pairs={{0,4},{4,8},{8,12},{12,16},{16,20},{20,24},{24,28},{28,32},{32,36}... | collective-permute-start | bytes 98312 | tf_op jit(solution)/shard_map/ppermute | solution.py:287
  118.6 5.3 %collective-permute-start.16 = (f32[16,512]{1,0:T(8,128)S(1)}, f32[16,512]{1,0:T(8,128)S(1)}, u32[]{:S(2)}, u32[]{:S(2)}) collective-permute-start(f32[16,512]{1,0:T(8,128)S(1)} %get-tuple-element.62), channel_id=1, source_target_pairs={{4,0},{8,4},{12,8},{16,12},{20,16},{24,20},{28,24},{32,28},{36,32}... | collective-permute-start | bytes 98312 | tf_op jit(solution)/shard_map/ppermute | solution.py:288
  123.9 3.1 %collective-permute-start.17 = (f32[16,512]{1,0:T(8,128)S(1)}, f32[16,512]{1,0:T(8,128)S(1)}, u32[]{:S(2)}, u32[]{:S(2)}) collective-permute-start(f32[16,512]{1,0:T(8,128)S(1)} %get-tuple-element.63), channel_id=1, source_target_pairs={{0,1},{1,2},{2,3},{4,5},{5,6},{6,7},{8,9},{9,10},{10,11},{12,13},{... | collective-permute-start | bytes 98312 | tf_op jit(solution)/shard_map/ppermute | solution.py:289
  128.3 7.5 %coarse.3 = (f32[16,384]{1,0:T(8,128)S(1)}, f32[16,128]{1,0:T(8,128)S(1)}) custom-call(s32[1]{0:T(128)} %bitcast.1.y_ref, f32[32,16,128]{2,1,0:T(8,128)S(1)} %all_to_all.11.ta, f32[32,16,128]{2,1,0:T(8,128)S(1)} %collective-permute-done.22.tb, f32[32,24,128]{2,1,0:T(8,128)S(1)} %all_to_all.10.ta.ma, f32[32,24,128]{2,1,0:T(8,128)S(1)} %collective-permute-done.11.tb.mb, ...), custom_call_target="tpu_custom_call" | custom-call | tf_op jit(solution)/shard_map/coarse/pallas_call | solution.py:256
  135.8 4.0 %collective-permute-start.25 = (f32[16,384]{1,0:T(8,128)S(1)}, f32[16,384]{1,0:T(8,128)S(1)}, u32[]{:S(2)}, u32[]{:S(2)}) collective-permute-start(f32[16,384]{1,0:T(8,128)S(1)} %get-tuple-element.67.p0), channel_id=1, source_target_pairs={{0,3},{1,0},{2,1},{3,2},{4,7},{5,4},{6,5},{7,6},{8,11},{9,8},{10,9... | collective-permute-start | bytes 73736 | tf_op jit(solution)/shard_map/ppermute | solution.py:294
  141.8 3.3 %collective-permute-done.24.p2 = f32[16,384]{1,0:T(8,128)S(1)} collective-permute-done((f32[16,384]{1,0:T(8,128)S(1)}, f32[16,384]{1,0:T(8,128)S(1)}, u32[]{:S(2)}, u32[]{:S(2)}) %collective-permute-start.24) | collective-permute-done | bytes 24608 | tf_op jit(solution)/shard_map/ppermute | solution.py:294
  145.6 1.9 %finish.1 = (f32[16,2048]{1,0:T(8,128)}, f32[16,2048]{1,0:T(8,128)}) custom-call(s32[4,4]{1,0:T(4,128)S(1)} %bitcast.23, f32[16,2048]{1,0:T(8,128)S(1)} %get-tuple-element.60.z1, f32[16,512]{1,0:T(8,128)S(1)} %collective-permute-done.15.i0, f32[16,512]{1,0:T(8,128)S(1)} %collective-permute-done.16.i1, f32[16,512]{1,0:T(8,128)S(1)} %collective-permute-done.17.i2, ...), custom_call_target="tpu_custom_call" | custom-call | tf_op jit(solution)/shard_map/finish/pallas_call | solution.py:256
  (60 shorter events, 14.3 us)
Async XLA Ops:
  3.5 17.7 %collective-permute-start = (f32[24,512]{1,0:T(8,128)S(1)}, f32[24,512]{1,0:T(8,128)S(1)}, u32[]{:S(2)}, u32[]{:S(2)}) collective-permute-start(f32[24,512]{1,0:T(8,128)S(1)} %get-tuple-element.37), channel_id=1, source_target_pairs={{0,4},{4,8},{8,12},{12,16},{16,20},{20,24},{24,28},{28,32},{32,36}... | collective-permute-start | bytes 147464 | tf_op jit(solution)/shard_map/ppermute | solution.py:287
  5.4 15.8 %collective-permute-start.1 = (f32[24,512]{1,0:T(8,128)S(1)}, f32[24,512]{1,0:T(8,128)S(1)}, u32[]{:S(2)}, u32[]{:S(2)}) collective-permute-start(f32[24,512]{1,0:T(8,128)S(1)} %get-tuple-element.38), channel_id=1, source_target_pairs={{4,0},{8,4},{12,8},{16,12},{20,16},{24,20},{28,24},{32,28},{36,32}... | collective-permute-start | bytes 147464 | tf_op jit(solution)/shard_map/ppermute | solution.py:288
  11.2 10.0 %collective-permute-start.2 = (f32[16,512]{1,0:T(8,128)S(1)}, f32[16,512]{1,0:T(8,128)S(1)}, u32[]{:S(2)}, u32[]{:S(2)}) collective-permute-start(f32[16,512]{1,0:T(8,128)S(1)} %get-tuple-element.39), channel_id=1, source_target_pairs={{0,1},{1,2},{2,3},{4,5},{5,6},{6,7},{8,9},{9,10},{10,11},{12,13},{... | collective-permute-start | bytes 98312 | tf_op jit(solution)/shard_map/ppermute | solution.py:289
  14.7 6.6 %collective-permute-start.3 = (f32[16,512]{1,0:T(8,128)S(1)}, f32[16,512]{1,0:T(8,128)S(1)}, u32[]{:S(2)}, u32[]{:S(2)}) collective-permute-start(f32[16,512]{1,0:T(8,128)S(1)} %get-tuple-element.40), channel_id=1, source_target_pairs={{1,0},{2,1},{3,2},{5,4},{6,5},{7,6},{9,8},{10,9},{11,10},{13,12},{... | collective-permute-start | bytes 98312 | tf_op jit(solution)/shard_map/ppermute | solution.py:290
  16.0 2.2 %copy-start.1 = (f32[512,2048]{1,0:T(8,128)S(1)}, f32[512,2048]{1,0:T(8,128)}, u32[]{:S(2)}) copy-start(f32[512,2048]{1,0:T(8,128)} %factor.1) | copy-start | bytes 12582916
  21.2 32.5 %copy-start.3 = (f32[1,24,2048]{2,1,0:T(8,128)S(1)}, f32[1,24,2048]{2,1,0:T(8,128)}, u32[]{:S(2)}) copy-start(f32[1,24,2048]{2,1,0:T(8,128)} %param.8) | copy-start | bytes 589828
  22.3 5.7 %collective-permute-start.10 = (f32[24,128]{1,0:T(8,128)S(1)}, f32[24,128]{1,0:T(8,128)S(1)}, u32[]{:S(2)}, u32[]{:S(2)}) collective-permute-start(f32[24,128]{1,0:T(8,128)S(1)} %get-tuple-element.51), channel_id=1, source_target_pairs={{0,3},{1,0},{2,1},{3,2},{4,7},{5,4},{6,5},{7,6},{8,11},{9,8},{10,9... | collective-permute-start | bytes 36872 | tf_op jit(solution)/shard_map/ppermute | solution.py:294
  26.5 5.2 %collective-permute-start.9 = (f32[24,128]{1,0:T(8,128)S(1)}, f32[24,128]{1,0:T(8,128)S(1)}, u32[]{:S(2)}, u32[]{:S(2)}) collective-permute-start(f32[24,128]{1,0:T(8,128)S(1)} %get-tuple-element.51), channel_id=1, source_target_pairs={{0,2},{1,3},{2,0},{3,1},{4,6},{5,7},{6,4},{7,5},{8,10},{9,11},{10,... | collective-permute-start | bytes 36872 | tf_op jit(solution)/shard_map/ppermute | solution.py:294
  27.1 4.9 %collective-permute-start.8 = (f32[24,128]{1,0:T(8,128)S(1)}, f32[24,128]{1,0:T(8,128)S(1)}, u32[]{:S(2)}, u32[]{:S(2)}) collective-permute-start(f32[24,128]{1,0:T(8,128)S(1)} %get-tuple-element.51), channel_id=1, source_target_pairs={{0,1},{1,2},{2,3},{3,0},{4,5},{5,6},{6,7},{7,4},{8,9},{9,10},{10,1... | collective-permute-start | bytes 36872 | tf_op jit(solution)/shard_map/ppermute | solution.py:294
  53.7 20.5 %collective-permute-start.11 = (f32[32,24,128]{2,1,0:T(8,128)S(1)}, f32[32,24,128]{2,1,0:T(8,128)S(1)}, u32[]{:S(2)}, u32[]{:S(2)}) collective-permute-start(f32[32,24,128]{2,1,0:T(8,128)S(1)} %all_to_all.10.ta.ma), channel_id=1, source_target_pairs={{0,4},{4,0},{1,5},{5,1},{2,6},{6,2},{3,7},{7,3},{8,12},{12,8},{9,1... | collective-permute-start | bytes 1179656 | tf_op jit(solution)/shard_map/ppermute | solution.py:299
  53.7 3.4 %copy-start = (bf16[1,2048,2048]{2,1,0:T(8,128)(2,1)S(1)}, bf16[1,2048,2048]{2,1,0:T(8,128)(2,1)}, u32[]{:S(2)}) copy-start(bf16[1,2048,2048]{2,1,0:T(8,128)(2,1)} %param.7) | copy-start | bytes 25165828
  61.1 23.8 %collective-permute-start.4 = (f32[40,512]{1,0:T(8,128)S(1)}, f32[40,512]{1,0:T(8,128)S(1)}, u32[]{:S(2)}, u32[]{:S(2)}) collective-permute-start(f32[40,512]{1,0:T(8,128)S(1)} %get-tuple-element.47), channel_id=1, source_target_pairs={{0,4},{4,8},{8,12},{12,16},{16,20},{20,24},{24,28},{28,32},{32,36}... | collective-permute-start | bytes 245768 | tf_op jit(solution)/shard_map/ppermute | solution.py:287
  63.6 22.8 %collective-permute-start.5 = (f32[40,512]{1,0:T(8,128)S(1)}, f32[40,512]{1,0:T(8,128)S(1)}, u32[]{:S(2)}, u32[]{:S(2)}) collective-permute-start(f32[40,512]{1,0:T(8,128)S(1)} %get-tuple-element.48), channel_id=1, source_target_pairs={{4,0},{8,4},{12,8},{16,12},{20,16},{24,20},{28,24},{32,28},{36,32}... | collective-permute-start | bytes 245768 | tf_op jit(solution)/shard_map/ppermute | solution.py:288
  68.8 18.9 %collective-permute-start.6 = (f32[40,512]{1,0:T(8,128)S(1)}, f32[40,512]{1,0:T(8,128)S(1)}, u32[]{:S(2)}, u32[]{:S(2)}) collective-permute-start(f32[40,512]{1,0:T(8,128)S(1)} %get-tuple-element.49), channel_id=1, source_target_pairs={{0,1},{1,2},{2,3},{4,5},{5,6},{6,7},{8,9},{9,10},{10,11},{12,13},{... | collective-permute-start | bytes 245768 | tf_op jit(solution)/shard_map/ppermute | solution.py:289
  70.5 17.2 %collective-permute-start.7 = (f32[40,512]{1,0:T(8,128)S(1)}, f32[40,512]{1,0:T(8,128)S(1)}, u32[]{:S(2)}, u32[]{:S(2)}) collective-permute-start(f32[40,512]{1,0:T(8,128)S(1)} %get-tuple-element.50), channel_id=1, source_target_pairs={{1,0},{2,1},{3,2},{5,4},{6,5},{7,6},{9,8},{10,9},{11,10},{13,12},{... | collective-permute-start | bytes 245768 | tf_op jit(solution)/shard_map/ppermute | solution.py:290
  71.8 23.6 %slice-start = ((s8[8388608]{0:T(1024)(128)(4,1)}), s8[4194304]{0:T(1024)(128)(4,1)S(1)}, s32[]{:S(2)}) async-start(s8[8388608]{0:T(1024)(128)(4,1)} %bitcast.8), calls=%async_computation.2 | async-start | bytes 8388608
  74.2 13.5 %copy-start.7 = (s32[1,4,4]{2,1,0:T(4,128)S(1)}, s32[1,4,4]{2,1,0:T(4,128)}, u32[]{:S(2)}) copy-start(s32[1,4,4]{2,1,0:T(4,128)} %param.10) | copy-start | bytes 196
  74.2 21.2 %slice-start.1 = ((s8[8388608]{0:T(1024)(128)(4,1)}), s8[4194304]{0:T(1024)(128)(4,1)S(1)}, s32[]{:S(2)}) async-start(s8[8388608]{0:T(1024)(128)(4,1)} %bitcast.8), calls=%async_computation.3 | async-start | bytes 8388608
  81.6 7.7 %collective-permute-start.14 = (f32[16,384]{1,0:T(8,128)S(1)}, f32[16,384]{1,0:T(8,128)S(1)}, u32[]{:S(2)}, u32[]{:S(2)}) collective-permute-start(f32[16,384]{1,0:T(8,128)S(1)} %get-tuple-element.56.p0), channel_id=1, source_target_pairs={{0,3},{1,0},{2,1},{3,2},{4,7},{5,4},{6,5},{7,6},{8,11},{9,8},{10,9... | collective-permute-start | bytes 73736 | tf_op jit(solution)/shard_map/ppermute | solution.py:294
  85.0 5.3 %collective-permute-start.13 = (f32[16,384]{1,0:T(8,128)S(1)}, f32[16,384]{1,0:T(8,128)S(1)}, u32[]{:S(2)}, u32[]{:S(2)}) collective-permute-start(f32[16,384]{1,0:T(8,128)S(1)} %get-tuple-element.56.p0), channel_id=1, source_target_pairs={{0,2},{1,3},{2,0},{3,1},{4,6},{5,7},{6,4},{7,5},{8,10},{9,11},{10,... | collective-permute-start | bytes 73736 | tf_op jit(solution)/shard_map/ppermute | solution.py:294
  86.4 5.0 %collective-permute-start.12 = (f32[16,384]{1,0:T(8,128)S(1)}, f32[16,384]{1,0:T(8,128)S(1)}, u32[]{:S(2)}, u32[]{:S(2)}) collective-permute-start(f32[16,384]{1,0:T(8,128)S(1)} %get-tuple-element.56.p0), channel_id=1, source_target_pairs={{0,1},{1,2},{2,3},{3,0},{4,5},{5,6},{6,7},{7,4},{8,9},{9,10},{10,1... | collective-permute-start | bytes 73736 | tf_op jit(solution)/shard_map/ppermute | solution.py:294
  93.0 6.5 %collective-permute-start.21 = (f32[16,128]{1,0:T(8,128)S(1)}, f32[16,128]{1,0:T(8,128)S(1)}, u32[]{:S(2)}, u32[]{:S(2)}) collective-permute-start(f32[16,128]{1,0:T(8,128)S(1)} %get-tuple-element.65), channel_id=1, source_target_pairs={{0,3},{1,0},{2,1},{3,2},{4,7},{5,4},{6,5},{7,6},{8,11},{9,8},{10,9... | collective-permute-start | bytes 24584 | tf_op jit(solution)/shard_map/ppermute | solution.py:294
  93.8 5.7 %collective-permute-start.20 = (f32[16,128]{1,0:T(8,128)S(1)}, f32[16,128]{1,0:T(8,128)S(1)}, u32[]{:S(2)}, u32[]{:S(2)}) collective-permute-start(f32[16,128]{1,0:T(8,128)S(1)} %get-tuple-element.65), channel_id=1, source_target_pairs={{0,2},{1,3},{2,0},{3,1},{4,6},{5,7},{6,4},{7,5},{8,10},{9,11},{10,... | collective-permute-start | bytes 24584 | tf_op jit(solution)/shard_map/ppermute | solution.py:294
  95.2 4.9 %collective-permute-start.19 = (f32[16,128]{1,0:T(8,128)S(1)}, f32[16,128]{1,0:T(8,128)S(1)}, u32[]{:S(2)}, u32[]{:S(2)}) collective-permute-start(f32[16,128]{1,0:T(8,128)S(1)} %get-tuple-element.65), channel_id=1, source_target_pairs={{0,1},{1,2},{2,3},{3,0},{4,5},{5,6},{6,7},{7,4},{8,9},{9,10},{10,1... | collective-permute-start | bytes 24584 | tf_op jit(solution)/shard_map/ppermute | solution.py:294
  116.2 12.1 %collective-permute-start.22 = (f32[32,16,128]{2,1,0:T(8,128)S(1)}, f32[32,16,128]{2,1,0:T(8,128)S(1)}, u32[]{:S(2)}, u32[]{:S(2)}) collective-permute-start(f32[32,16,128]{2,1,0:T(8,128)S(1)} %all_to_all.11.ta), channel_id=1, source_target_pairs={{0,4},{4,0},{1,5},{5,1},{2,6},{6,2},{3,7},{7,3},{8,12},{12,8},{9,1... | collective-permute-start | bytes 786440 | tf_op jit(solution)/shard_map/ppermute | solution.py:299
  116.2 23.5 %collective-permute-start.15 = (f32[16,512]{1,0:T(8,128)S(1)}, f32[16,512]{1,0:T(8,128)S(1)}, u32[]{:S(2)}, u32[]{:S(2)}) collective-permute-start(f32[16,512]{1,0:T(8,128)S(1)} %get-tuple-element.61), channel_id=1, source_target_pairs={{0,4},{4,8},{8,12},{12,16},{16,20},{20,24},{24,28},{28,32},{32,36}... | collective-permute-start | bytes 98312 | tf_op jit(solution)/shard_map/ppermute | solution.py:287
  118.6 21.9 %collective-permute-start.16 = (f32[16,512]{1,0:T(8,128)S(1)}, f32[16,512]{1,0:T(8,128)S(1)}, u32[]{:S(2)}, u32[]{:S(2)}) collective-permute-start(f32[16,512]{1,0:T(8,128)S(1)} %get-tuple-element.62), channel_id=1, source_target_pairs={{4,0},{8,4},{12,8},{16,12},{20,16},{24,20},{28,24},{32,28},{36,32}... | collective-permute-start | bytes 98312 | tf_op jit(solution)/shard_map/ppermute | solution.py:288
  123.9 17.9 %collective-permute-start.17 = (f32[16,512]{1,0:T(8,128)S(1)}, f32[16,512]{1,0:T(8,128)S(1)}, u32[]{:S(2)}, u32[]{:S(2)}) collective-permute-start(f32[16,512]{1,0:T(8,128)S(1)} %get-tuple-element.63), channel_id=1, source_target_pairs={{0,1},{1,2},{2,3},{4,5},{5,6},{6,7},{8,9},{9,10},{10,11},{12,13},{... | collective-permute-start | bytes 98312 | tf_op jit(solution)/shard_map/ppermute | solution.py:289
  127.0 14.8 %collective-permute-start.18 = (f32[16,512]{1,0:T(8,128)S(1)}, f32[16,512]{1,0:T(8,128)S(1)}, u32[]{:S(2)}, u32[]{:S(2)}) collective-permute-start(f32[16,512]{1,0:T(8,128)S(1)} %get-tuple-element.64), channel_id=1, source_target_pairs={{1,0},{2,1},{3,2},{5,4},{6,5},{7,6},{9,8},{10,9},{11,10},{13,12},{... | collective-permute-start | bytes 98312 | tf_op jit(solution)/shard_map/ppermute | solution.py:290
  135.8 6.0 %collective-permute-start.25 = (f32[16,384]{1,0:T(8,128)S(1)}, f32[16,384]{1,0:T(8,128)S(1)}, u32[]{:S(2)}, u32[]{:S(2)}) collective-permute-start(f32[16,384]{1,0:T(8,128)S(1)} %get-tuple-element.67.p0), channel_id=1, source_target_pairs={{0,3},{1,0},{2,1},{3,2},{4,7},{5,4},{6,5},{7,6},{8,11},{9,8},{10,9... | collective-permute-start | bytes 73736 | tf_op jit(solution)/shard_map/ppermute | solution.py:294
  139.8 5.3 %collective-permute-start.24 = (f32[16,384]{1,0:T(8,128)S(1)}, f32[16,384]{1,0:T(8,128)S(1)}, u32[]{:S(2)}, u32[]{:S(2)}) collective-permute-start(f32[16,384]{1,0:T(8,128)S(1)} %get-tuple-element.67.p0), channel_id=1, source_target_pairs={{0,2},{1,3},{2,0},{3,1},{4,6},{5,7},{6,4},{7,5},{8,10},{9,11},{10,... | collective-permute-start | bytes 73736 | tf_op jit(solution)/shard_map/ppermute | solution.py:294
  140.5 5.0 %collective-permute-start.23 = (f32[16,384]{1,0:T(8,128)S(1)}, f32[16,384]{1,0:T(8,128)S(1)}, u32[]{:S(2)}, u32[]{:S(2)}) collective-permute-start(f32[16,384]{1,0:T(8,128)S(1)} %get-tuple-element.67.p0), channel_id=1, source_target_pairs={{0,1},{1,2},{2,3},{3,0},{4,5},{5,6},{6,7},{7,4},{8,9},{9,10},{10,1... | collective-permute-start | bytes 73736 | tf_op jit(solution)/shard_map/ppermute | solution.py:294
  (5 other events, 5.3 us)

commit v2 on v1

v2 whole, which is shorter than its diff:
```python
import functools

import jax
import jax.numpy as jnp
from jax import lax
from jax.experimental import pallas as pl
from jax.experimental.pallas import tpu as pltpu
from jax.sharding import Mesh, PartitionSpec as P

BW = 128
LANES = 32
NORM, CROSS, SQUARE, LOCAL = 24, 25, 26, 27
MAP, PER = 26, 6
RADIX = 256
F32, BF16 = jnp.float32, jnp.bfloat16
ALL = ("z", "x", "c", "y")
SUB = ("z", "x", "c")
FETCH = 44

NN = (((1,), (0,)), ((), ()))
NT = (((1,), (1,)), ((), ()))

VMEM = pl.BlockSpec(memory_space=pltpu.VMEM)
SMEM = pl.BlockSpec(memory_space=pltpu.SMEM)


def split(x):
    hi = x.astype(BF16)
    return hi, (x - hi.astype(F32)).astype(BF16)


def dot(a, b, dims):
    return lax.dot_general(a, b, dims, preferred_element_type=F32)


def dot3(a, b_hi, b_lo, dims):
    rows = a.shape[0]
    a_hi, a_lo = split(a)
    both = dot(jnp.concatenate([a_hi, a_lo], axis=0), b_hi, dims)
    return both[:rows] + both[rows:] + dot(a_hi, b_lo, dims)


def block_at(b):
    return pl.ds(pl.multiple_of(jnp.maximum(b, 0) * BW, BW), BW)


def place_of(ints):
    return ints[ints.shape[0] - 2], ints[ints.shape[0] - 1]


def faces_of(ints):
    y, core = place_of(ints)
    odd = y % 2
    return (1 - core, core, 3 - odd, 2 + odd)


def subtract_faces(ref, ints, incoming):
    for f, (got, col0) in zip(faces_of(ints), incoming):
        for c in range(4):
            b = ints[f * 4 + c]
            at = block_at(b)
            held = ref[:, at]
            ref[:, at] = jnp.where(b >= 0, held - got[0:16, col0 + c * BW : col0 + (c + 1) * BW], held)


def pack_face(values, ints, f, out):
    rows = values.shape[0]
    for c in range(4):
        out[0:rows, c * BW : (c + 1) * BW] = values[:, block_at(ints[f * 4 + c])]


def lane_sum(x):
    return jnp.sum(x, axis=1, keepdims=True)


def place(lane, y, slot, column):
    return jnp.where(lane == y * LANES + slot, column, 0.0)


def first_pack(ints, both, o0, o1, o2, o3, own_map):
    row = lax.broadcasted_iota(jnp.int32, (8, BW), 0)
    lane = lax.broadcasted_iota(jnp.int32, (8, BW), 1) - (place_of(ints)[0] * LANES + MAP)
    placed = jnp.zeros((8, BW), jnp.int32)
    for j in range(24):
        here = jnp.logical_and(row == j // PER, lane == j % PER)
        placed = jnp.where(here, ints[16 + j], placed)
    placed = placed.astype(F32)
    own_map[...] = placed
    for f, o in zip(faces_of(ints), (o0, o1, o2, o3)):
        pack_face(both, ints, f, o)
    for o in (o0, o1):
        o[40:48, 0:BW] = placed
        o[40:48, BW:] = jnp.zeros((8, 3 * BW), F32)


def spread_coupling(ints, both, mat, bx_hi, bx_lo, weight, held, bx, sems):
    rows = mat.shape[0] // 4
    copies = []
    for n in range(4):
        at = pl.ds(n * rows, rows)
        copies.append(pltpu.make_async_copy(mat.at[at], held.at[at], sems.at[n]))
        copies[n].start()
    bx[...] = jnp.zeros_like(bx)
    bx[pl.ds(pl.multiple_of(place_of(ints)[0] * LANES, LANES), 24), :] = both[16:40, :]
    hi, lo = split(bx[...])
    bx_hi[...] = hi
    bx_lo[...] = lo
    weight[...] = jnp.ones_like(weight)
    for f in range(4):
        for c in range(4):
            b = ints[f * 4 + c]
            at = block_at(b)
            weight[:, at] = jnp.where(b >= 0, jnp.full((8, BW), 0.5, F32), weight[:, at])
    for copy in copies:
        copy.wait()


def first_vector(ints, both, i0, i1, i2, i3, bx_hi, bx_lo, weight, own_map, v0, pay):
    v0[...] = both[0:16, :]
    subtract_faces(v0, ints, [(i, 0) for i in (i0, i1, i2, i3)])
    v = v0[...]
    norm = lane_sum(v * v * weight[0:1, :])
    lane = lax.broadcasted_iota(jnp.int32, (16, BW), 1)
    maps = jnp.concatenate(
        [own_map[0:4, :], i0[40:44, 0:BW], i1[40:44, 0:BW], jnp.zeros((4, BW), F32)], axis=0
    )
    pay[...] = dot3(v, bx_hi[...], bx_lo[...], NT) + place(lane, place_of(ints)[0], NORM, norm) + maps


def local_product(final, ints, v, mat, z, o0, o1, o2, o3, *rest):
    width = 256
    hi, lo = split(v[...])
    pieces = jnp.concatenate([hi, lo], axis=0)
    for step in range(mat.shape[1] // width):
        at = slice(step * width, (step + 1) * width)
        both = dot(pieces, mat[:, at], NN)
        z[:, at] = both[:16] + both[16:]
    for f, o in zip(faces_of(ints), (o0, o1, o2, o3)):
        pack_face(z, ints, f, o)
    if final:
        (dot_out,) = rest
        lane = lax.broadcasted_iota(jnp.int32, (16, BW), 1)
        dot_out[...] = place(lane, place_of(ints)[0], LOCAL, lane_sum(v[...] * z[...]))


def jumped_coupling(ints, both, i0, i1, i2, i3, b_hi, b_lo, full):
    y = place_of(ints)[0]
    full[...] = jnp.zeros_like(full)

    def rows(n):
        return pl.ds(pl.multiple_of(n * LANES, LANES), 24)

    full[rows(y), :] = both[16:40, :]
    beside = y + 2 * (y % 2) - 1
    places = (rows(4), rows(5), rows(y + 1 - 2 * (y % 2)), rows(jnp.clip(beside, 0, 3)))
    for f, to, got in zip(faces_of(ints), places, (i0, i1, i2, i3)):
        for c in range(4):
            b = ints[f * 4 + c]
            at = block_at(b)
            full[to, at] = jnp.where(b >= 0, -got[16:40, c * BW : (c + 1) * BW], full[to, at])
    hi, lo = split(full[...])
    b_hi[...] = hi
    b_lo[...] = lo


def unpacked_map(rows):
    slot = lax.broadcasted_iota(jnp.int32, rows[0].shape, 1) % LANES
    found = jnp.zeros_like(rows[0])
    for k, row in enumerate(rows):
        found = jnp.where(slot // PER == k, pltpu.roll(row, BW - (MAP - PER * k), 1), found)
    return found.astype(jnp.int32), slot


def picked_columns(pay, f_hi, f_lo, c_hi, c_lo):
    dofs = f_hi.shape[1]
    wanted = []
    for n in range(3):
        rows = [jnp.broadcast_to(pay[4 * n + k : 4 * n + k + 1, :], (8, BW)) for k in range(4)]
        wanted.append(unpacked_map(rows)[0][0:1, :])
    wanted = jnp.concatenate(wanted, axis=1)
    row = lax.broadcasted_iota(jnp.int32, (dofs, 3 * BW), 0)
    hot = (row == wanted).astype(F32).astype(BF16)
    c_hi[...] = dot(f_hi[...], hot, NN).astype(BF16)
    c_lo[...] = dot(f_lo[...], hot, NN).astype(BF16)


def coarse_half(first, t, near, *rest):
    if first:
        factor, out, f_hi, f_lo, top, hot, terms_at = rest
    else:
        f_hi, f_lo, top, hot, out, terms_at = rest
    groups = t.shape[0]
    owned = f_hi.shape[0]
    digits = f_hi.shape[1] // RADIX
    half = digits * 16
    if first:
        dof, slot = unpacked_map([t[:, k, :] for k in range(4)])
        top[...] = jnp.where(slot < 24, dof // RADIX, -1).astype(F32)
        low = (dof % RADIX).astype(F32)
        low = jnp.transpose(jnp.concatenate([low] * (BW // groups), axis=0))
        lane = lax.broadcasted_iota(jnp.int32, (BW, BW), 1).astype(F32)
        one, zero = (jnp.ones((BW, BW), BF16), jnp.zeros((BW, BW), BF16))
        for j in range(groups):
            column = jnp.broadcast_to(low[:, j : j + 1], (BW, BW)).astype(BF16)
            for n in range(RADIX // BW):
                wanted = (lane + float(n * BW)).astype(BF16)
                hot[j * BW : (j + 1) * BW, n * BW : (n + 1) * BW] = jnp.where(
                    wanted == column, one, zero
                )
    none = jnp.zeros((16, BW), BF16)

    def body(j, acc):
        terms = t[j]
        digit = jnp.broadcast_to(top[pl.ds(j, 1), :], (16, BW)).astype(BF16)
        hi, lo = split(terms)
        at = pl.ds(pl.multiple_of(j * BW, BW), BW)
        for d in range(digits):
            mine = digit == jnp.full((16, BW), d, BF16)
            terms_at[d * 16 : d * 16 + 16, at] = jnp.where(mine, hi, none)
            terms_at[half + d * 16 : half + d * 16 + 16, at] = jnp.where(mine, lo, none)
        return acc + terms

    total = lax.fori_loop(0, groups, body, jnp.zeros((16, BW), F32), unroll=4)
    sums = dot(terms_at[...], hot[...], NN)
    sums = sums[:half] + sums[half:]
    rhs = jnp.concatenate([sums[d * 16 : d * 16 + 16, :] for d in range(digits)], axis=1)
    hi, lo = split(rhs)
    pieces = jnp.concatenate([hi, lo], axis=0)
    if first:
        f_hi[...], f_lo[...] = split(factor[...])
    column = lax.broadcasted_iota(jnp.int32, (owned, 32), 1)
    mid = dot(f_hi[...], pieces, NT) + jnp.where(column < 16, dot(f_lo[...], pieces, NT), 0.0)
    mid = jnp.transpose(mid)
    out[:, 0:owned] = mid[:16] + mid[16:]
    out[:, owned : owned + BW] = total
    out[:, owned + BW :] = near[...]


def coarse_part(final, ints, own, got, beside, c_hi, c_lo, out, scal):
    owned = c_hi.shape[0]
    mid = own[:, 0:owned] + got[:, 0:owned]
    total = own[:, owned : owned + BW] + got[:, owned : owned + BW]
    picked = dot3(mid, c_hi[...], c_lo[...], NN)
    lane = lax.broadcasted_iota(jnp.int32, (16, BW), 1)
    slot = lane % LANES

    def over(which):
        return lane_sum(jnp.where(which, total, 0.0))

    if final:
        energy = over(lane == place_of(ints)[0] * LANES + LOCAL) + lane_sum(mid * mid)
        wide = lax.broadcasted_iota(jnp.int32, picked.shape, 1)
        picked = jnp.where(wide == NORM, energy, picked)
        scal[...] = jnp.where(lane == 0, over(slot == CROSS), over(slot == SQUARE))
    else:
        scal[...] = jnp.broadcast_to(over(slot == NORM), (16, BW))
    width = picked.shape[1]
    out[:, 0:width] = picked
    out[:, width:] = beside[...]


def second_part(own, got, beside, out):
    width = own.shape[1] - beside.shape[1]
    out[:, 0:width] = own[:, 0:width] + got[:, 0:width]
    out[:, width:] = beside[...]


def jumped(out, z, ints, got, far, p1, sent, p2, b_hi, b_lo):
    width = sent.shape[1] - 4 * BW
    picked = sent[:, 0:width] + p2[:, 0:width]
    y = place_of(ints)[0]
    lane = lax.broadcasted_iota(jnp.int32, (16, BW), 1)
    beside = pltpu.roll(picked[:, BW : 2 * BW], (BW - y * LANES) % BW, 1)
    beyond = pltpu.roll(picked[:, 2 * BW :], (BW + LANES - y * LANES) % BW, 1)
    beside = jnp.where(lane < LANES, beside, jnp.where(lane < 2 * LANES, beyond, 0.0))
    needed = jnp.concatenate([picked[:, 0:BW], beside], axis=1)
    out[...] = z[...] + dot3(needed, b_hi[...], b_lo[...], NN)
    near_at = got.shape[1] - 4 * BW
    subtract_faces(out, ints, ((got, near_at), (far, 0), (p1, width), (p2, width)))
    return picked


def next_vector(
    ints, z0, got, far, p1, sent, p2, b_hi, b_lo, v0, bx_hi, bx_lo, weight, v1, pay
):
    jumped(v1, z0, ints, got, far, p1, sent, p2, b_hi, b_lo)
    v = v1[...]
    w = v * weight[0:1, :]
    lane = lax.broadcasted_iota(jnp.int32, (16, BW), 1)
    y = place_of(ints)[0]
    pay[...] = (
        dot3(v, bx_hi[...], bx_lo[...], NT)
        + place(lane, y, CROSS, lane_sum(v0[...] * w))
        + place(lane, y, SQUARE, lane_sum(v * w))
    )


def finish(ints, z1, got, far, p1, sent, p2, b_hi, b_lo, v0, v1, s0, s1, mult, resid):
    picked = jumped(resid, z1, ints, got, far, p1, sent, p2, b_hi, b_lo)
    norm, cross, square = (s0[:, 0:1], s1[:, 0:1], s1[:, 1:2])
    energy = picked[:, NORM : NORM + 1]
    step1 = norm / cross
    fresh = norm - 2.0 * step1 * cross + step1 * step1 * square
    c = 1.0 + fresh / norm
    curvature = c * c * cross - 2.0 * c * step1 * square + step1 * step1 * energy
    step2 = fresh / curvature
    first, second = (v0[...], v1[...])
    mult[...] = (step1 + step2 * c) * first - (step2 * step1) * second
    resid[...] = first - (step1 + step2 * c) * second + (step2 * step1) * resid[...]


def call(kernel, name, ins, outs, scalars, micros, scratch=(), mib=8, outside=()):
    specs = [SMEM] * scalars + [VMEM] * (len(ins) - scalars)
    for n in outside:
        specs[n] = pl.BlockSpec(memory_space=pl.ANY)
    return pl.pallas_call(
        kernel,
        out_shape=[jax.ShapeDtypeStruct(s, d) for s, d in outs],
        in_specs=specs,
        out_specs=[VMEM] * len(outs),
        scratch_shapes=[pltpu.VMEM(*s) if isinstance(s, tuple) else s for s in scratch],
        compiler_params=pltpu.CompilerParams(vmem_limit_bytes=mib * 1024 * 1024),
        cost_estimate=pl.CostEstimate(
            flops=int(micros * 1e6), bytes_accessed=int(micros * 3.5e6), transcendentals=0
        ),
        name=name,
    )(*ins)


def per_device(interface_load, flexibility, corner_coupling, coarse_factor, face_slots, corner_map):
    both = jnp.concatenate([interface_load[0], corner_coupling[0]], axis=0)
    cases, dofs = interface_load.shape[1:]
    owned, coarse_dofs = coarse_factor.shape
    zs, xs, cs, ys = (lax.axis_size(a) for a in ALL)
    subs = zs * xs * cs
    face = 4 * BW
    here = jnp.stack([lax.axis_index("y"), lax.axis_index("c")]).astype(jnp.int32)
    ints = jnp.concatenate([*(face_slots[0, f] for f in range(4)), corner_map[0], here])
    near_pairs = [(i, i ^ 1) for i in range(cs)]
    far_pairs = [(i, (i + 1) % subs) for i in range(1, subs, 2)]
    far_pairs = far_pairs + [(j, i) for i, j in far_pairs]
    one_pairs = [(j, j ^ 1) for j in range(ys)]
    two_pairs = [(j, j ^ 3) for j in range(ys)]

    def near(p):
        return lax.ppermute(p, "c", near_pairs)

    def far(p):
        return lax.ppermute(p, SUB, far_pairs)

    def one(p):
        return lax.ppermute(p, "y", one_pairs)

    def two(p):
        return lax.ppermute(p, "y", two_pairs)

    def gather(row):
        every = jnp.broadcast_to(row[None], (zs * xs,) + row.shape)
        return lax.all_to_all(every, ("z", "x"), 0, 0)

    def product(final, v):
        outs = [((cases, dofs), F32)] + [((cases, face), F32)] * 4
        if final:
            outs = outs + [((cases, BW), F32)]
        return call(
            functools.partial(local_product, final),
            "local_product",
            (ints, v, matrix),
            outs,
            1,
            2,
            mib=6,
        )

    def half(first, t, face_near, *held):
        terms = t.shape[0] * BW
        outs = [((cases, owned + BW + face), F32)]
        if first:
            outs = outs + [((owned, coarse_dofs), BF16)] * 2
            outs = outs + [((t.shape[0], BW), F32), ((terms, RADIX), BF16)]
        return call(
            functools.partial(coarse_half, first),
            "coarse_half",
            (t, face_near, *held),
            outs,
            0,
            4,
            [((2 * cases * (coarse_dofs // RADIX), terms), BF16)],
            mib=16,
        )

    def rest_of_solve(final, own, face_one, face_two, *early):
        got = near(own)
        sent, scal = call(
            functools.partial(coarse_part, final),
            "coarse_part",
            (ints, own, got, face_one, c_hi, c_lo),
            [((cases, 3 * BW + face), F32), ((cases, BW), F32)],
            1,
            1,
        )
        p1, *early = lax.optimization_barrier((one(sent), *early))
        (sent,) = call(
            second_part, "second_part", (sent, p1, face_two), [((cases, 3 * BW + face), F32)], 0, 0.5
        )
        return early, scal, got, p1, sent, two(sent)

    o0, o1, o2, o3, own_map = call(
        first_pack,
        "first_pack",
        (ints, both),
        [((48, face), F32)] * 2 + [((40, face), F32)] * 2 + [((8, BW), F32)],
        1,
        1,
    )
    far_came = far(o1)
    came = (near(o0), far_came, one(o2), two(o3))
    bx_hi, bx_lo, weight, matrix = call(
        spread_coupling,
        "spread_coupling",
        (ints, both, flexibility[0]),
        [((BW, dofs), BF16)] * 2 + [((8, dofs), F32), ((dofs, dofs), BF16)],
        1,
        3,
        [((BW, dofs), F32), pltpu.SemaphoreType.DMA((4,))],
        mib=FETCH,
        outside=(2,),
    )
    v0, pay = call(
        first_vector,
        "first_vector",
        (ints, both, *came, bx_hi, bx_lo, weight, own_map),
        [((cases, dofs), F32), ((cases, BW), F32)],
        1,
        1,
    )
    came_one, z0, *faces = lax.optimization_barrier((one(pay), *product(False, v0)))
    pair = pay + came_one
    row = pair + two(pair)
    terms0, face_far = lax.optimization_barrier((gather(row), faces[1]))
    face_far = far(face_far)
    own, *held = half(True, terms0, faces[0], coarse_factor)
    f_hi, f_lo = held[:2]
    c_hi, c_lo = call(
        picked_columns,
        "picked_columns",
        (row, f_hi, f_lo),
        [((owned, 3 * BW), BF16)] * 2,
        0,
        2.5,
        mib=16,
    )
    b_hi, b_lo = call(
        jumped_coupling,
        "jumped_coupling",
        (ints, both, *came),
        [((2 * BW, dofs), BF16)] * 2,
        1,
        1.2,
        [((2 * BW, dofs), F32)],
        mib=10,
    )
    (b_hi, b_lo), scal0, got, *parts = rest_of_solve(False, own, faces[2], faces[3], b_hi, b_lo)
    v1, pay = call(
        next_vector,
        "next_vector",
        (ints, z0, got, face_far, *parts, b_hi, b_lo, v0, bx_hi, bx_lo, weight),
        [((cases, dofs), F32), ((cases, BW), F32)],
        1,
        1.6,
        mib=12,
    )
    came_one, z1, *faces, local_dot = lax.optimization_barrier((one(pay), *product(True, v1)))
    pair = pay + came_one
    row = pair + two(pair) + local_dot
    terms1, face_far = lax.optimization_barrier((gather(row), faces[1]))
    face_far = far(face_far)
    (own,) = half(False, terms1, faces[0], *held)
    _, scal1, got, *parts = rest_of_solve(True, own, faces[2], faces[3])
    mult, resid = call(
        finish,
        "finish",
        (ints, z1, got, face_far, *parts, b_hi, b_lo, v0, v1, scal0, scal1),
        [((cases, dofs), F32)] * 2,
        1,
        1.9,
        mib=12,
    )
    return mult[None], resid[None]


def solution(mesh):
    fine = Mesh(mesh.devices.reshape(8, 4, 2, 4), ALL)
    in_specs = (
        P(ALL, None, None),
        P(ALL, None, None),
        P(ALL, None, None),
        P("y", None),
        P(ALL, None, None),
        P(ALL, None),
    )
    out_specs = (P(ALL, None, None), P(ALL, None, None))
    return jax.shard_map(
        per_device, mesh=fine, in_specs=in_specs, out_specs=out_specs, check_vma=False
    )
```

time: 148 us -> 109 us (0.74)
  starting transfers between devices: 55.3 us -> 14.7 us
  waiting for transfers between devices: 10.4 us -> 27.8 us
  Pallas kernels: 34.2 us -> 26.3 us
  local copies, waits for them, and re-layouts: 8.81 us -> 1.62 us
  blocking collectives: 37.7 us -> 35.7 us
    ppermute x26 -> x16, starting transfers between devices: 55.3 us -> 14.7 us  [the longest x5 8.43 us: two(): return lax.ppermute(p, 'y', two_pairs)]
    ppermute x26 -> x16, waiting for transfers between devices: 10.4 us -> 27.8 us  [the longest x3 10 us: far(): return lax.ppermute(p, SUB, far_pairs)]
    unnamed x22 -> x2, local copies, waits for them, and re-layouts: 8.76 us -> 0.01 us
    pallas_call x2 -> x0, Pallas kernels: 8.14 us -> none  [product(): pl.pallas_call(functools.partial(local_product, first), grid=(dofs // wid...]
    all_to_all x2, blocking collectives: 37.7 us -> 35.7 us  [gather(): return lax.all_to_all(every, ('z', 'x'), 0, 0)]
    pallas_call x9 -> x15, Pallas kernels: 26.1 us -> 26.3 us  [call(): pl.pallas_call(kernel, out_shape=[jax.ShapeDtypeStruct(s, d) for s, d in...]
  transfers between devices with their start and end apart: 26 -> 16, of which waited for: 7 -> 9; matrix products, arithmetic and copies ran while one was open for 0% -> 0% of each run, Pallas kernels for 20% -> 11%
where the time goes in v2:
time: 109 us; the launch traced here: 108 us
  blocking collectives  35.7 us (33%)
  waiting for transfers between devices  27.8 us (26%)
  Pallas kernels  26.3 us (24%)
  starting transfers between devices  14.7 us (13%)
  local copies, waits for them, and re-layouts  1.62 us (1%)
    all_to_all x2, blocking collectives, gather(): return lax.all_to_all(every, ('z', 'x'), 0, 0)  35.7 us
    pallas_call x15, Pallas kernels, call(): pl.pallas_call(kernel, out_shape=[jax.ShapeDtypeStruct(s, d) for s, d in...  26.3 us
    ppermute x3, waiting for transfers between devices, far(): return lax.ppermute(p, SUB, far_pairs)  10 us
    ppermute x5, waiting for transfers between devices, one(): return lax.ppermute(p, 'y', one_pairs)  9.68 us
    ppermute x5, starting transfers between devices, two(): return lax.ppermute(p, 'y', two_pairs)  8.43 us
    ppermute x5, waiting for transfers between devices, two(): return lax.ppermute(p, 'y', two_pairs)  6.85 us
    ppermute x3, starting transfers between devices, far(): return lax.ppermute(p, SUB, far_pairs)  3.29 us
    ppermute x5, starting transfers between devices, one(): return lax.ppermute(p, 'y', one_pairs)  2.73 us
  transfers between devices with their start and end apart: 16, of which 9 were waited for; matrix products, arithmetic and copies ran while one was open for 0% of the time, Pallas kernels for 11%

profile of v2, /device:TPU:32, one launch (start us, length us, event | category | flops | bytes accessed | tf_op | source)
XLA Modules:
  0.0 108.0 jit_solution(17868084172738110923)
XLA Ops:
  0.6 0.8 slice_bitcast_fusion
  1.5 1.0 pad_maximum_fusion.both
  4.0 2.4 %collective-permute-start.1 = (f32[48,512]{1,0:T(8,128)S(1)}, f32[48,512]{1,0:T(8,128)S(1)}, u32[]{:S(2)}, u32[]{:S(2)}) collective-permute-start(f32[48,512]{1,0:T(8,128)S(1)} %get-tuple-element.62), channel_id=1, source_target_pairs={{4,8},{12,16},{20,24},{28,32},{36,40},{44,48},{52,56},{60,64},{68,... | collective-permute-start | bytes 294920 | tf_op jit(solution)/shard_map/ppermute | solution.py:349
  6.4 1.6 %collective-permute-start.2 = (f32[40,512]{1,0:T(8,128)S(1)}, f32[40,512]{1,0:T(8,128)S(1)}, u32[]{:S(2)}, u32[]{:S(2)}) collective-permute-start(f32[40,512]{1,0:T(8,128)S(1)} %get-tuple-element.63), channel_id=1, source_target_pairs={{0,1},{1,0},{2,3},{3,2},{4,5},{5,4},{6,7},{7,6},{8,9},{9,8},{10,11... | collective-permute-start | bytes 245768 | tf_op jit(solution)/shard_map/ppermute | solution.py:352
  7.9 2.2 %collective-permute-start.3 = (f32[40,512]{1,0:T(8,128)S(1)}, f32[40,512]{1,0:T(8,128)S(1)}, u32[]{:S(2)}, u32[]{:S(2)}) collective-permute-start(f32[40,512]{1,0:T(8,128)S(1)} %get-tuple-element.64), channel_id=1, source_target_pairs={{0,3},{1,2},{2,1},{3,0},{4,7},{5,6},{6,5},{7,4},{8,11},{9,10},{10,... | collective-permute-start | bytes 245768 | tf_op jit(solution)/shard_map/ppermute | solution.py:355
  10.1 4.0 %spread_coupling.1 = (bf16[128,2048]{1,0:T(8,128)(2,1)S(1)}, bf16[128,2048]{1,0:T(8,128)(2,1)S(1)}, f32[8,2048]{1,0:T(8,128)S(1)}, bf16[2048,2048]{1,0:T(8,128)(2,1)S(1)}) custom-call(s32[42]{0:T(128)S(1)} %concatenate.6.ints, f32[40,2048]{1,0:T(8,128)S(1)} %pad_maximum_fusion.both, bf16[2048,2048]{1,0:T(8,128)(2,1)} %bitcast.16), custom_call_target="tpu_custom_call" | custom-call | flops 3000000 | bytes 10500000 | tf_op jit(solution)/shard_map/spread_coupling/pallas_call | solution.py:316
  14.2 1.0 first_vector.1
  16.0 2.0 %local_product.2 = (f32[16,2048]{1,0:T(8,128)S(1)}, f32[16,512]{1,0:T(8,128)S(1)}, f32[16,512]{1,0:T(8,128)S(1)}, f32[16,512]{1,0:T(8,128)S(1)}, f32[16,512]{1,0:T(8,128)S(1)}) custom-call(s32[42]{0:T(128)S(1)} %concatenate.6.ints, f32[16,2048]{1,0:T(8,128)S(1)} %get-tuple-element.70.v.v0, bf16[2048,2048]{1,0:T(8,128)(2,1)S(1)} %get-tuple-element.71.mat), custom_call_target="tpu_custom_call" | custom-call | flops 2000000 | bytes 7000000 | tf_op jit(solution)/shard_map/local_product/pallas_call | solution.py:316
  18.0 1.0 collective-permute-done.4
  19.0 1.6 %collective-permute-start.5 = (f32[16,128]{1,0:T(8,128)S(1)}, f32[16,128]{1,0:T(8,128)S(1)}, u32[]{:S(2)}, u32[]{:S(2)}) collective-permute-start(f32[16,128]{1,0:T(8,128)S(1)} %add.15), channel_id=1, source_target_pairs={{0,3},{1,2},{2,1},{3,0},{4,7},{5,6},{6,5},{7,4},{8,11},{9,10},{10,... | collective-permute-start | bytes 24584 | tf_op jit(solution)/shard_map/ppermute | solution.py:355
  20.5 3.3 %collective-permute-done.5 = f32[16,128]{1,0:T(8,128)S(1)} collective-permute-done((f32[16,128]{1,0:T(8,128)S(1)}, f32[16,128]{1,0:T(8,128)S(1)}, u32[]{:S(2)}, u32[]{:S(2)}) %collective-permute-start.5) | collective-permute-done | bytes 8224 | tf_op jit(solution)/shard_map/ppermute | solution.py:355
  23.9 20.0 %all_to_all.10.t = f32[32,16,128]{2,1,0:T(8,128)S(1)} all-to-all(f32[32,16,128]{2,1,0:T(8,128)S(1)} %broadcast_in_dim.8), channel_id=1, replica_groups=mesh['z'=8,'x'=4,'c'=2,'y'=4] {'z','x'}, dimensions={0} | all-to-all | bytes 524288 | tf_op jit(solution)/shard_map/all_to_all | solution.py:359
  43.9 4.3 %coarse_half.2 = (f32[16,1152]{1,0:T(8,128)S(1)}, bf16[512,2048]{1,0:T(8,128)(2,1)S(1)}, bf16[512,2048]{1,0:T(8,128)(2,1)S(1)}, f32[32,128]{1,0:T(8,128)S(1)}, bf16[4096,256]{1,0:T(8,128)(2,1)S(1)}) custom-call(f32[32,16,128]{2,1,0:T(8,128)S(1)} %all_to_all.10.t, f32[16,512]{1,0:T(8,128)S(1)} %get-tuple-element.81.near, f32[512,2048]{1,0:T(8,128)S(1)} %copy-done), custom_call_target="tpu_custom_call" | custom-call | flops 4000000 | bytes 14000000 | tf_op jit(solution)/shard_map/coarse_half/pallas_call | solution.py:316
  48.3 2.5 %picked_columns.1 = (bf16[512,384]{1,0:T(8,128)(2,1)S(1)}, bf16[512,384]{1,0:T(8,128)(2,1)S(1)}) custom-call(f32[16,128]{1,0:T(8,128)S(1)} %add.16.pay, bf16[512,2048]{1,0:T(8,128)(2,1)S(1)} %get-tuple-element.85.f_hi.rest_0_, bf16[512,2048]{1,0:T(8,128)(2,1)S(1)} %get-tuple-element.86.f_lo.rest_1_), custom_call_target="tpu_custom_call" | custom-call | flops 2500000 | bytes 8750000 | tf_op jit(solution)/shard_map/picked_columns/pallas_call | solution.py:316
  50.8 0.8 coarse_part.2
  51.8 1.4 %jumped_coupling.1 = (bf16[256,2048]{1,0:T(8,128)(2,1)S(1)}, bf16[256,2048]{1,0:T(8,128)(2,1)S(1)}) custom-call(s32[42]{0:T(128)S(1)} %concatenate.6.ints, f32[40,2048]{1,0:T(8,128)S(1)} %pad_maximum_fusion.both, f32[48,512]{1,0:T(8,128)S(1)} %collective-permute-done.i0, f32[48,512]{1,0:T(8,128)S(1)} %collective-permute-done.1.i1, ...), custom_call_target="tpu_custom_call" | custom-call | flops 1200000 | bytes 4200000 | tf_op jit(solution)/shard_map/jumped_coupling/pallas_call | solution.py:316
  53.2 2.9 %collective-permute-done.8.got.p1 = f32[16,896]{1,0:T(8,128)S(1)} collective-permute-done((f32[16,896]{1,0:T(8,128)S(1)}, f32[16,896]{1,0:T(8,128)S(1)}, u32[]{:S(2)}, u32[]{:S(2)}) %collective-permute-start.8) | collective-permute-done | bytes 57376 | tf_op jit(solution)/shard_map/ppermute | solution.py:352
  56.2 1.9 %collective-permute-start.9 = (f32[16,896]{1,0:T(8,128)S(1)}, f32[16,896]{1,0:T(8,128)S(1)}, u32[]{:S(2)}, u32[]{:S(2)}) collective-permute-start(f32[16,896]{1,0:T(8,128)S(1)} %second_part.2.sent), channel_id=1, source_target_pairs={{0,3},{1,2},{2,1},{3,0},{4,7},{5,6},{6,5},{7,4},{8,11},{9,10},{10,... | collective-permute-start | bytes 172040 | tf_op jit(solution)/shard_map/ppermute | solution.py:355
  58.1 0.8 collective-permute-start.7
  58.8 4.7 %collective-permute-done.7.far = f32[16,512]{1,0:T(8,128)S(1)} collective-permute-done((f32[16,512]{1,0:T(8,128)S(1)}, f32[16,512]{1,0:T(8,128)S(1)}, u32[]{:S(2)}, u32[]{:S(2)}) %collective-permute-start.7) | collective-permute-done | bytes 32800 | tf_op jit(solution)/shard_map/ppermute | solution.py:349
  63.5 1.5 %next_vector.1 = (f32[16,2048]{1,0:T(8,128)S(1)}, f32[16,128]{1,0:T(8,128)S(1)}) custom-call(s32[42]{0:T(128)S(1)} %concatenate.6.ints, f32[16,2048]{1,0:T(8,128)S(1)} %get-tuple-element.77.z0, f32[16,1152]{1,0:T(8,128)S(1)} %collective-permute-done.6.got, f32[16,512]{1,0:T(8,128)S(1)} %collective-permute-done.7.far, ...), custom_call_target="tpu_custom_call" | custom-call | flops 1600000 | bytes 5600000 | tf_op jit(solution)/shard_map/next_vector/pallas_call | solution.py:316
  65.1 2.1 %local_product.3 = (f32[16,2048]{1,0:T(8,128)S(1)}, f32[16,512]{1,0:T(8,128)S(1)}, f32[16,512]{1,0:T(8,128)S(1)}, f32[16,512]{1,0:T(8,128)S(1)}, f32[16,512]{1,0:T(8,128)S(1)}, /*index=5*/f32[16,128]{1,0:T(8,128)S(1)}) custom-call(s32[42]{0:T(128)S(1)} %concatenate.6.ints, f32[16,2048]{1,0:T(8,128)S(1)} %get-tuple-element.97.v.v1, ...), custom_call_target="tpu_custom_call" | custom-call | flops 2000000 | bytes 7000000 | tf_op jit(solution)/shard_map/local_product/pallas_call | solution.py:316
  67.2 1.6 %collective-permute-done.10 = f32[16,128]{1,0:T(8,128)S(1)} collective-permute-done((f32[16,128]{1,0:T(8,128)S(1)}, f32[16,128]{1,0:T(8,128)S(1)}, u32[]{:S(2)}, u32[]{:S(2)}) %collective-permute-start.10) | collective-permute-done | bytes 8224 | tf_op jit(solution)/shard_map/ppermute | solution.py:352
  68.7 1.3 %collective-permute-start.11 = (f32[16,128]{1,0:T(8,128)S(1)}, f32[16,128]{1,0:T(8,128)S(1)}, u32[]{:S(2)}, u32[]{:S(2)}) collective-permute-start(f32[16,128]{1,0:T(8,128)S(1)} %add.17), channel_id=1, source_target_pairs={{0,3},{1,2},{2,1},{3,0},{4,7},{5,6},{6,5},{7,4},{8,11},{9,10},{10,... | collective-permute-start | bytes 24584 | tf_op jit(solution)/shard_map/ppermute | solution.py:355
  70.1 3.6 %collective-permute-done.11 = f32[16,128]{1,0:T(8,128)S(1)} collective-permute-done((f32[16,128]{1,0:T(8,128)S(1)}, f32[16,128]{1,0:T(8,128)S(1)}, u32[]{:S(2)}, u32[]{:S(2)}) %collective-permute-start.11) | collective-permute-done | bytes 8224 | tf_op jit(solution)/shard_map/ppermute | solution.py:355
  73.6 15.7 %all_to_all.11.t = f32[32,16,128]{2,1,0:T(8,128)S(1)} all-to-all(f32[32,16,128]{2,1,0:T(8,128)S(1)} %broadcast_in_dim.9), channel_id=1, replica_groups=mesh['z'=8,'x'=4,'c'=2,'y'=4] {'z','x'}, dimensions={0} | all-to-all | bytes 524288 | tf_op jit(solution)/shard_map/all_to_all | solution.py:359
  89.3 3.6 %coarse_half.3.own = f32[16,1152]{1,0:T(8,128)S(1)} custom-call(f32[32,16,128]{2,1,0:T(8,128)S(1)} %all_to_all.11.t, f32[16,512]{1,0:T(8,128)S(1)} %get-tuple-element.109.near, bf16[512,2048]{1,0:T(8,128)(2,1)S(1)} %get-tuple-element.85.f_hi.rest_0_, bf16[512,2048]{1,0:T(8,128)(2,1)S(1)} %get-tuple-element.86.f_lo.rest_1_, ...), custom_call_target="tpu_custom_call" | custom-call | flops 4000000 | bytes 14000000 | tf_op jit(solution)/shard_map/coarse_half/pallas_call | solution.py:316
  93.0 1.3 %collective-permute-done.12.got = f32[16,1152]{1,0:T(8,128)S(1)} collective-permute-done((f32[16,1152]{1,0:T(8,128)S(1)}, f32[16,1152]{1,0:T(8,128)S(1)}, u32[]{:S(2)}, u32[]{:S(2)}) %collective-permute-start.12) | collective-permute-done | bytes 73760 | tf_op jit(solution)/shard_map/ppermute | solution.py:346
  95.1 4.2 %collective-permute-done.14.got.p1 = f32[16,896]{1,0:T(8,128)S(1)} collective-permute-done((f32[16,896]{1,0:T(8,128)S(1)}, f32[16,896]{1,0:T(8,128)S(1)}, u32[]{:S(2)}, u32[]{:S(2)}) %collective-permute-start.14) | collective-permute-done | bytes 57376 | tf_op jit(solution)/shard_map/ppermute | solution.py:352
  99.3 1.4 %collective-permute-start.15 = (f32[16,896]{1,0:T(8,128)S(1)}, f32[16,896]{1,0:T(8,128)S(1)}, u32[]{:S(2)}, u32[]{:S(2)}) collective-permute-start(f32[16,896]{1,0:T(8,128)S(1)} %second_part.3.sent), channel_id=1, source_target_pairs={{0,3},{1,2},{2,1},{3,0},{4,7},{5,6},{6,5},{7,4},{8,11},{9,10},{10,... | collective-permute-start | bytes 172040 | tf_op jit(solution)/shard_map/ppermute | solution.py:355
  100.9 5.3 %collective-permute-done.13.far = f32[16,512]{1,0:T(8,128)S(1)} collective-permute-done((f32[16,512]{1,0:T(8,128)S(1)}, f32[16,512]{1,0:T(8,128)S(1)}, u32[]{:S(2)}, u32[]{:S(2)}) %collective-permute-start.13) | collective-permute-done | bytes 32800 | tf_op jit(solution)/shard_map/ppermute | solution.py:349
  106.2 1.8 %finish.1 = (f32[16,2048]{1,0:T(8,128)}, f32[16,2048]{1,0:T(8,128)}) custom-call(s32[42]{0:T(128)S(1)} %concatenate.6.ints, f32[16,2048]{1,0:T(8,128)S(1)} %get-tuple-element.104.z1, f32[16,1152]{1,0:T(8,128)S(1)} %collective-permute-done.12.got, f32[16,512]{1,0:T(8,128)S(1)} %collective-permute-done.13.far, f32[16,896]{1,0:T(8,128)S(1)} %collective-permute-done.14.got.p1, ...), custom_call_target="tpu_custom_call" | custom-call | flops 1900000 | bytes 6650000 | tf_op jit(solution)/shard_map/finish/pallas_call | solution.py:316
  (28 shorter events, 3.7 us)
Async XLA Ops:
  3.8 10.3 %collective-permute-start = (f32[48,512]{1,0:T(8,128)S(1)}, f32[48,512]{1,0:T(8,128)S(1)}, u32[]{:S(2)}, u32[]{:S(2)}) collective-permute-start(f32[48,512]{1,0:T(8,128)S(1)} %get-tuple-element.61), channel_id=1, source_target_pairs={{0,4},{4,0},{1,5},{5,1},{2,6},{6,2},{3,7},{7,3},{8,12},{12,8},{9,1... | collective-permute-start | bytes 294920 | tf_op jit(solution)/shard_map/ppermute | solution.py:346
  4.0 10.2 %collective-permute-start.1 = (f32[48,512]{1,0:T(8,128)S(1)}, f32[48,512]{1,0:T(8,128)S(1)}, u32[]{:S(2)}, u32[]{:S(2)}) collective-permute-start(f32[48,512]{1,0:T(8,128)S(1)} %get-tuple-element.62), channel_id=1, source_target_pairs={{4,8},{12,16},{20,24},{28,32},{36,40},{44,48},{52,56},{60,64},{68,... | collective-permute-start | bytes 294920 | tf_op jit(solution)/shard_map/ppermute | solution.py:349
  6.4 7.8 %collective-permute-start.2 = (f32[40,512]{1,0:T(8,128)S(1)}, f32[40,512]{1,0:T(8,128)S(1)}, u32[]{:S(2)}, u32[]{:S(2)}) collective-permute-start(f32[40,512]{1,0:T(8,128)S(1)} %get-tuple-element.63), channel_id=1, source_target_pairs={{0,1},{1,0},{2,3},{3,2},{4,5},{5,4},{6,7},{7,6},{8,9},{9,8},{10,11... | collective-permute-start | bytes 245768 | tf_op jit(solution)/shard_map/ppermute | solution.py:352
  7.9 6.2 %collective-permute-start.3 = (f32[40,512]{1,0:T(8,128)S(1)}, f32[40,512]{1,0:T(8,128)S(1)}, u32[]{:S(2)}, u32[]{:S(2)}) collective-permute-start(f32[40,512]{1,0:T(8,128)S(1)} %get-tuple-element.64), channel_id=1, source_target_pairs={{0,3},{1,2},{2,1},{3,0},{4,7},{5,6},{6,5},{7,4},{8,11},{9,10},{10,... | collective-permute-start | bytes 245768 | tf_op jit(solution)/shard_map/ppermute | solution.py:355
  15.2 3.7 %collective-permute-start.4 = (f32[16,128]{1,0:T(8,128)S(1)}, f32[16,128]{1,0:T(8,128)S(1)}, u32[]{:S(2)}, u32[]{:S(2)}) collective-permute-start(f32[16,128]{1,0:T(8,128)S(1)} %get-tuple-element.69), channel_id=1, source_target_pairs={{0,1},{1,0},{2,3},{3,2},{4,5},{5,4},{6,7},{7,6},{8,9},{9,8},{10,11... | collective-permute-start | bytes 24584 | tf_op jit(solution)/shard_map/ppermute | solution.py:352
  16.0 27.9 %copy-start = (f32[512,2048]{1,0:T(8,128)S(1)}, f32[512,2048]{1,0:T(8,128)}, u32[]{:S(2)}) copy-start(f32[512,2048]{1,0:T(8,128)} %rest_0_.1) | copy-start | bytes 12582916
  19.0 4.9 %collective-permute-start.5 = (f32[16,128]{1,0:T(8,128)S(1)}, f32[16,128]{1,0:T(8,128)S(1)}, u32[]{:S(2)}, u32[]{:S(2)}) collective-permute-start(f32[16,128]{1,0:T(8,128)S(1)} %add.15), channel_id=1, source_target_pairs={{0,3},{1,2},{2,1},{3,0},{4,7},{5,6},{6,5},{7,4},{8,11},{9,10},{10,... | collective-permute-start | bytes 24584 | tf_op jit(solution)/shard_map/ppermute | solution.py:355
  48.2 2.6 %collective-permute-start.6 = (f32[16,1152]{1,0:T(8,128)S(1)}, f32[16,1152]{1,0:T(8,128)S(1)}, u32[]{:S(2)}, u32[]{:S(2)}) collective-permute-start(f32[16,1152]{1,0:T(8,128)S(1)} %get-tuple-element.82.own), channel_id=1, source_target_pairs={{0,4},{4,0},{1,5},{5,1},{2,6},{6,2},{3,7},{7,3},{8,12},{12,8},{9,1... | collective-permute-start | bytes 221192 | tf_op jit(solution)/shard_map/ppermute | solution.py:346
  51.6 4.6 %collective-permute-start.8 = (f32[16,896]{1,0:T(8,128)S(1)}, f32[16,896]{1,0:T(8,128)S(1)}, u32[]{:S(2)}, u32[]{:S(2)}) collective-permute-start(f32[16,896]{1,0:T(8,128)S(1)} %get-tuple-element.89.own), channel_id=1, source_target_pairs={{0,1},{1,0},{2,3},{3,2},{4,5},{5,4},{6,7},{7,6},{8,9},{9,8},{10,11... | collective-permute-start | bytes 172040 | tf_op jit(solution)/shard_map/ppermute | solution.py:352
  56.2 7.4 %collective-permute-start.9 = (f32[16,896]{1,0:T(8,128)S(1)}, f32[16,896]{1,0:T(8,128)S(1)}, u32[]{:S(2)}, u32[]{:S(2)}) collective-permute-start(f32[16,896]{1,0:T(8,128)S(1)} %second_part.2.sent), channel_id=1, source_target_pairs={{0,3},{1,2},{2,1},{3,0},{4,7},{5,6},{6,5},{7,4},{8,11},{9,10},{10,... | collective-permute-start | bytes 172040 | tf_op jit(solution)/shard_map/ppermute | solution.py:355
  58.1 5.4 %collective-permute-start.7 = (f32[16,512]{1,0:T(8,128)S(1)}, f32[16,512]{1,0:T(8,128)S(1)}, u32[]{:S(2)}, u32[]{:S(2)}) collective-permute-start(f32[16,512]{1,0:T(8,128)S(1)} %get-tuple-element.83), channel_id=1, source_target_pairs={{4,8},{12,16},{20,24},{28,32},{36,40},{44,48},{52,56},{60,64},{68,... | collective-permute-start | bytes 98312 | tf_op jit(solution)/shard_map/ppermute | solution.py:349
  65.0 3.7 %collective-permute-start.10 = (f32[16,128]{1,0:T(8,128)S(1)}, f32[16,128]{1,0:T(8,128)S(1)}, u32[]{:S(2)}, u32[]{:S(2)}) collective-permute-start(f32[16,128]{1,0:T(8,128)S(1)} %get-tuple-element.96), channel_id=1, source_target_pairs={{0,1},{1,0},{2,3},{3,2},{4,5},{5,4},{6,7},{7,6},{8,9},{9,8},{10,11... | collective-permute-start | bytes 24584 | tf_op jit(solution)/shard_map/ppermute | solution.py:352
  68.7 4.9 %collective-permute-start.11 = (f32[16,128]{1,0:T(8,128)S(1)}, f32[16,128]{1,0:T(8,128)S(1)}, u32[]{:S(2)}, u32[]{:S(2)}) collective-permute-start(f32[16,128]{1,0:T(8,128)S(1)} %add.17), channel_id=1, source_target_pairs={{0,3},{1,2},{2,1},{3,0},{4,7},{5,6},{6,5},{7,4},{8,11},{9,10},{10,... | collective-permute-start | bytes 24584 | tf_op jit(solution)/shard_map/ppermute | solution.py:355
  92.9 1.3 %collective-permute-start.12 = (f32[16,1152]{1,0:T(8,128)S(1)}, f32[16,1152]{1,0:T(8,128)S(1)}, u32[]{:S(2)}, u32[]{:S(2)}) collective-permute-start(f32[16,1152]{1,0:T(8,128)S(1)} %coarse_half.3.own), channel_id=1, source_target_pairs={{0,4},{4,0},{1,5},{5,1},{2,6},{6,2},{3,7},{7,3},{8,12},{12,8},{9,1... | collective-permute-start | bytes 221192 | tf_op jit(solution)/shard_map/ppermute | solution.py:346
  95.0 4.3 %collective-permute-start.14 = (f32[16,896]{1,0:T(8,128)S(1)}, f32[16,896]{1,0:T(8,128)S(1)}, u32[]{:S(2)}, u32[]{:S(2)}) collective-permute-start(f32[16,896]{1,0:T(8,128)S(1)} %get-tuple-element.114.own), channel_id=1, source_target_pairs={{0,1},{1,0},{2,3},{3,2},{4,5},{5,4},{6,7},{7,6},{8,9},{9,8},{10,11... | collective-permute-start | bytes 172040 | tf_op jit(solution)/shard_map/ppermute | solution.py:352
  99.3 6.9 %collective-permute-start.15 = (f32[16,896]{1,0:T(8,128)S(1)}, f32[16,896]{1,0:T(8,128)S(1)}, u32[]{:S(2)}, u32[]{:S(2)}) collective-permute-start(f32[16,896]{1,0:T(8,128)S(1)} %second_part.3.sent), channel_id=1, source_target_pairs={{0,3},{1,2},{2,1},{3,0},{4,7},{5,6},{6,5},{7,4},{8,11},{9,10},{10,... | collective-permute-start | bytes 172040 | tf_op jit(solution)/shard_map/ppermute | solution.py:355
  100.7 5.4 %collective-permute-start.13 = (f32[16,512]{1,0:T(8,128)S(1)}, f32[16,512]{1,0:T(8,128)S(1)}, u32[]{:S(2)}, u32[]{:S(2)}) collective-permute-start(f32[16,512]{1,0:T(8,128)S(1)} %get-tuple-element.112), channel_id=1, source_target_pairs={{4,8},{12,16},{20,24},{28,32},{36,40},{44,48},{52,56},{60,64},{68,... | collective-permute-start | bytes 98312 | tf_op jit(solution)/shard_map/ppermute | solution.py:349

commit v3 on v2

--- a/solution.py
+++ b/solution.py
@@ -16,6 +16,7 @@
 ALL = ("z", "x", "c", "y")
 SUB = ("z", "x", "c")
 FETCH = 44
+CHUNKS = 16
 
 NN = (((1,), (0,)), ((), ()))
 NT = (((1,), (1,)), ((), ()))
@@ -94,9 +95,9 @@
 
 
 def spread_coupling(ints, both, mat, bx_hi, bx_lo, weight, held, bx, sems):
-    rows = mat.shape[0] // 4
+    rows = mat.shape[0] // CHUNKS
     copies = []
-    for n in range(4):
+    for n in range(CHUNKS):
         at = pl.ds(n * rows, rows)
         copies.append(pltpu.make_async_copy(mat.at[at], held.at[at], sems.at[n]))
         copies[n].start()
@@ -236,7 +237,7 @@
     out[:, owned + BW :] = near[...]
 
 
-def coarse_part(final, ints, own, got, beside, c_hi, c_lo, out, scal):
+def coarse_part(final, ints, own, got, face_one, face_two, c_hi, c_lo, part, out_one, out_two, scal):
     owned = c_hi.shape[0]
     mid = own[:, 0:owned] + got[:, 0:owned]
     total = own[:, owned : owned + BW] + got[:, owned : owned + BW]
@@ -255,19 +256,15 @@
     else:
         scal[...] = jnp.broadcast_to(over(slot == NORM), (16, BW))
     width = picked.shape[1]
-    out[:, 0:width] = picked
-    out[:, width:] = beside[...]
-
-
-def second_part(own, got, beside, out):
-    width = own.shape[1] - beside.shape[1]
-    out[:, 0:width] = own[:, 0:width] + got[:, 0:width]
-    out[:, width:] = beside[...]
-
-
-def jumped(out, z, ints, got, far, p1, sent, p2, b_hi, b_lo):
-    width = sent.shape[1] - 4 * BW
-    picked = sent[:, 0:width] + p2[:, 0:width]
+    part[...] = picked
+    for out, beside in ((out_one, face_one), (out_two, face_two)):
+        out[:, 0:width] = picked
+        out[:, width:] = beside[...]
+
+
+def jumped(out, z, ints, got, far, p0, p1, p2, p3, b_hi, b_lo):
+    width = p0.shape[1]
+    picked = (p0[...] + p1[:, 0:width]) + (p2[...] + p3[:, 0:width])
     y = place_of(ints)[0]
     lane = lax.broadcasted_iota(jnp.int32, (16, BW), 1)
     beside = pltpu.roll(picked[:, BW : 2 * BW], (BW - y * LANES) % BW, 1)
@@ -276,14 +273,14 @@
     needed = jnp.concatenate([picked[:, 0:BW], beside], axis=1)
     out[...] = z[...] + dot3(needed, b_hi[...], b_lo[...], NN)
     near_at = got.shape[1] - 4 * BW
-    subtract_faces(out, ints, ((got, near_at), (far, 0), (p1, width), (p2, width)))
+    subtract_faces(out, ints, ((got, near_at), (far, 0), (p1, width), (p3, width)))
     return picked
 
 
 def next_vector(
-    ints, z0, got, far, p1, sent, p2, b_hi, b_lo, v0, bx_hi, bx_lo, weight, v1, pay
+    ints, z0, got, far, p0, p1, p2, p3, b_hi, b_lo, v0, bx_hi, bx_lo, weight, v1, pay
 ):
-    jumped(v1, z0, ints, got, far, p1, sent, p2, b_hi, b_lo)
+    jumped(v1, z0, ints, got, far, p0, p1, p2, p3, b_hi, b_lo)
     v = v1[...]
     w = v * weight[0:1, :]
     lane = lax.broadcasted_iota(jnp.int32, (16, BW), 1)
@@ -295,8 +292,8 @@
     )
 
 
-def finish(ints, z1, got, far, p1, sent, p2, b_hi, b_lo, v0, v1, s0, s1, mult, resid):
-    picked = jumped(resid, z1, ints, got, far, p1, sent, p2, b_hi, b_lo)
+def finish(ints, z1, got, far, p0, p1, p2, p3, b_hi, b_lo, v0, v1, s0, s1, mult, resid):
+    picked = jumped(resid, z1, ints, got, far, p0, p1, p2, p3, b_hi, b_lo)
     norm, cross, square = (s0[:, 0:1], s1[:, 0:1], s1[:, 1:2])
     energy = picked[:, NORM : NORM + 1]
     step1 = norm / cross
@@ -340,6 +337,7 @@
     far_pairs = [(i, (i + 1) % subs) for i in range(1, subs, 2)]
     far_pairs = far_pairs + [(j, i) for i, j in far_pairs]
     one_pairs = [(j, j ^ 1) for j in range(ys)]
+    across_pairs = [(j, j ^ 2) for j in range(ys)]
     two_pairs = [(j, j ^ 3) for j in range(ys)]
 
     def near(p):
@@ -350,6 +348,9 @@
 
     def one(p):
         return lax.ppermute(p, "y", one_pairs)
+
+    def across(p):
+        return lax.ppermute(p, "y", across_pairs)
 
     def two(p):
         return lax.ppermute(p, "y", two_pairs)
@@ -389,21 +390,18 @@
             mib=16,
         )
 
-    def rest_of_solve(final, own, face_one, face_two, *early):
+    def rest_of_solve(final, own, face_one, face_two):
         got = near(own)
-        sent, scal = call(
+        wide = 3 * BW
+        part, out_one, out_two, scal = call(
             functools.partial(coarse_part, final),
             "coarse_part",
-            (ints, own, got, face_one, c_hi, c_lo),
-            [((cases, 3 * BW + face), F32), ((cases, BW), F32)],
+            (ints, own, got, face_one, face_two, c_hi, c_lo),
+            [((cases, wide), F32)] + [((cases, wide + face), F32)] * 2 + [((cases, BW), F32)],
             1,
             1,
         )
-        p1, *early = lax.optimization_barrier((one(sent), *early))
-        (sent,) = call(
-            second_part, "second_part", (sent, p1, face_two), [((cases, 3 * BW + face), F32)], 0, 0.5
-        )
-        return early, scal, got, p1, sent, two(sent)
+        return scal, got, part, one(out_one), across(part), two(out_two)
 
     o0, o1, o2, o3, own_map = call(
         first_pack,
@@ -422,7 +420,7 @@
         [((BW, dofs), BF16)] * 2 + [((8, dofs), F32), ((dofs, dofs), BF16)],
         1,
         3,
-        [((BW, dofs), F32), pltpu.SemaphoreType.DMA((4,))],
+        [((BW, dofs), F32), pltpu.SemaphoreType.DMA((CHUNKS,))],
         mib=FETCH,
         outside=(2,),
     )
@@ -434,9 +432,10 @@
         1,
         1,
     )
-    came_one, z0, *faces = lax.optimization_barrier((one(pay), *product(False, v0)))
-    pair = pay + came_one
-    row = pair + two(pair)
+    rows = (across(pay), one(pay), two(pay))
+    *rows, z0, n0, f0, a0, b0 = lax.optimization_barrier((*rows, *product(False, v0)))
+    faces = (n0, f0, a0, b0)
+    row = (pay + rows[0]) + (rows[1] + rows[2])
     terms0, face_far = lax.optimization_barrier((gather(row), faces[1]))
     face_far = far(face_far)
     own, *held = half(True, terms0, faces[0], coarse_factor)
@@ -460,7 +459,7 @@
         [((2 * BW, dofs), F32)],
         mib=10,
     )
-    (b_hi, b_lo), scal0, got, *parts = rest_of_solve(False, own, faces[2], faces[3], b_hi, b_lo)
+    scal0, got, *parts = rest_of_solve(False, own, faces[2], faces[3])
     v1, pay = call(
         next_vector,
         "next_vector",
@@ -470,13 +469,14 @@
         1.6,
         mib=12,
     )
-    came_one, z1, *faces, local_dot = lax.optimization_barrier((one(pay), *product(True, v1)))
-    pair = pay + came_one
-    row = pair + two(pair) + local_dot
+    rows = (across(pay), one(pay), two(pay))
+    *rows, z1, n1, f1, a1, b1, local_dot = lax.optimization_barrier((*rows, *product(True, v1)))
+    faces = (n1, f1, a1, b1)
+    row = (pay + rows[0]) + (rows[1] + rows[2]) + local_dot
     terms1, face_far = lax.optimization_barrier((gather(row), faces[1]))
     face_far = far(face_far)
     (own,) = half(False, terms1, faces[0], *held)
-    _, scal1, got, *parts = rest_of_solve(True, own, faces[2], faces[3])
+    scal1, got, *parts = rest_of_solve(True, own, faces[2], faces[3])
     mult, resid = call(
         finish,
         "finish",

time: 109 us -> 103 us (0.945)
  waiting for transfers between devices: 27.8 us -> 8.34 us
  starting transfers between devices: 14.7 us -> 26.7 us
  blocking collectives: 35.7 us -> 37.5 us
    ppermute x5, waiting for transfers between devices: 9.68 us -> 0.01 us  [one(): return lax.ppermute(p, 'y', one_pairs)]
    ppermute x0 -> x4, starting transfers between devices: none -> 8.49 us  [across(): return lax.ppermute(p, 'y', across_pairs)]
    ppermute x5, waiting for transfers between devices: 6.85 us -> 0.01 us  [two(): return lax.ppermute(p, 'y', two_pairs)]
    ppermute x3, waiting for transfers between devices: 10 us -> 4.6 us  [far(): return lax.ppermute(p, SUB, far_pairs)]
    ppermute x0 -> x4, waiting for transfers between devices: none -> 2.46 us  [across(): return lax.ppermute(p, 'y', across_pairs)]
    ppermute x5, starting transfers between devices: 2.73 us -> 4.69 us  [one(): return lax.ppermute(p, 'y', one_pairs)]
    all_to_all x2, blocking collectives: 35.7 us -> 37.5 us  [gather(): return lax.all_to_all(every, ('z', 'x'), 0, 0)]
    ppermute x3, starting transfers between devices: 3.29 us -> 4.81 us  [far(): return lax.ppermute(p, SUB, far_pairs)]
  transfers between devices with their start and end apart: 16 -> 20, of which waited for: 9 -> 6; matrix products, arithmetic and copies ran while one was open for 0% -> 0% of each run, Pallas kernels for 11% -> 12%
where the time goes in v3:
time: 103 us; the launch traced here: 102 us
  blocking collectives  37.5 us (36%)
  starting transfers between devices  26.7 us (26%)
  Pallas kernels  26.3 us (26%)
  waiting for transfers between devices  8.34 us (8%)
  local copies, waits for them, and re-layouts  1.62 us (2%)
  other arithmetic  1.04 us (1%)
    all_to_all x2, blocking collectives, gather(): return lax.all_to_all(every, ('z', 'x'), 0, 0)  37.5 us
    pallas_call x13, Pallas kernels, call(): pl.pallas_call(kernel, out_shape=[jax.ShapeDtypeStruct(s, d) for s, d in...  26.3 us
    ppermute x4, starting transfers between devices, across(): return lax.ppermute(p, 'y', across_pairs)  8.49 us
    ppermute x5, starting transfers between devices, two(): return lax.ppermute(p, 'y', two_pairs)  8.48 us
    ppermute x3, starting transfers between devices, far(): return lax.ppermute(p, SUB, far_pairs)  4.81 us
    ppermute x5, starting transfers between devices, one(): return lax.ppermute(p, 'y', one_pairs)  4.69 us
    ppermute x3, waiting for transfers between devices, far(): return lax.ppermute(p, SUB, far_pairs)  4.6 us
    ppermute x4, waiting for transfers between devices, across(): return lax.ppermute(p, 'y', across_pairs)  2.46 us
  transfers between devices with their start and end apart: 20, of which 6 were waited for; matrix products, arithmetic and copies ran while one was open for 0% of the time, Pallas kernels for 12%

profile of v3, /device:TPU:32, one launch (start us, length us, event | category | flops | bytes accessed | tf_op | source)
XLA Modules:
  0.0 102.3 jit_solution(6225147366415797576)
XLA Ops:
  1.5 1.0 %pad_maximum_fusion.both = f32[40,2048]{1,0:T(8,128)S(1)} fusion(f32[24,2048]{1,0:T(8,128)} %bitcast.17, f32[16,2048]{1,0:T(8,128)} %bitcast.18), kind=kLoop, calls=%fused_computation | loop fusion | flops 81920 | bytes 655360 | tf_op jit(solution)/shard_map/concatenate | solution.py:328
  4.0 2.4 %collective-permute-start.1 = (f32[48,512]{1,0:T(8,128)S(1)}, f32[48,512]{1,0:T(8,128)S(1)}, u32[]{:S(2)}, u32[]{:S(2)}) collective-permute-start(f32[48,512]{1,0:T(8,128)S(1)} %get-tuple-element.67), channel_id=1, source_target_pairs={{4,8},{12,16},{20,24},{28,32},{36,40},{44,48},{52,56},{60,64},{68,... | collective-permute-start | bytes 294920 | tf_op jit(solution)/shard_map/ppermute | solution.py:347
  6.4 1.6 %collective-permute-start.2 = (f32[40,512]{1,0:T(8,128)S(1)}, f32[40,512]{1,0:T(8,128)S(1)}, u32[]{:S(2)}, u32[]{:S(2)}) collective-permute-start(f32[40,512]{1,0:T(8,128)S(1)} %get-tuple-element.68), channel_id=1, source_target_pairs={{0,1},{1,0},{2,3},{3,2},{4,5},{5,4},{6,7},{7,6},{8,9},{9,8},{10,11... | collective-permute-start | bytes 245768 | tf_op jit(solution)/shard_map/ppermute | solution.py:350
  7.9 2.2 %collective-permute-start.3 = (f32[40,512]{1,0:T(8,128)S(1)}, f32[40,512]{1,0:T(8,128)S(1)}, u32[]{:S(2)}, u32[]{:S(2)}) collective-permute-start(f32[40,512]{1,0:T(8,128)S(1)} %get-tuple-element.69), channel_id=1, source_target_pairs={{0,3},{1,2},{2,1},{3,0},{4,7},{5,6},{6,5},{7,4},{8,11},{9,10},{10,... | collective-permute-start | bytes 245768 | tf_op jit(solution)/shard_map/ppermute | solution.py:356
  10.1 4.1 %spread_coupling.1 = (bf16[128,2048]{1,0:T(8,128)(2,1)S(1)}, bf16[128,2048]{1,0:T(8,128)(2,1)S(1)}, f32[8,2048]{1,0:T(8,128)S(1)}, bf16[2048,2048]{1,0:T(8,128)(2,1)S(1)}) custom-call(s32[42]{0:T(128)S(1)} %concatenate.6.ints, f32[40,2048]{1,0:T(8,128)S(1)} %pad_maximum_fusion.both, bf16[2048,2048]{1,0:T(8,128)(2,1)} %bitcast.16), custom_call_target="tpu_custom_call" | custom-call | flops 3000000 | bytes 10500000 | tf_op jit(solution)/shard_map/spread_coupling/pallas_call | solution.py:313
  14.2 1.0 %first_vector.1 = (f32[16,2048]{1,0:T(8,128)S(1)}, f32[16,128]{1,0:T(8,128)S(1)}) custom-call(s32[42]{0:T(128)S(1)} %concatenate.6.ints, f32[40,2048]{1,0:T(8,128)S(1)} %pad_maximum_fusion.both, f32[48,512]{1,0:T(8,128)S(1)} %collective-permute-done.i0, f32[48,512]{1,0:T(8,128)S(1)} %collective-permute-done.1.i1, f32[40,512]{1,0:T(8,128)S(1)} %collective-permute-done.2.i2, ...), custom_call_target="tpu_custom_call" | custom-call | flops 1000000 | bytes 3500000 | tf_op jit(solution)/shard_map/first_vector/pallas_call | solution.py:313
  15.3 1.6 %collective-permute-start.6 = (f32[16,128]{1,0:T(8,128)S(1)}, f32[16,128]{1,0:T(8,128)S(1)}, u32[]{:S(2)}, u32[]{:S(2)}) collective-permute-start(f32[16,128]{1,0:T(8,128)S(1)} %get-tuple-element.74), channel_id=1, source_target_pairs={{0,3},{1,2},{2,1},{3,0},{4,7},{5,6},{6,5},{7,4},{8,11},{9,10},{10,... | collective-permute-start | bytes 24584 | tf_op jit(solution)/shard_map/ppermute | solution.py:356
  16.9 3.1 %collective-permute-start.4 = (f32[16,128]{1,0:T(8,128)S(1)}, f32[16,128]{1,0:T(8,128)S(1)}, u32[]{:S(2)}, u32[]{:S(2)}) collective-permute-start(f32[16,128]{1,0:T(8,128)S(1)} %get-tuple-element.74), channel_id=1, source_target_pairs={{0,2},{1,3},{2,0},{3,1},{4,6},{5,7},{6,4},{7,5},{8,10},{9,11},{10,... | collective-permute-start | bytes 24584 | tf_op jit(solution)/shard_map/ppermute | solution.py:353
  20.0 2.0 %local_product.2 = (f32[16,2048]{1,0:T(8,128)S(1)}, f32[16,512]{1,0:T(8,128)S(1)}, f32[16,512]{1,0:T(8,128)S(1)}, f32[16,512]{1,0:T(8,128)S(1)}, f32[16,512]{1,0:T(8,128)S(1)}) custom-call(s32[42]{0:T(128)S(1)} %concatenate.6.ints, f32[16,2048]{1,0:T(8,128)S(1)} %get-tuple-element.75.v.v0, bf16[2048,2048]{1,0:T(8,128)(2,1)S(1)} %get-tuple-element.76.mat), custom_call_target="tpu_custom_call" | custom-call | flops 2000000 | bytes 7000000 | tf_op jit(solution)/shard_map/local_product/pallas_call | solution.py:313
  22.1 20.8 %all_to_all.10.t = f32[32,16,128]{2,1,0:T(8,128)S(1)} all-to-all(f32[32,16,128]{2,1,0:T(8,128)S(1)} %broadcast_in_dim.8), channel_id=1, replica_groups=mesh['z'=8,'x'=4,'c'=2,'y'=4] {'z','x'}, dimensions={0} | all-to-all | bytes 524288 | tf_op jit(solution)/shard_map/all_to_all | solution.py:360
  42.9 4.3 %coarse_half.2 = (f32[16,1152]{1,0:T(8,128)S(1)}, bf16[512,2048]{1,0:T(8,128)(2,1)S(1)}, bf16[512,2048]{1,0:T(8,128)(2,1)S(1)}, f32[32,128]{1,0:T(8,128)S(1)}, bf16[4096,256]{1,0:T(8,128)(2,1)S(1)}) custom-call(f32[32,16,128]{2,1,0:T(8,128)S(1)} %all_to_all.10.t, f32[16,512]{1,0:T(8,128)S(1)} %get-tuple-element.88.near, f32[512,2048]{1,0:T(8,128)S(1)} %copy-done), custom_call_target="tpu_custom_call" | custom-call | flops 4000000 | bytes 14000000 | tf_op jit(solution)/shard_map/coarse_half/pallas_call | solution.py:313
  47.4 2.5 %picked_columns.1 = (bf16[512,384]{1,0:T(8,128)(2,1)S(1)}, bf16[512,384]{1,0:T(8,128)(2,1)S(1)}) custom-call(f32[16,128]{1,0:T(8,128)S(1)} %add_add_fusion.1.pay, bf16[512,2048]{1,0:T(8,128)(2,1)S(1)} %get-tuple-element.93.f_hi.rest_0_, bf16[512,2048]{1,0:T(8,128)(2,1)S(1)} %get-tuple-element.94.f_lo.rest_1_), custom_call_target="tpu_custom_call" | custom-call | flops 2500000 | bytes 8750000 | tf_op jit(solution)/shard_map/picked_columns/pallas_call | solution.py:313
  50.6 1.6 %collective-permute-start.9 = (f32[16,896]{1,0:T(8,128)S(1)}, f32[16,896]{1,0:T(8,128)S(1)}, u32[]{:S(2)}, u32[]{:S(2)}) collective-permute-start(f32[16,896]{1,0:T(8,128)S(1)} %get-tuple-element.98), channel_id=1, source_target_pairs={{0,1},{1,0},{2,3},{3,2},{4,5},{5,4},{6,7},{7,6},{8,9},{9,8},{10,11... | collective-permute-start | bytes 172040 | tf_op jit(solution)/shard_map/ppermute | solution.py:350
  52.3 1.4 %collective-permute-start.11 = (f32[16,896]{1,0:T(8,128)S(1)}, f32[16,896]{1,0:T(8,128)S(1)}, u32[]{:S(2)}, u32[]{:S(2)}) collective-permute-start(f32[16,896]{1,0:T(8,128)S(1)} %get-tuple-element.99), channel_id=1, source_target_pairs={{0,3},{1,2},{2,1},{3,0},{4,7},{5,6},{6,5},{7,4},{8,11},{9,10},{10,... | collective-permute-start | bytes 172040 | tf_op jit(solution)/shard_map/ppermute | solution.py:356
  53.6 1.3 %collective-permute-start.8 = (f32[16,512]{1,0:T(8,128)S(1)}, f32[16,512]{1,0:T(8,128)S(1)}, u32[]{:S(2)}, u32[]{:S(2)}) collective-permute-start(f32[16,512]{1,0:T(8,128)S(1)} %get-tuple-element.90), channel_id=1, source_target_pairs={{4,8},{12,16},{20,24},{28,32},{36,40},{44,48},{52,56},{60,64},{68,... | collective-permute-start | bytes 98312 | tf_op jit(solution)/shard_map/ppermute | solution.py:347
  54.9 1.3 %collective-permute-start.10 = (f32[16,384]{1,0:T(8,128)S(1)}, f32[16,384]{1,0:T(8,128)S(1)}, u32[]{:S(2)}, u32[]{:S(2)}) collective-permute-start(f32[16,384]{1,0:T(8,128)S(1)} %get-tuple-element.97.p0), channel_id=1, source_target_pairs={{0,2},{1,3},{2,0},{3,1},{4,6},{5,7},{6,4},{7,5},{8,10},{9,11},{10,... | collective-permute-start | bytes 73736 | tf_op jit(solution)/shard_map/ppermute | solution.py:353
  56.2 1.3 %jumped_coupling.1 = (bf16[256,2048]{1,0:T(8,128)(2,1)S(1)}, bf16[256,2048]{1,0:T(8,128)(2,1)S(1)}) custom-call(s32[42]{0:T(128)S(1)} %concatenate.6.ints, f32[40,2048]{1,0:T(8,128)S(1)} %pad_maximum_fusion.both, f32[48,512]{1,0:T(8,128)S(1)} %collective-permute-done.i0, f32[48,512]{1,0:T(8,128)S(1)} %collective-permute-done.1.i1, ...), custom_call_target="tpu_custom_call" | custom-call | flops 1200000 | bytes 4200000 | tf_op jit(solution)/shard_map/jumped_coupling/pallas_call | solution.py:313
  57.6 1.5 %collective-permute-done.8.far = f32[16,512]{1,0:T(8,128)S(1)} collective-permute-done((f32[16,512]{1,0:T(8,128)S(1)}, f32[16,512]{1,0:T(8,128)S(1)}, u32[]{:S(2)}, u32[]{:S(2)}) %collective-permute-start.8) | collective-permute-done | bytes 32800 | tf_op jit(solution)/shard_map/ppermute | solution.py:347
  59.1 1.2 %collective-permute-done.10.p2 = f32[16,384]{1,0:T(8,128)S(1)} collective-permute-done((f32[16,384]{1,0:T(8,128)S(1)}, f32[16,384]{1,0:T(8,128)S(1)}, u32[]{:S(2)}, u32[]{:S(2)}) %collective-permute-start.10) | collective-permute-done | bytes 24608 | tf_op jit(solution)/shard_map/ppermute | solution.py:353
  60.3 1.5 %next_vector.1 = (f32[16,2048]{1,0:T(8,128)S(1)}, f32[16,128]{1,0:T(8,128)S(1)}) custom-call(s32[42]{0:T(128)S(1)} %concatenate.6.ints, f32[16,2048]{1,0:T(8,128)S(1)} %get-tuple-element.82.z0, f32[16,1152]{1,0:T(8,128)S(1)} %collective-permute-done.7.got, f32[16,512]{1,0:T(8,128)S(1)} %collective-permute-done.8.far, f32[16,384]{1,0:T(8,128)S(1)} %get-tuple-element.97.p0, ...), custom_call_target="tpu_custom_call" | custom-call | flops 1600000 | bytes 5600000 | tf_op jit(solution)/shard_map/next_vector/pallas_call | solution.py:313
  61.8 2.0 %collective-permute-start.14 = (f32[16,128]{1,0:T(8,128)S(1)}, f32[16,128]{1,0:T(8,128)S(1)}, u32[]{:S(2)}, u32[]{:S(2)}) collective-permute-start(f32[16,128]{1,0:T(8,128)S(1)} %get-tuple-element.102), channel_id=1, source_target_pairs={{0,3},{1,2},{2,1},{3,0},{4,7},{5,6},{6,5},{7,4},{8,11},{9,10},{10,... | collective-permute-start | bytes 24584 | tf_op jit(solution)/shard_map/ppermute | solution.py:356
  63.7 2.8 %collective-permute-start.12 = (f32[16,128]{1,0:T(8,128)S(1)}, f32[16,128]{1,0:T(8,128)S(1)}, u32[]{:S(2)}, u32[]{:S(2)}) collective-permute-start(f32[16,128]{1,0:T(8,128)S(1)} %get-tuple-element.102), channel_id=1, source_target_pairs={{0,2},{1,3},{2,0},{3,1},{4,6},{5,7},{6,4},{7,5},{8,10},{9,11},{10,... | collective-permute-start | bytes 24584 | tf_op jit(solution)/shard_map/ppermute | solution.py:353
  66.5 2.1 %local_product.3 = (f32[16,2048]{1,0:T(8,128)S(1)}, f32[16,512]{1,0:T(8,128)S(1)}, f32[16,512]{1,0:T(8,128)S(1)}, f32[16,512]{1,0:T(8,128)S(1)}, f32[16,512]{1,0:T(8,128)S(1)}, /*index=5*/f32[16,128]{1,0:T(8,128)S(1)}) custom-call(s32[42]{0:T(128)S(1)} %concatenate.6.ints, f32[16,2048]{1,0:T(8,128)S(1)} %get-tuple-element.103.v.v1, ...), custom_call_target="tpu_custom_call" | custom-call | flops 2000000 | bytes 7000000 | tf_op jit(solution)/shard_map/local_product/pallas_call | solution.py:313
  68.9 16.6 %all_to_all.11.t = f32[32,16,128]{2,1,0:T(8,128)S(1)} all-to-all(f32[32,16,128]{2,1,0:T(8,128)S(1)} %broadcast_in_dim.9), channel_id=1, replica_groups=mesh['z'=8,'x'=4,'c'=2,'y'=4] {'z','x'}, dimensions={0} | all-to-all | bytes 524288 | tf_op jit(solution)/shard_map/all_to_all | solution.py:360
  85.5 3.6 %coarse_half.3.own = f32[16,1152]{1,0:T(8,128)S(1)} custom-call(f32[32,16,128]{2,1,0:T(8,128)S(1)} %all_to_all.11.t, f32[16,512]{1,0:T(8,128)S(1)} %get-tuple-element.117.near, bf16[512,2048]{1,0:T(8,128)(2,1)S(1)} %get-tuple-element.93.f_hi.rest_0_, bf16[512,2048]{1,0:T(8,128)(2,1)S(1)} %get-tuple-element.94.f_lo.rest_1_, ...), custom_call_target="tpu_custom_call" | custom-call | flops 4000000 | bytes 14000000 | tf_op jit(solution)/shard_map/coarse_half/pallas_call | solution.py:313
  89.2 1.3 %collective-permute-done.15.got = f32[16,1152]{1,0:T(8,128)S(1)} collective-permute-done((f32[16,1152]{1,0:T(8,128)S(1)}, f32[16,1152]{1,0:T(8,128)S(1)}, u32[]{:S(2)}, u32[]{:S(2)}) %collective-permute-start.15) | collective-permute-done | bytes 73760 | tf_op jit(solution)/shard_map/ppermute | solution.py:344
  91.2 1.5 %collective-permute-start.17 = (f32[16,896]{1,0:T(8,128)S(1)}, f32[16,896]{1,0:T(8,128)S(1)}, u32[]{:S(2)}, u32[]{:S(2)}) collective-permute-start(f32[16,896]{1,0:T(8,128)S(1)} %get-tuple-element.124), channel_id=1, source_target_pairs={{0,1},{1,0},{2,3},{3,2},{4,5},{5,4},{6,7},{7,6},{8,9},{9,8},{10,11... | collective-permute-start | bytes 172040 | tf_op jit(solution)/shard_map/ppermute | solution.py:350
  92.7 1.4 %collective-permute-start.19 = (f32[16,896]{1,0:T(8,128)S(1)}, f32[16,896]{1,0:T(8,128)S(1)}, u32[]{:S(2)}, u32[]{:S(2)}) collective-permute-start(f32[16,896]{1,0:T(8,128)S(1)} %get-tuple-element.125), channel_id=1, source_target_pairs={{0,3},{1,2},{2,1},{3,0},{4,7},{5,6},{6,5},{7,4},{8,11},{9,10},{10,... | collective-permute-start | bytes 172040 | tf_op jit(solution)/shard_map/ppermute | solution.py:356
  94.1 1.1 %collective-permute-start.16 = (f32[16,512]{1,0:T(8,128)S(1)}, f32[16,512]{1,0:T(8,128)S(1)}, u32[]{:S(2)}, u32[]{:S(2)}) collective-permute-start(f32[16,512]{1,0:T(8,128)S(1)} %get-tuple-element.120), channel_id=1, source_target_pairs={{4,8},{12,16},{20,24},{28,32},{36,40},{44,48},{52,56},{60,64},{68,... | collective-permute-start | bytes 98312 | tf_op jit(solution)/shard_map/ppermute | solution.py:347
  95.2 1.3 %collective-permute-start.18 = (f32[16,384]{1,0:T(8,128)S(1)}, f32[16,384]{1,0:T(8,128)S(1)}, u32[]{:S(2)}, u32[]{:S(2)}) collective-permute-start(f32[16,384]{1,0:T(8,128)S(1)} %get-tuple-element.123.p0), channel_id=1, source_target_pairs={{0,2},{1,3},{2,0},{3,1},{4,6},{5,7},{6,4},{7,5},{8,10},{9,11},{10,... | collective-permute-start | bytes 73736 | tf_op jit(solution)/shard_map/ppermute | solution.py:353
  96.4 3.1 %collective-permute-done.16.far = f32[16,512]{1,0:T(8,128)S(1)} collective-permute-done((f32[16,512]{1,0:T(8,128)S(1)}, f32[16,512]{1,0:T(8,128)S(1)}, u32[]{:S(2)}, u32[]{:S(2)}) %collective-permute-start.16) | collective-permute-done | bytes 32800 | tf_op jit(solution)/shard_map/ppermute | solution.py:347
  100.5 1.8 %finish.1 = (f32[16,2048]{1,0:T(8,128)}, f32[16,2048]{1,0:T(8,128)}) custom-call(s32[42]{0:T(128)S(1)} %concatenate.6.ints, f32[16,2048]{1,0:T(8,128)S(1)} %get-tuple-element.110.z1, f32[16,1152]{1,0:T(8,128)S(1)} %collective-permute-done.15.got, f32[16,512]{1,0:T(8,128)S(1)} %collective-permute-done.16.far, f32[16,384]{1,0:T(8,128)S(1)} %get-tuple-element.123.p0, ...), custom_call_target="tpu_custom_call" | custom-call | flops 1900000 | bytes 6650000 | tf_op jit(solution)/shard_map/finish/pallas_call | solution.py:313
  (32 shorter events, 5.3 us)
Async XLA Ops:
  3.8 10.3 %collective-permute-start = (f32[48,512]{1,0:T(8,128)S(1)}, f32[48,512]{1,0:T(8,128)S(1)}, u32[]{:S(2)}, u32[]{:S(2)}) collective-permute-start(f32[48,512]{1,0:T(8,128)S(1)} %get-tuple-element.66), channel_id=1, source_target_pairs={{0,4},{4,0},{1,5},{5,1},{2,6},{6,2},{3,7},{7,3},{8,12},{12,8},{9,1... | collective-permute-start | bytes 294920 | tf_op jit(solution)/shard_map/ppermute | solution.py:344
  4.0 10.3 %collective-permute-start.1 = (f32[48,512]{1,0:T(8,128)S(1)}, f32[48,512]{1,0:T(8,128)S(1)}, u32[]{:S(2)}, u32[]{:S(2)}) collective-permute-start(f32[48,512]{1,0:T(8,128)S(1)} %get-tuple-element.67), channel_id=1, source_target_pairs={{4,8},{12,16},{20,24},{28,32},{36,40},{44,48},{52,56},{60,64},{68,... | collective-permute-start | bytes 294920 | tf_op jit(solution)/shard_map/ppermute | solution.py:347
  6.4 7.8 %collective-permute-start.2 = (f32[40,512]{1,0:T(8,128)S(1)}, f32[40,512]{1,0:T(8,128)S(1)}, u32[]{:S(2)}, u32[]{:S(2)}) collective-permute-start(f32[40,512]{1,0:T(8,128)S(1)} %get-tuple-element.68), channel_id=1, source_target_pairs={{0,1},{1,0},{2,3},{3,2},{4,5},{5,4},{6,7},{7,6},{8,9},{9,8},{10,11... | collective-permute-start | bytes 245768 | tf_op jit(solution)/shard_map/ppermute | solution.py:350
  7.9 6.3 %collective-permute-start.3 = (f32[40,512]{1,0:T(8,128)S(1)}, f32[40,512]{1,0:T(8,128)S(1)}, u32[]{:S(2)}, u32[]{:S(2)}) collective-permute-start(f32[40,512]{1,0:T(8,128)S(1)} %get-tuple-element.69), channel_id=1, source_target_pairs={{0,3},{1,2},{2,1},{3,0},{4,7},{5,6},{6,5},{7,4},{8,11},{9,10},{10,... | collective-permute-start | bytes 245768 | tf_op jit(solution)/shard_map/ppermute | solution.py:356
  15.3 6.8 %collective-permute-start.6 = (f32[16,128]{1,0:T(8,128)S(1)}, f32[16,128]{1,0:T(8,128)S(1)}, u32[]{:S(2)}, u32[]{:S(2)}) collective-permute-start(f32[16,128]{1,0:T(8,128)S(1)} %get-tuple-element.74), channel_id=1, source_target_pairs={{0,3},{1,2},{2,1},{3,0},{4,7},{5,6},{6,5},{7,4},{8,11},{9,10},{10,... | collective-permute-start | bytes 24584 | tf_op jit(solution)/shard_map/ppermute | solution.py:356
  16.9 5.2 %collective-permute-start.5 = (f32[16,128]{1,0:T(8,128)S(1)}, f32[16,128]{1,0:T(8,128)S(1)}, u32[]{:S(2)}, u32[]{:S(2)}) collective-permute-start(f32[16,128]{1,0:T(8,128)S(1)} %get-tuple-element.74), channel_id=1, source_target_pairs={{0,1},{1,0},{2,3},{3,2},{4,5},{5,4},{6,7},{7,6},{8,9},{9,8},{10,11... | collective-permute-start | bytes 24584 | tf_op jit(solution)/shard_map/ppermute | solution.py:350
  16.9 5.2 %collective-permute-start.4 = (f32[16,128]{1,0:T(8,128)S(1)}, f32[16,128]{1,0:T(8,128)S(1)}, u32[]{:S(2)}, u32[]{:S(2)}) collective-permute-start(f32[16,128]{1,0:T(8,128)S(1)} %get-tuple-element.74), channel_id=1, source_target_pairs={{0,2},{1,3},{2,0},{3,1},{4,6},{5,7},{6,4},{7,5},{8,10},{9,11},{10,... | collective-permute-start | bytes 24584 | tf_op jit(solution)/shard_map/ppermute | solution.py:353
  20.0 22.9 %copy-start = (f32[512,2048]{1,0:T(8,128)S(1)}, f32[512,2048]{1,0:T(8,128)}, u32[]{:S(2)}) copy-start(f32[512,2048]{1,0:T(8,128)} %rest_0_.1) | copy-start | bytes 12582916
  47.3 2.6 %collective-permute-start.7 = (f32[16,1152]{1,0:T(8,128)S(1)}, f32[16,1152]{1,0:T(8,128)S(1)}, u32[]{:S(2)}, u32[]{:S(2)}) collective-permute-start(f32[16,1152]{1,0:T(8,128)S(1)} %get-tuple-element.89.own), channel_id=1, source_target_pairs={{0,4},{4,0},{1,5},{5,1},{2,6},{6,2},{3,7},{7,3},{8,12},{12,8},{9,1... | collective-permute-start | bytes 221192 | tf_op jit(solution)/shard_map/ppermute | solution.py:344
  50.6 9.7 %collective-permute-start.9 = (f32[16,896]{1,0:T(8,128)S(1)}, f32[16,896]{1,0:T(8,128)S(1)}, u32[]{:S(2)}, u32[]{:S(2)}) collective-permute-start(f32[16,896]{1,0:T(8,128)S(1)} %get-tuple-element.98), channel_id=1, source_target_pairs={{0,1},{1,0},{2,3},{3,2},{4,5},{5,4},{6,7},{7,6},{8,9},{9,8},{10,11... | collective-permute-start | bytes 172040 | tf_op jit(solution)/shard_map/ppermute | solution.py:350
  52.3 8.0 %collective-permute-start.11 = (f32[16,896]{1,0:T(8,128)S(1)}, f32[16,896]{1,0:T(8,128)S(1)}, u32[]{:S(2)}, u32[]{:S(2)}) collective-permute-start(f32[16,896]{1,0:T(8,128)S(1)} %get-tuple-element.99), channel_id=1, source_target_pairs={{0,3},{1,2},{2,1},{3,0},{4,7},{5,6},{6,5},{7,4},{8,11},{9,10},{10,... | collective-permute-start | bytes 172040 | tf_op jit(solution)/shard_map/ppermute | solution.py:356
  53.6 5.4 %collective-permute-start.8 = (f32[16,512]{1,0:T(8,128)S(1)}, f32[16,512]{1,0:T(8,128)S(1)}, u32[]{:S(2)}, u32[]{:S(2)}) collective-permute-start(f32[16,512]{1,0:T(8,128)S(1)} %get-tuple-element.90), channel_id=1, source_target_pairs={{4,8},{12,16},{20,24},{28,32},{36,40},{44,48},{52,56},{60,64},{68,... | collective-permute-start | bytes 98312 | tf_op jit(solution)/shard_map/ppermute | solution.py:347
  54.9 5.3 %collective-permute-start.10 = (f32[16,384]{1,0:T(8,128)S(1)}, f32[16,384]{1,0:T(8,128)S(1)}, u32[]{:S(2)}, u32[]{:S(2)}) collective-permute-start(f32[16,384]{1,0:T(8,128)S(1)} %get-tuple-element.97.p0), channel_id=1, source_target_pairs={{0,2},{1,3},{2,0},{3,1},{4,6},{5,7},{6,4},{7,5},{8,10},{9,11},{10,... | collective-permute-start | bytes 73736 | tf_op jit(solution)/shard_map/ppermute | solution.py:353
  61.8 6.8 %collective-permute-start.14 = (f32[16,128]{1,0:T(8,128)S(1)}, f32[16,128]{1,0:T(8,128)S(1)}, u32[]{:S(2)}, u32[]{:S(2)}) collective-permute-start(f32[16,128]{1,0:T(8,128)S(1)} %get-tuple-element.102), channel_id=1, source_target_pairs={{0,3},{1,2},{2,1},{3,0},{4,7},{5,6},{6,5},{7,4},{8,11},{9,10},{10,... | collective-permute-start | bytes 24584 | tf_op jit(solution)/shard_map/ppermute | solution.py:356
  63.7 4.9 %collective-permute-start.13 = (f32[16,128]{1,0:T(8,128)S(1)}, f32[16,128]{1,0:T(8,128)S(1)}, u32[]{:S(2)}, u32[]{:S(2)}) collective-permute-start(f32[16,128]{1,0:T(8,128)S(1)} %get-tuple-element.102), channel_id=1, source_target_pairs={{0,1},{1,0},{2,3},{3,2},{4,5},{5,4},{6,7},{7,6},{8,9},{9,8},{10,11... | collective-permute-start | bytes 24584 | tf_op jit(solution)/shard_map/ppermute | solution.py:350
  63.7 5.2 %collective-permute-start.12 = (f32[16,128]{1,0:T(8,128)S(1)}, f32[16,128]{1,0:T(8,128)S(1)}, u32[]{:S(2)}, u32[]{:S(2)}) collective-permute-start(f32[16,128]{1,0:T(8,128)S(1)} %get-tuple-element.102), channel_id=1, source_target_pairs={{0,2},{1,3},{2,0},{3,1},{4,6},{5,7},{6,4},{7,5},{8,10},{9,11},{10,... | collective-permute-start | bytes 24584 | tf_op jit(solution)/shard_map/ppermute | solution.py:353
  89.1 1.3 %collective-permute-start.15 = (f32[16,1152]{1,0:T(8,128)S(1)}, f32[16,1152]{1,0:T(8,128)S(1)}, u32[]{:S(2)}, u32[]{:S(2)}) collective-permute-start(f32[16,1152]{1,0:T(8,128)S(1)} %coarse_half.3.own), channel_id=1, source_target_pairs={{0,4},{4,0},{1,5},{5,1},{2,6},{6,2},{3,7},{7,3},{8,12},{12,8},{9,1... | collective-permute-start | bytes 221192 | tf_op jit(solution)/shard_map/ppermute | solution.py:344
  91.2 9.3 %collective-permute-start.17 = (f32[16,896]{1,0:T(8,128)S(1)}, f32[16,896]{1,0:T(8,128)S(1)}, u32[]{:S(2)}, u32[]{:S(2)}) collective-permute-start(f32[16,896]{1,0:T(8,128)S(1)} %get-tuple-element.124), channel_id=1, source_target_pairs={{0,1},{1,0},{2,3},{3,2},{4,5},{5,4},{6,7},{7,6},{8,9},{9,8},{10,11... | collective-permute-start | bytes 172040 | tf_op jit(solution)/shard_map/ppermute | solution.py:350
  92.7 7.8 %collective-permute-start.19 = (f32[16,896]{1,0:T(8,128)S(1)}, f32[16,896]{1,0:T(8,128)S(1)}, u32[]{:S(2)}, u32[]{:S(2)}) collective-permute-start(f32[16,896]{1,0:T(8,128)S(1)} %get-tuple-element.125), channel_id=1, source_target_pairs={{0,3},{1,2},{2,1},{3,0},{4,7},{5,6},{6,5},{7,4},{8,11},{9,10},{10,... | collective-permute-start | bytes 172040 | tf_op jit(solution)/shard_map/ppermute | solution.py:356
  94.1 5.4 %collective-permute-start.16 = (f32[16,512]{1,0:T(8,128)S(1)}, f32[16,512]{1,0:T(8,128)S(1)}, u32[]{:S(2)}, u32[]{:S(2)}) collective-permute-start(f32[16,512]{1,0:T(8,128)S(1)} %get-tuple-element.120), channel_id=1, source_target_pairs={{4,8},{12,16},{20,24},{28,32},{36,40},{44,48},{52,56},{60,64},{68,... | collective-permute-start | bytes 98312 | tf_op jit(solution)/shard_map/ppermute | solution.py:347
  95.2 5.3 %collective-permute-start.18 = (f32[16,384]{1,0:T(8,128)S(1)}, f32[16,384]{1,0:T(8,128)S(1)}, u32[]{:S(2)}, u32[]{:S(2)}) collective-permute-start(f32[16,384]{1,0:T(8,128)S(1)} %get-tuple-element.123.p0), channel_id=1, source_target_pairs={{0,2},{1,3},{2,0},{3,1},{4,6},{5,7},{6,4},{7,5},{8,10},{9,11},{10,... | collective-permute-start | bytes 73736 | tf_op jit(solution)/shard_map/ppermute | solution.py:353

commit v4 on v3

--- a/solution.py
+++ b/solution.py
@@ -16,7 +16,7 @@
 ALL = ("z", "x", "c", "y")
 SUB = ("z", "x", "c")
 FETCH = 44
-CHUNKS = 16
+CHUNKS = 8
 
 NN = (((1,), (0,)), ((), ()))
 NT = (((1,), (1,)), ((), ()))
@@ -46,7 +46,7 @@
 
 
 def place_of(ints):
-    return ints[ints.shape[0] - 2], ints[ints.shape[0] - 1]
+    return ints[0, 40], ints[0, 41]
 
 
 def faces_of(ints):
@@ -58,7 +58,7 @@
 def subtract_faces(ref, ints, incoming):
     for f, (got, col0) in zip(faces_of(ints), incoming):
         for c in range(4):
-            b = ints[f * 4 + c]
+            b = ints[0, f * 4 + c]
             at = block_at(b)
             held = ref[:, at]
             ref[:, at] = jnp.where(b >= 0, held - got[0:16, col0 + c * BW : col0 + (c + 1) * BW], held)
@@ -67,7 +67,7 @@
 def pack_face(values, ints, f, out):
     rows = values.shape[0]
     for c in range(4):
-        out[0:rows, c * BW : (c + 1) * BW] = values[:, block_at(ints[f * 4 + c])]
+        out[0:rows, c * BW : (c + 1) * BW] = values[:, block_at(ints[0, f * 4 + c])]
 
 
 def lane_sum(x):
@@ -78,29 +78,46 @@
     return jnp.where(lane == y * LANES + slot, column, 0.0)
 
 
-def first_pack(ints, both, o0, o1, o2, o3, own_map):
+def first_pack(table, both, o0, o1, o2, o3, own_map, ints):
+    flat = [table[f, c] for f in range(4) for c in range(4)]
+    flat = flat + [table[4, j] for j in range(24)] + [table[5, 0], table[5, 1]]
     row = lax.broadcasted_iota(jnp.int32, (8, BW), 0)
-    lane = lax.broadcasted_iota(jnp.int32, (8, BW), 1) - (place_of(ints)[0] * LANES + MAP)
+    at = lax.broadcasted_iota(jnp.int32, (8, BW), 1)
+    every = jnp.zeros((8, BW), jnp.int32)
+    for n, value in enumerate(flat):
+        every = jnp.where(at == n, value, every)
+    ints[...] = every[0:1, :]
+    y, core = (flat[40], flat[41])
+    lane = at - (y * LANES + MAP)
     placed = jnp.zeros((8, BW), jnp.int32)
     for j in range(24):
         here = jnp.logical_and(row == j // PER, lane == j % PER)
-        placed = jnp.where(here, ints[16 + j], placed)
+        placed = jnp.where(here, flat[16 + j], placed)
     placed = placed.astype(F32)
     own_map[...] = placed
-    for f, o in zip(faces_of(ints), (o0, o1, o2, o3)):
-        pack_face(both, ints, f, o)
+    for f, o in zip((1 - core, core, 3 - y % 2, 2 + y % 2), (o0, o1, o2, o3)):
+        for c in range(4):
+            o[0:40, c * BW : (c + 1) * BW] = both[:, block_at(table[f, c])]
     for o in (o0, o1):
         o[40:48, 0:BW] = placed
         o[40:48, BW:] = jnp.zeros((8, 3 * BW), F32)
 
 
-def spread_coupling(ints, both, mat, bx_hi, bx_lo, weight, held, bx, sems):
-    rows = mat.shape[0] // CHUNKS
+def fetches(mat, row0, held, sems):
+    rows = held.shape[0] // CHUNKS
     copies = []
     for n in range(CHUNKS):
-        at = pl.ds(n * rows, rows)
-        copies.append(pltpu.make_async_copy(mat.at[at], held.at[at], sems.at[n]))
+        copies.append(
+            pltpu.make_async_copy(
+                mat.at[pl.ds(row0 + n * rows, rows)], held.at[pl.ds(n * rows, rows)], sems.at[n]
+            )
+        )
         copies[n].start()
+    return copies
+
+
+def spread_coupling(ints, both, mat, bx_hi, bx_lo, weight, held, bx, sems):
+    copies = fetches(mat, 0, held, sems)
     bx[...] = jnp.zeros_like(bx)
     bx[pl.ds(pl.multiple_of(place_of(ints)[0] * LANES, LANES), 24), :] = both[16:40, :]
     hi, lo = split(bx[...])
@@ -109,7 +126,7 @@
     weight[...] = jnp.ones_like(weight)
     for f in range(4):
         for c in range(4):
-            b = ints[f * 4 + c]
+            b = ints[0, f * 4 + c]
             at = block_at(b)
             weight[:, at] = jnp.where(b >= 0, jnp.full((8, BW), 0.5, F32), weight[:, at])
     for copy in copies:
@@ -128,14 +145,24 @@
     pay[...] = dot3(v, bx_hi[...], bx_lo[...], NT) + place(lane, place_of(ints)[0], NORM, norm) + maps
 
 
-def local_product(final, ints, v, mat, z, o0, o1, o2, o3, *rest):
+def local_product(final, ints, v, top, bottom, z, o0, o1, o2, o3, *rest):
     width = 256
+    depth = top.shape[0]
+    if not final:
+        held, sems = rest
+        copies = fetches(bottom, depth, held, sems)
     hi, lo = split(v[...])
     pieces = jnp.concatenate([hi, lo], axis=0)
-    for step in range(mat.shape[1] // width):
-        at = slice(step * width, (step + 1) * width)
-        both = dot(pieces, mat[:, at], NN)
-        z[:, at] = both[:16] + both[16:]
+    for part, mat in enumerate((top, bottom if final else held)):
+        if part == 1 and not final:
+            for copy in copies:
+                copy.wait()
+        rows = slice(0, depth) if part == 0 else slice(depth, v.shape[1])
+        for step in range(mat.shape[1] // width):
+            at = slice(step * width, (step + 1) * width)
+            both = dot(pieces[:, rows], mat[:, at], NN)
+            both = both[:16] + both[16:]
+            z[:, at] = both if part == 0 else z[:, at] + both
     for f, o in zip(faces_of(ints), (o0, o1, o2, o3)):
         pack_face(z, ints, f, o)
     if final:
@@ -156,7 +183,7 @@
     places = (rows(4), rows(5), rows(y + 1 - 2 * (y % 2)), rows(jnp.clip(beside, 0, 3)))
     for f, to, got in zip(faces_of(ints), places, (i0, i1, i2, i3)):
         for c in range(4):
-            b = ints[f * 4 + c]
+            b = ints[0, f * 4 + c]
             at = block_at(b)
             full[to, at] = jnp.where(b >= 0, -got[16:40, c * BW : (c + 1) * BW], full[to, at])
     hi, lo = split(full[...])
@@ -331,8 +358,16 @@
     zs, xs, cs, ys = (lax.axis_size(a) for a in ALL)
     subs = zs * xs * cs
     face = 4 * BW
+    ahead = dofs * 7 // 8
     here = jnp.stack([lax.axis_index("y"), lax.axis_index("c")]).astype(jnp.int32)
-    ints = jnp.concatenate([*(face_slots[0, f] for f in range(4)), corner_map[0], here])
+    wide = corner_map.shape[1]
+    table = jnp.concatenate(
+        [
+            jnp.pad(face_slots[0], ((0, 0), (0, wide - face_slots.shape[2]))),
+            corner_map,
+            jnp.pad(here[None], ((0, 0), (0, wide - 2))),
+        ]
+    )
     near_pairs = [(i, i ^ 1) for i in range(cs)]
     far_pairs = [(i, (i + 1) % subs) for i in range(1, subs, 2)]
     far_pairs = far_pairs + [(j, i) for i, j in far_pairs]
@@ -361,16 +396,17 @@
 
     def product(final, v):
         outs = [((cases, dofs), F32)] + [((cases, face), F32)] * 4
-        if final:
-            outs = outs + [((cases, BW), F32)]
+        outs = outs + [((cases, BW), F32) if final else ((dofs - ahead, dofs), BF16)]
         return call(
             functools.partial(local_product, final),
             "local_product",
-            (ints, v, matrix),
+            (ints, v, top, bottom if final else flexibility[0]),
             outs,
             1,
             2,
-            mib=6,
+            () if final else (pltpu.SemaphoreType.DMA((CHUNKS,)),),
+            mib=6 if final else FETCH,
+            outside=() if final else (3,),
         )
 
     def half(first, t, face_near, *held):
@@ -403,21 +439,23 @@
         )
         return scal, got, part, one(out_one), across(part), two(out_two)
 
-    o0, o1, o2, o3, own_map = call(
+    o0, o1, o2, o3, own_map, ints = call(
         first_pack,
         "first_pack",
-        (ints, both),
-        [((48, face), F32)] * 2 + [((40, face), F32)] * 2 + [((8, BW), F32)],
+        (table, both),
+        [((48, face), F32)] * 2
+        + [((40, face), F32)] * 2
+        + [((8, BW), F32), ((1, BW), jnp.int32)],
         1,
         1,
     )
     far_came = far(o1)
     came = (near(o0), far_came, one(o2), two(o3))
-    bx_hi, bx_lo, weight, matrix = call(
+    bx_hi, bx_lo, weight, top = call(
         spread_coupling,
         "spread_coupling",
         (ints, both, flexibility[0]),
-        [((BW, dofs), BF16)] * 2 + [((8, dofs), F32), ((dofs, dofs), BF16)],
+        [((BW, dofs), BF16)] * 2 + [((8, dofs), F32), ((ahead, dofs), BF16)],
         1,
         3,
         [((BW, dofs), F32), pltpu.SemaphoreType.DMA((CHUNKS,))],
@@ -432,8 +470,8 @@
         1,
         1,
     )
-    rows = (across(pay), one(pay), two(pay))
-    *rows, z0, n0, f0, a0, b0 = lax.optimization_barrier((*rows, *product(False, v0)))
+    rows = (two(pay), one(pay), across(pay))
+    *rows, z0, n0, f0, a0, b0, bottom = lax.optimization_barrier((*rows, *product(False, v0)))
     faces = (n0, f0, a0, b0)
     row = (pay + rows[0]) + (rows[1] + rows[2])
     terms0, face_far = lax.optimization_barrier((gather(row), faces[1]))
@@ -469,7 +507,7 @@
         1.6,
         mib=12,
     )
-    rows = (across(pay), one(pay), two(pay))
+    rows = (two(pay), one(pay), across(pay))
     *rows, z1, n1, f1, a1, b1, local_dot = lax.optimization_barrier((*rows, *product(True, v1)))
     faces = (n1, f1, a1, b1)
     row = (pay + rows[0]) + (rows[1] + rows[2]) + local_dot

time: 103 us -> 101 us (0.981)
  local copies, waits for them, and re-layouts: 1.62 us -> 0.05 us
  blocking collectives: 37.5 us -> 36.3 us
  starting transfers between devices: 26.7 us -> 25.6 us
    ppermute x5, waiting for transfers between devices: 0.01 us -> 2.54 us  [two(): return lax.ppermute(p, 'y', two_pairs)]
    ppermute x3, waiting for transfers between devices: 4.6 us -> 2.75 us  [far(): return lax.ppermute(p, SUB, far_pairs)]
    all_to_all x2, blocking collectives: 37.5 us -> 36.3 us  [gather(): return lax.all_to_all(every, ('z', 'x'), 0, 0)]
where the time goes in v4:
time: 101 us; the launch traced here: 100 us
  blocking collectives  36.3 us (36%)
  Pallas kernels  26.5 us (26%)
  starting transfers between devices  25.6 us (25%)
  waiting for transfers between devices  9.01 us (9%)
  other arithmetic  1.81 us (2%)
    all_to_all x2, blocking collectives, gather(): return lax.all_to_all(every, ('z', 'x'), 0, 0)  36.3 us
    pallas_call x13, Pallas kernels, call(): pl.pallas_call(kernel, out_shape=[jax.ShapeDtypeStruct(s, d) for s, d in...  26.5 us
    ppermute x4, starting transfers between devices, across(): return lax.ppermute(p, 'y', across_pairs)  8.03 us
    ppermute x5, starting transfers between devices, two(): return lax.ppermute(p, 'y', two_pairs)  7.86 us
    ppermute x3, starting transfers between devices, far(): return lax.ppermute(p, SUB, far_pairs)  5.12 us
    ppermute x5, starting transfers between devices, one(): return lax.ppermute(p, 'y', one_pairs)  4.34 us
    ppermute x3, waiting for transfers between devices, far(): return lax.ppermute(p, SUB, far_pairs)  2.75 us
    ppermute x5, waiting for transfers between devices, two(): return lax.ppermute(p, 'y', two_pairs)  2.54 us
  transfers between devices with their start and end apart: 20, of which 6 were waited for; matrix products, arithmetic and copies ran while one was open for 0% of the time, Pallas kernels for 12%

profile of v4, /device:TPU:32, one launch (start us, length us, event | category | flops | bytes accessed | tf_op | source)
XLA Modules:
  0.0 100.1 jit_solution(16677998973055470519)
XLA Ops:
  0.7 1.0 %pad_maximum_fusion.both = f32[40,2048]{1,0:T(8,128)S(1)} fusion(f32[24,2048]{1,0:T(8,128)} %bitcast.12, f32[16,2048]{1,0:T(8,128)} %bitcast.13), kind=kLoop, calls=%fused_computation | loop fusion | flops 81920 | bytes 655360 | tf_op jit(solution)/shard_map/concatenate | solution.py:355
  3.2 2.4 %collective-permute-start.1 = (f32[48,512]{1,0:T(8,128)S(1)}, f32[48,512]{1,0:T(8,128)S(1)}, u32[]{:S(2)}, u32[]{:S(2)}) collective-permute-start(f32[48,512]{1,0:T(8,128)S(1)} %get-tuple-element.71), channel_id=1, source_target_pairs={{4,8},{12,16},{20,24},{28,32},{36,40},{44,48},{52,56},{60,64},{68,... | collective-permute-start | bytes 294920 | tf_op jit(solution)/shard_map/ppermute | solution.py:382
  5.6 1.6 %collective-permute-start.2 = (f32[40,512]{1,0:T(8,128)S(1)}, f32[40,512]{1,0:T(8,128)S(1)}, u32[]{:S(2)}, u32[]{:S(2)}) collective-permute-start(f32[40,512]{1,0:T(8,128)S(1)} %get-tuple-element.72), channel_id=1, source_target_pairs={{0,1},{1,0},{2,3},{3,2},{4,5},{5,4},{6,7},{7,6},{8,9},{9,8},{10,11... | collective-permute-start | bytes 245768 | tf_op jit(solution)/shard_map/ppermute | solution.py:385
  7.2 2.2 %collective-permute-start.3 = (f32[40,512]{1,0:T(8,128)S(1)}, f32[40,512]{1,0:T(8,128)S(1)}, u32[]{:S(2)}, u32[]{:S(2)}) collective-permute-start(f32[40,512]{1,0:T(8,128)S(1)} %get-tuple-element.73), channel_id=1, source_target_pairs={{0,3},{1,2},{2,1},{3,0},{4,7},{5,6},{6,5},{7,4},{8,11},{9,10},{10,... | collective-permute-start | bytes 245768 | tf_op jit(solution)/shard_map/ppermute | solution.py:391
  9.4 3.7 %spread_coupling.1 = (bf16[128,2048]{1,0:T(8,128)(2,1)S(1)}, bf16[128,2048]{1,0:T(8,128)(2,1)S(1)}, f32[8,2048]{1,0:T(8,128)S(1)}, bf16[1792,2048]{1,0:T(8,128)(2,1)S(1)}) custom-call(s32[1,128]{1,0:T(1,128)S(1)} %get-tuple-element.69.ints, f32[40,2048]{1,0:T(8,128)S(1)} %pad_maximum_fusion.both, bf16[2048,2048]{1,0:T(8,128)(2,1)} %bitcast.10), custom_call_target="tpu_custom_call" | custom-call | flops 3000000 | bytes 10500000 | tf_op jit(solution)/shard_map/spread_coupling/pallas_call | solution.py:340
  13.1 1.0 %first_vector.1 = (f32[16,2048]{1,0:T(8,128)S(1)}, f32[16,128]{1,0:T(8,128)S(1)}) custom-call(s32[1,128]{1,0:T(1,128)S(1)} %get-tuple-element.69.ints, f32[40,2048]{1,0:T(8,128)S(1)} %pad_maximum_fusion.both, f32[48,512]{1,0:T(8,128)S(1)} %collective-permute-done.i0, f32[48,512]{1,0:T(8,128)S(1)} %collective-permute-done.1.i1, ...), custom_call_target="tpu_custom_call" | custom-call | flops 1000000 | bytes 3500000 | tf_op jit(solution)/shard_map/first_vector/pallas_call | solution.py:340
  14.2 1.5 %collective-permute-start.6 = (f32[16,128]{1,0:T(8,128)S(1)}, f32[16,128]{1,0:T(8,128)S(1)}, u32[]{:S(2)}, u32[]{:S(2)}) collective-permute-start(f32[16,128]{1,0:T(8,128)S(1)} %get-tuple-element.78), channel_id=1, source_target_pairs={{0,2},{1,3},{2,0},{3,1},{4,6},{5,7},{6,4},{7,5},{8,10},{9,11},{10,... | collective-permute-start | bytes 24584 | tf_op jit(solution)/shard_map/ppermute | solution.py:388
  15.6 1.4 %collective-permute-start.5 = (f32[16,128]{1,0:T(8,128)S(1)}, f32[16,128]{1,0:T(8,128)S(1)}, u32[]{:S(2)}, u32[]{:S(2)}) collective-permute-start(f32[16,128]{1,0:T(8,128)S(1)} %get-tuple-element.78), channel_id=1, source_target_pairs={{0,1},{1,0},{2,3},{3,2},{4,5},{5,4},{6,7},{7,6},{8,9},{9,8},{10,11... | collective-permute-start | bytes 24584 | tf_op jit(solution)/shard_map/ppermute | solution.py:385
  17.0 1.3 %collective-permute-start.4 = (f32[16,128]{1,0:T(8,128)S(1)}, f32[16,128]{1,0:T(8,128)S(1)}, u32[]{:S(2)}, u32[]{:S(2)}) collective-permute-start(f32[16,128]{1,0:T(8,128)S(1)} %get-tuple-element.78), channel_id=1, source_target_pairs={{0,3},{1,2},{2,1},{3,0},{4,7},{5,6},{6,5},{7,4},{8,11},{9,10},{10,... | collective-permute-start | bytes 24584 | tf_op jit(solution)/shard_map/ppermute | solution.py:391
  18.3 2.5 %local_product.2 = (f32[16,2048]{1,0:T(8,128)S(1)}, f32[16,512]{1,0:T(8,128)S(1)}, f32[16,512]{1,0:T(8,128)S(1)}, f32[16,512]{1,0:T(8,128)S(1)}, f32[16,512]{1,0:T(8,128)S(1)}, /*index=5*/bf16[256,2048]{1,0:T(8,128)(2,1)S(1)}) custom-call(s32[1,128]{1,0:T(1,128)S(1)} %get-tuple-element.69.ints, f32[16,2048]{1,0:T(8,128)S(1)} %get-tuple-element.79.v.v0, ...), custom_call_target="tpu_custom_call" | custom-call | flops 2000000 | bytes 7000000 | tf_op jit(solution)/shard_map/local_product/pallas_call | solution.py:340
  20.8 1.0 %collective-permute-done.4 = f32[16,128]{1,0:T(8,128)S(1)} collective-permute-done((f32[16,128]{1,0:T(8,128)S(1)}, f32[16,128]{1,0:T(8,128)S(1)}, u32[]{:S(2)}, u32[]{:S(2)}) %collective-permute-start.4) | collective-permute-done | bytes 8224 | tf_op jit(solution)/shard_map/ppermute | solution.py:391
  21.9 20.4 %all_to_all.10.t = f32[32,16,128]{2,1,0:T(8,128)S(1)} all-to-all(f32[32,16,128]{2,1,0:T(8,128)S(1)} %broadcast_in_dim.22), channel_id=1, replica_groups=mesh['z'=8,'x'=4,'c'=2,'y'=4] {'z','x'}, dimensions={0} | all-to-all | bytes 524288 | tf_op jit(solution)/shard_map/all_to_all | solution.py:395
  42.3 4.4 %coarse_half.2 = (f32[16,1152]{1,0:T(8,128)S(1)}, bf16[512,2048]{1,0:T(8,128)(2,1)S(1)}, bf16[512,2048]{1,0:T(8,128)(2,1)S(1)}, f32[32,128]{1,0:T(8,128)S(1)}, bf16[4096,256]{1,0:T(8,128)(2,1)S(1)}) custom-call(f32[32,16,128]{2,1,0:T(8,128)S(1)} %all_to_all.10.t, f32[16,512]{1,0:T(8,128)S(1)} %get-tuple-element.93.near, f32[512,2048]{1,0:T(8,128)S(1)} %copy-done), custom_call_target="tpu_custom_call" | custom-call | flops 4000000 | bytes 14000000 | tf_op jit(solution)/shard_map/coarse_half/pallas_call | solution.py:340
  46.7 2.5 %picked_columns.1 = (bf16[512,384]{1,0:T(8,128)(2,1)S(1)}, bf16[512,384]{1,0:T(8,128)(2,1)S(1)}) custom-call(f32[16,128]{1,0:T(8,128)S(1)} %add_add_fusion.1.pay, bf16[512,2048]{1,0:T(8,128)(2,1)S(1)} %get-tuple-element.98.f_hi.rest_0_, bf16[512,2048]{1,0:T(8,128)(2,1)S(1)} %get-tuple-element.99.f_lo.rest_1_), custom_call_target="tpu_custom_call" | custom-call | flops 2500000 | bytes 8750000 | tf_op jit(solution)/shard_map/picked_columns/pallas_call | solution.py:340
  50.3 1.2 %collective-permute-start.11 = (f32[16,896]{1,0:T(8,128)S(1)}, f32[16,896]{1,0:T(8,128)S(1)}, u32[]{:S(2)}, u32[]{:S(2)}) collective-permute-start(f32[16,896]{1,0:T(8,128)S(1)} %get-tuple-element.104), channel_id=1, source_target_pairs={{0,3},{1,2},{2,1},{3,0},{4,7},{5,6},{6,5},{7,4},{8,11},{9,10},{10,... | collective-permute-start | bytes 172040 | tf_op jit(solution)/shard_map/ppermute | solution.py:391
  51.6 1.7 %collective-permute-start.8 = (f32[16,512]{1,0:T(8,128)S(1)}, f32[16,512]{1,0:T(8,128)S(1)}, u32[]{:S(2)}, u32[]{:S(2)}) collective-permute-start(f32[16,512]{1,0:T(8,128)S(1)} %get-tuple-element.95), channel_id=1, source_target_pairs={{4,8},{12,16},{20,24},{28,32},{36,40},{44,48},{52,56},{60,64},{68,... | collective-permute-start | bytes 98312 | tf_op jit(solution)/shard_map/ppermute | solution.py:382
  53.3 2.4 %collective-permute-start.10 = (f32[16,384]{1,0:T(8,128)S(1)}, f32[16,384]{1,0:T(8,128)S(1)}, u32[]{:S(2)}, u32[]{:S(2)}) collective-permute-start(f32[16,384]{1,0:T(8,128)S(1)} %get-tuple-element.102.p0), channel_id=1, source_target_pairs={{0,2},{1,3},{2,0},{3,1},{4,6},{5,7},{6,4},{7,5},{8,10},{9,11},{10,... | collective-permute-start | bytes 73736 | tf_op jit(solution)/shard_map/ppermute | solution.py:388
  55.7 1.3 %jumped_coupling.1 = (bf16[256,2048]{1,0:T(8,128)(2,1)S(1)}, bf16[256,2048]{1,0:T(8,128)(2,1)S(1)}) custom-call(s32[1,128]{1,0:T(1,128)S(1)} %get-tuple-element.69.ints, f32[40,2048]{1,0:T(8,128)S(1)} %pad_maximum_fusion.both, f32[48,512]{1,0:T(8,128)S(1)} %collective-permute-done.i0, f32[48,512]{1,0:T(8,128)S(1)} %collective-permute-done.1.i1, ...), custom_call_target="tpu_custom_call" | custom-call | flops 1200000 | bytes 4200000 | tf_op jit(solution)/shard_map/jumped_coupling/pallas_call | solution.py:340
  57.1 1.6 %collective-permute-done.10.p2 = f32[16,384]{1,0:T(8,128)S(1)} collective-permute-done((f32[16,384]{1,0:T(8,128)S(1)}, f32[16,384]{1,0:T(8,128)S(1)}, u32[]{:S(2)}, u32[]{:S(2)}) %collective-permute-start.10) | collective-permute-done | bytes 24608 | tf_op jit(solution)/shard_map/ppermute | solution.py:388
  58.6 1.5 %next_vector.1 = (f32[16,2048]{1,0:T(8,128)S(1)}, f32[16,128]{1,0:T(8,128)S(1)}) custom-call(s32[1,128]{1,0:T(1,128)S(1)} %get-tuple-element.69.ints, f32[16,2048]{1,0:T(8,128)S(1)} %get-tuple-element.87.z0, f32[16,1152]{1,0:T(8,128)S(1)} %collective-permute-done.7.got, f32[16,512]{1,0:T(8,128)S(1)} %collective-permute-done.8.far, ...), custom_call_target="tpu_custom_call" | custom-call | flops 1600000 | bytes 5600000 | tf_op jit(solution)/shard_map/next_vector/pallas_call | solution.py:340
  60.1 2.5 %collective-permute-start.14 = (f32[16,128]{1,0:T(8,128)S(1)}, f32[16,128]{1,0:T(8,128)S(1)}, u32[]{:S(2)}, u32[]{:S(2)}) collective-permute-start(f32[16,128]{1,0:T(8,128)S(1)} %get-tuple-element.107), channel_id=1, source_target_pairs={{0,2},{1,3},{2,0},{3,1},{4,6},{5,7},{6,4},{7,5},{8,10},{9,11},{10,... | collective-permute-start | bytes 24584 | tf_op jit(solution)/shard_map/ppermute | solution.py:388
  63.0 1.3 %collective-permute-start.12 = (f32[16,128]{1,0:T(8,128)S(1)}, f32[16,128]{1,0:T(8,128)S(1)}, u32[]{:S(2)}, u32[]{:S(2)}) collective-permute-start(f32[16,128]{1,0:T(8,128)S(1)} %get-tuple-element.107), channel_id=1, source_target_pairs={{0,3},{1,2},{2,1},{3,0},{4,7},{5,6},{6,5},{7,4},{8,11},{9,10},{10,... | collective-permute-start | bytes 24584 | tf_op jit(solution)/shard_map/ppermute | solution.py:391
  64.3 2.1 %local_product.3 = (f32[16,2048]{1,0:T(8,128)S(1)}, f32[16,512]{1,0:T(8,128)S(1)}, f32[16,512]{1,0:T(8,128)S(1)}, f32[16,512]{1,0:T(8,128)S(1)}, f32[16,512]{1,0:T(8,128)S(1)}, /*index=5*/f32[16,128]{1,0:T(8,128)S(1)}) custom-call(s32[1,128]{1,0:T(1,128)S(1)} %get-tuple-element.69.ints, f32[16,2048]{1,0:T(8,128)S(1)} %get-tuple-element.108.v.v1, ...), custom_call_target="tpu_custom_call" | custom-call | flops 2000000 | bytes 7000000 | tf_op jit(solution)/shard_map/local_product/pallas_call | solution.py:340
  66.4 1.5 %collective-permute-done.12 = f32[16,128]{1,0:T(8,128)S(1)} collective-permute-done((f32[16,128]{1,0:T(8,128)S(1)}, f32[16,128]{1,0:T(8,128)S(1)}, u32[]{:S(2)}, u32[]{:S(2)}) %collective-permute-start.12) | collective-permute-done | bytes 8224 | tf_op jit(solution)/shard_map/ppermute | solution.py:391
  67.9 15.9 %all_to_all.11.t = f32[32,16,128]{2,1,0:T(8,128)S(1)} all-to-all(f32[32,16,128]{2,1,0:T(8,128)S(1)} %broadcast_in_dim.23), channel_id=1, replica_groups=mesh['z'=8,'x'=4,'c'=2,'y'=4] {'z','x'}, dimensions={0} | all-to-all | bytes 524288 | tf_op jit(solution)/shard_map/all_to_all | solution.py:395
  83.8 3.6 %coarse_half.3.own = f32[16,1152]{1,0:T(8,128)S(1)} custom-call(f32[32,16,128]{2,1,0:T(8,128)S(1)} %all_to_all.11.t, f32[16,512]{1,0:T(8,128)S(1)} %get-tuple-element.123.near, bf16[512,2048]{1,0:T(8,128)(2,1)S(1)} %get-tuple-element.98.f_hi.rest_0_, bf16[512,2048]{1,0:T(8,128)(2,1)S(1)} %get-tuple-element.99.f_lo.rest_1_, ...), custom_call_target="tpu_custom_call" | custom-call | flops 4000000 | bytes 14000000 | tf_op jit(solution)/shard_map/coarse_half/pallas_call | solution.py:340
  87.4 1.3 %collective-permute-done.15.got = f32[16,1152]{1,0:T(8,128)S(1)} collective-permute-done((f32[16,1152]{1,0:T(8,128)S(1)}, f32[16,1152]{1,0:T(8,128)S(1)}, u32[]{:S(2)}, u32[]{:S(2)}) %collective-permute-start.15) | collective-permute-done | bytes 73760 | tf_op jit(solution)/shard_map/ppermute | solution.py:379
  90.1 1.8 %collective-permute-start.19 = (f32[16,896]{1,0:T(8,128)S(1)}, f32[16,896]{1,0:T(8,128)S(1)}, u32[]{:S(2)}, u32[]{:S(2)}) collective-permute-start(f32[16,896]{1,0:T(8,128)S(1)} %get-tuple-element.131), channel_id=1, source_target_pairs={{0,3},{1,2},{2,1},{3,0},{4,7},{5,6},{6,5},{7,4},{8,11},{9,10},{10,... | collective-permute-start | bytes 172040 | tf_op jit(solution)/shard_map/ppermute | solution.py:391
  91.9 1.0 %collective-permute-start.16 = (f32[16,512]{1,0:T(8,128)S(1)}, f32[16,512]{1,0:T(8,128)S(1)}, u32[]{:S(2)}, u32[]{:S(2)}) collective-permute-start(f32[16,512]{1,0:T(8,128)S(1)} %get-tuple-element.126), channel_id=1, source_target_pairs={{4,8},{12,16},{20,24},{28,32},{36,40},{44,48},{52,56},{60,64},{68,... | collective-permute-start | bytes 98312 | tf_op jit(solution)/shard_map/ppermute | solution.py:382
  92.9 1.7 %collective-permute-start.18 = (f32[16,384]{1,0:T(8,128)S(1)}, f32[16,384]{1,0:T(8,128)S(1)}, u32[]{:S(2)}, u32[]{:S(2)}) collective-permute-start(f32[16,384]{1,0:T(8,128)S(1)} %get-tuple-element.129.p0), channel_id=1, source_target_pairs={{0,2},{1,3},{2,0},{3,1},{4,6},{5,7},{6,4},{7,5},{8,10},{9,11},{10,... | collective-permute-start | bytes 73736 | tf_op jit(solution)/shard_map/ppermute | solution.py:388
  94.6 2.7 %collective-permute-done.16.far = f32[16,512]{1,0:T(8,128)S(1)} collective-permute-done((f32[16,512]{1,0:T(8,128)S(1)}, f32[16,512]{1,0:T(8,128)S(1)}, u32[]{:S(2)}, u32[]{:S(2)}) %collective-permute-start.16) | collective-permute-done | bytes 32800 | tf_op jit(solution)/shard_map/ppermute | solution.py:382
  98.3 1.8 %finish.1 = (f32[16,2048]{1,0:T(8,128)}, f32[16,2048]{1,0:T(8,128)}) custom-call(s32[1,128]{1,0:T(1,128)S(1)} %get-tuple-element.69.ints, f32[16,2048]{1,0:T(8,128)S(1)} %get-tuple-element.116.z1, f32[16,1152]{1,0:T(8,128)S(1)} %collective-permute-done.15.got, f32[16,512]{1,0:T(8,128)S(1)} %collective-permute-done.16.far, ...), custom_call_target="tpu_custom_call" | custom-call | flops 1900000 | bytes 6650000 | tf_op jit(solution)/shard_map/finish/pallas_call | solution.py:340
  (32 shorter events, 5.6 us)
Async XLA Ops:
  3.1 10.0 %collective-permute-start = (f32[48,512]{1,0:T(8,128)S(1)}, f32[48,512]{1,0:T(8,128)S(1)}, u32[]{:S(2)}, u32[]{:S(2)}) collective-permute-start(f32[48,512]{1,0:T(8,128)S(1)} %get-tuple-element.70), channel_id=1, source_target_pairs={{0,4},{4,0},{1,5},{5,1},{2,6},{6,2},{3,7},{7,3},{8,12},{12,8},{9,1... | collective-permute-start | bytes 294920 | tf_op jit(solution)/shard_map/ppermute | solution.py:379
  3.2 9.9 %collective-permute-start.1 = (f32[48,512]{1,0:T(8,128)S(1)}, f32[48,512]{1,0:T(8,128)S(1)}, u32[]{:S(2)}, u32[]{:S(2)}) collective-permute-start(f32[48,512]{1,0:T(8,128)S(1)} %get-tuple-element.71), channel_id=1, source_target_pairs={{4,8},{12,16},{20,24},{28,32},{36,40},{44,48},{52,56},{60,64},{68,... | collective-permute-start | bytes 294920 | tf_op jit(solution)/shard_map/ppermute | solution.py:382
  5.6 7.5 %collective-permute-start.2 = (f32[40,512]{1,0:T(8,128)S(1)}, f32[40,512]{1,0:T(8,128)S(1)}, u32[]{:S(2)}, u32[]{:S(2)}) collective-permute-start(f32[40,512]{1,0:T(8,128)S(1)} %get-tuple-element.72), channel_id=1, source_target_pairs={{0,1},{1,0},{2,3},{3,2},{4,5},{5,4},{6,7},{7,6},{8,9},{9,8},{10,11... | collective-permute-start | bytes 245768 | tf_op jit(solution)/shard_map/ppermute | solution.py:385
  7.2 5.9 %collective-permute-start.3 = (f32[40,512]{1,0:T(8,128)S(1)}, f32[40,512]{1,0:T(8,128)S(1)}, u32[]{:S(2)}, u32[]{:S(2)}) collective-permute-start(f32[40,512]{1,0:T(8,128)S(1)} %get-tuple-element.73), channel_id=1, source_target_pairs={{0,3},{1,2},{2,1},{3,0},{4,7},{5,6},{6,5},{7,4},{8,11},{9,10},{10,... | collective-permute-start | bytes 245768 | tf_op jit(solution)/shard_map/ppermute | solution.py:391
  14.2 6.6 %collective-permute-start.6 = (f32[16,128]{1,0:T(8,128)S(1)}, f32[16,128]{1,0:T(8,128)S(1)}, u32[]{:S(2)}, u32[]{:S(2)}) collective-permute-start(f32[16,128]{1,0:T(8,128)S(1)} %get-tuple-element.78), channel_id=1, source_target_pairs={{0,2},{1,3},{2,0},{3,1},{4,6},{5,7},{6,4},{7,5},{8,10},{9,11},{10,... | collective-permute-start | bytes 24584 | tf_op jit(solution)/shard_map/ppermute | solution.py:388
  15.6 5.2 %collective-permute-start.5 = (f32[16,128]{1,0:T(8,128)S(1)}, f32[16,128]{1,0:T(8,128)S(1)}, u32[]{:S(2)}, u32[]{:S(2)}) collective-permute-start(f32[16,128]{1,0:T(8,128)S(1)} %get-tuple-element.78), channel_id=1, source_target_pairs={{0,1},{1,0},{2,3},{3,2},{4,5},{5,4},{6,7},{7,6},{8,9},{9,8},{10,11... | collective-permute-start | bytes 24584 | tf_op jit(solution)/shard_map/ppermute | solution.py:385
  17.0 4.9 %collective-permute-start.4 = (f32[16,128]{1,0:T(8,128)S(1)}, f32[16,128]{1,0:T(8,128)S(1)}, u32[]{:S(2)}, u32[]{:S(2)}) collective-permute-start(f32[16,128]{1,0:T(8,128)S(1)} %get-tuple-element.78), channel_id=1, source_target_pairs={{0,3},{1,2},{2,1},{3,0},{4,7},{5,6},{6,5},{7,4},{8,11},{9,10},{10,... | collective-permute-start | bytes 24584 | tf_op jit(solution)/shard_map/ppermute | solution.py:391
  18.3 24.0 %copy-start = (f32[512,2048]{1,0:T(8,128)S(1)}, f32[512,2048]{1,0:T(8,128)}, u32[]{:S(2)}) copy-start(f32[512,2048]{1,0:T(8,128)} %rest_0_.1) | copy-start | bytes 12582916
  46.7 2.6 %collective-permute-start.7 = (f32[16,1152]{1,0:T(8,128)S(1)}, f32[16,1152]{1,0:T(8,128)S(1)}, u32[]{:S(2)}, u32[]{:S(2)}) collective-permute-start(f32[16,1152]{1,0:T(8,128)S(1)} %get-tuple-element.94.own), channel_id=1, source_target_pairs={{0,4},{4,0},{1,5},{5,1},{2,6},{6,2},{3,7},{7,3},{8,12},{12,8},{9,1... | collective-permute-start | bytes 221192 | tf_op jit(solution)/shard_map/ppermute | solution.py:379
  50.0 8.6 %collective-permute-start.9 = (f32[16,896]{1,0:T(8,128)S(1)}, f32[16,896]{1,0:T(8,128)S(1)}, u32[]{:S(2)}, u32[]{:S(2)}) collective-permute-start(f32[16,896]{1,0:T(8,128)S(1)} %get-tuple-element.103), channel_id=1, source_target_pairs={{0,1},{1,0},{2,3},{3,2},{4,5},{5,4},{6,7},{7,6},{8,9},{9,8},{10,11... | collective-permute-start | bytes 172040 | tf_op jit(solution)/shard_map/ppermute | solution.py:385
  50.3 8.3 %collective-permute-start.11 = (f32[16,896]{1,0:T(8,128)S(1)}, f32[16,896]{1,0:T(8,128)S(1)}, u32[]{:S(2)}, u32[]{:S(2)}) collective-permute-start(f32[16,896]{1,0:T(8,128)S(1)} %get-tuple-element.104), channel_id=1, source_target_pairs={{0,3},{1,2},{2,1},{3,0},{4,7},{5,6},{6,5},{7,4},{8,11},{9,10},{10,... | collective-permute-start | bytes 172040 | tf_op jit(solution)/shard_map/ppermute | solution.py:391
  51.6 5.5 %collective-permute-start.8 = (f32[16,512]{1,0:T(8,128)S(1)}, f32[16,512]{1,0:T(8,128)S(1)}, u32[]{:S(2)}, u32[]{:S(2)}) collective-permute-start(f32[16,512]{1,0:T(8,128)S(1)} %get-tuple-element.95), channel_id=1, source_target_pairs={{4,8},{12,16},{20,24},{28,32},{36,40},{44,48},{52,56},{60,64},{68,... | collective-permute-start | bytes 98312 | tf_op jit(solution)/shard_map/ppermute | solution.py:382
  53.3 5.3 %collective-permute-start.10 = (f32[16,384]{1,0:T(8,128)S(1)}, f32[16,384]{1,0:T(8,128)S(1)}, u32[]{:S(2)}, u32[]{:S(2)}) collective-permute-start(f32[16,384]{1,0:T(8,128)S(1)} %get-tuple-element.102.p0), channel_id=1, source_target_pairs={{0,2},{1,3},{2,0},{3,1},{4,6},{5,7},{6,4},{7,5},{8,10},{9,11},{10,... | collective-permute-start | bytes 73736 | tf_op jit(solution)/shard_map/ppermute | solution.py:388
  60.1 6.2 %collective-permute-start.14 = (f32[16,128]{1,0:T(8,128)S(1)}, f32[16,128]{1,0:T(8,128)S(1)}, u32[]{:S(2)}, u32[]{:S(2)}) collective-permute-start(f32[16,128]{1,0:T(8,128)S(1)} %get-tuple-element.107), channel_id=1, source_target_pairs={{0,2},{1,3},{2,0},{3,1},{4,6},{5,7},{6,4},{7,5},{8,10},{9,11},{10,... | collective-permute-start | bytes 24584 | tf_op jit(solution)/shard_map/ppermute | solution.py:388
  62.6 3.8 %collective-permute-start.13 = (f32[16,128]{1,0:T(8,128)S(1)}, f32[16,128]{1,0:T(8,128)S(1)}, u32[]{:S(2)}, u32[]{:S(2)}) collective-permute-start(f32[16,128]{1,0:T(8,128)S(1)} %get-tuple-element.107), channel_id=1, source_target_pairs={{0,1},{1,0},{2,3},{3,2},{4,5},{5,4},{6,7},{7,6},{8,9},{9,8},{10,11... | collective-permute-start | bytes 24584 | tf_op jit(solution)/shard_map/ppermute | solution.py:385
  63.0 4.9 %collective-permute-start.12 = (f32[16,128]{1,0:T(8,128)S(1)}, f32[16,128]{1,0:T(8,128)S(1)}, u32[]{:S(2)}, u32[]{:S(2)}) collective-permute-start(f32[16,128]{1,0:T(8,128)S(1)} %get-tuple-element.107), channel_id=1, source_target_pairs={{0,3},{1,2},{2,1},{3,0},{4,7},{5,6},{6,5},{7,4},{8,11},{9,10},{10,... | collective-permute-start | bytes 24584 | tf_op jit(solution)/shard_map/ppermute | solution.py:391
  87.4 1.3 %collective-permute-start.15 = (f32[16,1152]{1,0:T(8,128)S(1)}, f32[16,1152]{1,0:T(8,128)S(1)}, u32[]{:S(2)}, u32[]{:S(2)}) collective-permute-start(f32[16,1152]{1,0:T(8,128)S(1)} %coarse_half.3.own), channel_id=1, source_target_pairs={{0,4},{4,0},{1,5},{5,1},{2,6},{6,2},{3,7},{7,3},{8,12},{12,8},{9,1... | collective-permute-start | bytes 221192 | tf_op jit(solution)/shard_map/ppermute | solution.py:379
  89.5 8.8 %collective-permute-start.17 = (f32[16,896]{1,0:T(8,128)S(1)}, f32[16,896]{1,0:T(8,128)S(1)}, u32[]{:S(2)}, u32[]{:S(2)}) collective-permute-start(f32[16,896]{1,0:T(8,128)S(1)} %get-tuple-element.130), channel_id=1, source_target_pairs={{0,1},{1,0},{2,3},{3,2},{4,5},{5,4},{6,7},{7,6},{8,9},{9,8},{10,11... | collective-permute-start | bytes 172040 | tf_op jit(solution)/shard_map/ppermute | solution.py:385
  90.1 8.2 %collective-permute-start.19 = (f32[16,896]{1,0:T(8,128)S(1)}, f32[16,896]{1,0:T(8,128)S(1)}, u32[]{:S(2)}, u32[]{:S(2)}) collective-permute-start(f32[16,896]{1,0:T(8,128)S(1)} %get-tuple-element.131), channel_id=1, source_target_pairs={{0,3},{1,2},{2,1},{3,0},{4,7},{5,6},{6,5},{7,4},{8,11},{9,10},{10,... | collective-permute-start | bytes 172040 | tf_op jit(solution)/shard_map/ppermute | solution.py:391
  91.9 5.4 %collective-permute-start.16 = (f32[16,512]{1,0:T(8,128)S(1)}, f32[16,512]{1,0:T(8,128)S(1)}, u32[]{:S(2)}, u32[]{:S(2)}) collective-permute-start(f32[16,512]{1,0:T(8,128)S(1)} %get-tuple-element.126), channel_id=1, source_target_pairs={{4,8},{12,16},{20,24},{28,32},{36,40},{44,48},{52,56},{60,64},{68,... | collective-permute-start | bytes 98312 | tf_op jit(solution)/shard_map/ppermute | solution.py:382
  92.9 5.3 %collective-permute-start.18 = (f32[16,384]{1,0:T(8,128)S(1)}, f32[16,384]{1,0:T(8,128)S(1)}, u32[]{:S(2)}, u32[]{:S(2)}) collective-permute-start(f32[16,384]{1,0:T(8,128)S(1)} %get-tuple-element.129.p0), channel_id=1, source_target_pairs={{0,2},{1,3},{2,0},{3,1},{4,6},{5,7},{6,4},{7,5},{8,10},{9,11},{10,... | collective-permute-start | bytes 73736 | tf_op jit(solution)/shard_map/ppermute | solution.py:388

commit v5 on v4

--- a/solution.py
+++ b/solution.py
@@ -237,18 +237,17 @@
                 )
     none = jnp.zeros((16, BW), BF16)
 
-    def body(j, acc):
+    total = jnp.zeros((16, BW), F32)
+    for j in range(groups):
         terms = t[j]
-        digit = jnp.broadcast_to(top[pl.ds(j, 1), :], (16, BW)).astype(BF16)
+        digit = jnp.broadcast_to(top[j : j + 1, :], (16, BW)).astype(BF16)
         hi, lo = split(terms)
-        at = pl.ds(pl.multiple_of(j * BW, BW), BW)
+        at = slice(j * BW, (j + 1) * BW)
         for d in range(digits):
             mine = digit == jnp.full((16, BW), d, BF16)
             terms_at[d * 16 : d * 16 + 16, at] = jnp.where(mine, hi, none)
             terms_at[half + d * 16 : half + d * 16 + 16, at] = jnp.where(mine, lo, none)
-        return acc + terms
-
-    total = lax.fori_loop(0, groups, body, jnp.zeros((16, BW), F32), unroll=4)
+        total = total + terms
     sums = dot(terms_at[...], hot[...], NN)
     sums = sums[:half] + sums[half:]
     rhs = jnp.concatenate([sums[d * 16 : d * 16 + 16, :] for d in range(digits)], axis=1)

time: 101 us -> 99.1 us (0.981)
  Pallas kernels: 26.5 us -> 25.1 us
    pallas_call x13, Pallas kernels: 26.5 us -> 25.1 us  [call(): pl.pallas_call(kernel, out_shape=[jax.ShapeDtypeStruct(s, d) for s, d in...]
where the time goes in v5:
time: 99.1 us; the launch traced here: 98.5 us
  blocking collectives  36.2 us (37%)
  starting transfers between devices  25.8 us (26%)
  Pallas kernels  25.1 us (25%)
  waiting for transfers between devices  8.86 us (9%)
  other arithmetic  1.81 us (2%)
    all_to_all x2, blocking collectives, gather(): return lax.all_to_all(every, ('z', 'x'), 0, 0)  36.2 us
    pallas_call x13, Pallas kernels, call(): pl.pallas_call(kernel, out_shape=[jax.ShapeDtypeStruct(s, d) for s, d in...  25.1 us
    ppermute x4, starting transfers between devices, across(): return lax.ppermute(p, 'y', across_pairs)  8.17 us
    ppermute x5, starting transfers between devices, two(): return lax.ppermute(p, 'y', two_pairs)  7.81 us
    ppermute x3, starting transfers between devices, far(): return lax.ppermute(p, SUB, far_pairs)  5.11 us
    ppermute x5, starting transfers between devices, one(): return lax.ppermute(p, 'y', one_pairs)  4.42 us
    ppermute x3, waiting for transfers between devices, far(): return lax.ppermute(p, SUB, far_pairs)  2.62 us
    ppermute x5, waiting for transfers between devices, two(): return lax.ppermute(p, 'y', two_pairs)  2.53 us
  transfers between devices with their start and end apart: 20, of which 6 were waited for; matrix products, arithmetic and copies ran while one was open for 0% of the time, Pallas kernels for 12%

profile of v5, /device:TPU:32, one launch (start us, length us, event | category | flops | bytes accessed | tf_op | source)
XLA Modules:
  0.0 98.5 jit_solution(14689381151731999129)
XLA Ops:
  0.7 1.0 %pad_maximum_fusion.both = f32[40,2048]{1,0:T(8,128)S(1)} fusion(f32[24,2048]{1,0:T(8,128)} %bitcast.12, f32[16,2048]{1,0:T(8,128)} %bitcast.13), kind=kLoop, calls=%fused_computation | loop fusion | flops 81920 | bytes 655360 | tf_op jit(solution)/shard_map/concatenate | solution.py:354
  3.2 2.4 %collective-permute-start.1 = (f32[48,512]{1,0:T(8,128)S(1)}, f32[48,512]{1,0:T(8,128)S(1)}, u32[]{:S(2)}, u32[]{:S(2)}) collective-permute-start(f32[48,512]{1,0:T(8,128)S(1)} %get-tuple-element.71), channel_id=1, source_target_pairs={{4,8},{12,16},{20,24},{28,32},{36,40},{44,48},{52,56},{60,64},{68,... | collective-permute-start | bytes 294920 | tf_op jit(solution)/shard_map/ppermute | solution.py:381
  5.6 1.6 %collective-permute-start.2 = (f32[40,512]{1,0:T(8,128)S(1)}, f32[40,512]{1,0:T(8,128)S(1)}, u32[]{:S(2)}, u32[]{:S(2)}) collective-permute-start(f32[40,512]{1,0:T(8,128)S(1)} %get-tuple-element.72), channel_id=1, source_target_pairs={{0,1},{1,0},{2,3},{3,2},{4,5},{5,4},{6,7},{7,6},{8,9},{9,8},{10,11... | collective-permute-start | bytes 245768 | tf_op jit(solution)/shard_map/ppermute | solution.py:384
  7.2 2.2 %collective-permute-start.3 = (f32[40,512]{1,0:T(8,128)S(1)}, f32[40,512]{1,0:T(8,128)S(1)}, u32[]{:S(2)}, u32[]{:S(2)}) collective-permute-start(f32[40,512]{1,0:T(8,128)S(1)} %get-tuple-element.73), channel_id=1, source_target_pairs={{0,3},{1,2},{2,1},{3,0},{4,7},{5,6},{6,5},{7,4},{8,11},{9,10},{10,... | collective-permute-start | bytes 245768 | tf_op jit(solution)/shard_map/ppermute | solution.py:390
  9.4 3.7 %spread_coupling.1 = (bf16[128,2048]{1,0:T(8,128)(2,1)S(1)}, bf16[128,2048]{1,0:T(8,128)(2,1)S(1)}, f32[8,2048]{1,0:T(8,128)S(1)}, bf16[1792,2048]{1,0:T(8,128)(2,1)S(1)}) custom-call(s32[1,128]{1,0:T(1,128)S(1)} %get-tuple-element.69.ints, f32[40,2048]{1,0:T(8,128)S(1)} %pad_maximum_fusion.both, bf16[2048,2048]{1,0:T(8,128)(2,1)} %bitcast.10), custom_call_target="tpu_custom_call" | custom-call | flops 3000000 | bytes 10500000 | tf_op jit(solution)/shard_map/spread_coupling/pallas_call | solution.py:339
  13.1 1.0 %first_vector.1 = (f32[16,2048]{1,0:T(8,128)S(1)}, f32[16,128]{1,0:T(8,128)S(1)}) custom-call(s32[1,128]{1,0:T(1,128)S(1)} %get-tuple-element.69.ints, f32[40,2048]{1,0:T(8,128)S(1)} %pad_maximum_fusion.both, f32[48,512]{1,0:T(8,128)S(1)} %collective-permute-done.i0, f32[48,512]{1,0:T(8,128)S(1)} %collective-permute-done.1.i1, ...), custom_call_target="tpu_custom_call" | custom-call | flops 1000000 | bytes 3500000 | tf_op jit(solution)/shard_map/first_vector/pallas_call | solution.py:339
  14.2 1.5 %collective-permute-start.6 = (f32[16,128]{1,0:T(8,128)S(1)}, f32[16,128]{1,0:T(8,128)S(1)}, u32[]{:S(2)}, u32[]{:S(2)}) collective-permute-start(f32[16,128]{1,0:T(8,128)S(1)} %get-tuple-element.78), channel_id=1, source_target_pairs={{0,2},{1,3},{2,0},{3,1},{4,6},{5,7},{6,4},{7,5},{8,10},{9,11},{10,... | collective-permute-start | bytes 24584 | tf_op jit(solution)/shard_map/ppermute | solution.py:387
  15.6 1.4 %collective-permute-start.5 = (f32[16,128]{1,0:T(8,128)S(1)}, f32[16,128]{1,0:T(8,128)S(1)}, u32[]{:S(2)}, u32[]{:S(2)}) collective-permute-start(f32[16,128]{1,0:T(8,128)S(1)} %get-tuple-element.78), channel_id=1, source_target_pairs={{0,1},{1,0},{2,3},{3,2},{4,5},{5,4},{6,7},{7,6},{8,9},{9,8},{10,11... | collective-permute-start | bytes 24584 | tf_op jit(solution)/shard_map/ppermute | solution.py:384
  17.0 1.3 %collective-permute-start.4 = (f32[16,128]{1,0:T(8,128)S(1)}, f32[16,128]{1,0:T(8,128)S(1)}, u32[]{:S(2)}, u32[]{:S(2)}) collective-permute-start(f32[16,128]{1,0:T(8,128)S(1)} %get-tuple-element.78), channel_id=1, source_target_pairs={{0,3},{1,2},{2,1},{3,0},{4,7},{5,6},{6,5},{7,4},{8,11},{9,10},{10,... | collective-permute-start | bytes 24584 | tf_op jit(solution)/shard_map/ppermute | solution.py:390
  18.3 2.5 %local_product.2 = (f32[16,2048]{1,0:T(8,128)S(1)}, f32[16,512]{1,0:T(8,128)S(1)}, f32[16,512]{1,0:T(8,128)S(1)}, f32[16,512]{1,0:T(8,128)S(1)}, f32[16,512]{1,0:T(8,128)S(1)}, /*index=5*/bf16[256,2048]{1,0:T(8,128)(2,1)S(1)}) custom-call(s32[1,128]{1,0:T(1,128)S(1)} %get-tuple-element.69.ints, f32[16,2048]{1,0:T(8,128)S(1)} %get-tuple-element.79.v.v0, ...), custom_call_target="tpu_custom_call" | custom-call | flops 2000000 | bytes 7000000 | tf_op jit(solution)/shard_map/local_product/pallas_call | solution.py:339
  20.8 1.0 %collective-permute-done.4 = f32[16,128]{1,0:T(8,128)S(1)} collective-permute-done((f32[16,128]{1,0:T(8,128)S(1)}, f32[16,128]{1,0:T(8,128)S(1)}, u32[]{:S(2)}, u32[]{:S(2)}) %collective-permute-start.4) | collective-permute-done | bytes 8224 | tf_op jit(solution)/shard_map/ppermute | solution.py:390
  21.9 20.4 %all_to_all.10.t = f32[32,16,128]{2,1,0:T(8,128)S(1)} all-to-all(f32[32,16,128]{2,1,0:T(8,128)S(1)} %broadcast_in_dim.22), channel_id=1, replica_groups=mesh['z'=8,'x'=4,'c'=2,'y'=4] {'z','x'}, dimensions={0} | all-to-all | bytes 524288 | tf_op jit(solution)/shard_map/all_to_all | solution.py:394
  42.3 3.5 %coarse_half.2 = (f32[16,1152]{1,0:T(8,128)S(1)}, bf16[512,2048]{1,0:T(8,128)(2,1)S(1)}, bf16[512,2048]{1,0:T(8,128)(2,1)S(1)}, f32[32,128]{1,0:T(8,128)S(1)}, bf16[4096,256]{1,0:T(8,128)(2,1)S(1)}) custom-call(f32[32,16,128]{2,1,0:T(8,128)S(1)} %all_to_all.10.t, f32[16,512]{1,0:T(8,128)S(1)} %get-tuple-element.93.near, f32[512,2048]{1,0:T(8,128)S(1)} %copy-done), custom_call_target="tpu_custom_call" | custom-call | flops 4000000 | bytes 14000000 | tf_op jit(solution)/shard_map/coarse_half/pallas_call | solution.py:339
  45.9 2.5 %picked_columns.1 = (bf16[512,384]{1,0:T(8,128)(2,1)S(1)}, bf16[512,384]{1,0:T(8,128)(2,1)S(1)}) custom-call(f32[16,128]{1,0:T(8,128)S(1)} %add_add_fusion.1.pay, bf16[512,2048]{1,0:T(8,128)(2,1)S(1)} %get-tuple-element.98.f_hi.rest_0_, bf16[512,2048]{1,0:T(8,128)(2,1)S(1)} %get-tuple-element.99.f_lo.rest_1_), custom_call_target="tpu_custom_call" | custom-call | flops 2500000 | bytes 8750000 | tf_op jit(solution)/shard_map/picked_columns/pallas_call | solution.py:339
  49.5 1.2 %collective-permute-start.11 = (f32[16,896]{1,0:T(8,128)S(1)}, f32[16,896]{1,0:T(8,128)S(1)}, u32[]{:S(2)}, u32[]{:S(2)}) collective-permute-start(f32[16,896]{1,0:T(8,128)S(1)} %get-tuple-element.104), channel_id=1, source_target_pairs={{0,3},{1,2},{2,1},{3,0},{4,7},{5,6},{6,5},{7,4},{8,11},{9,10},{10,... | collective-permute-start | bytes 172040 | tf_op jit(solution)/shard_map/ppermute | solution.py:390
  50.7 1.7 %collective-permute-start.8 = (f32[16,512]{1,0:T(8,128)S(1)}, f32[16,512]{1,0:T(8,128)S(1)}, u32[]{:S(2)}, u32[]{:S(2)}) collective-permute-start(f32[16,512]{1,0:T(8,128)S(1)} %get-tuple-element.95), channel_id=1, source_target_pairs={{4,8},{12,16},{20,24},{28,32},{36,40},{44,48},{52,56},{60,64},{68,... | collective-permute-start | bytes 98312 | tf_op jit(solution)/shard_map/ppermute | solution.py:381
  52.4 2.4 %collective-permute-start.10 = (f32[16,384]{1,0:T(8,128)S(1)}, f32[16,384]{1,0:T(8,128)S(1)}, u32[]{:S(2)}, u32[]{:S(2)}) collective-permute-start(f32[16,384]{1,0:T(8,128)S(1)} %get-tuple-element.102.p0), channel_id=1, source_target_pairs={{0,2},{1,3},{2,0},{3,1},{4,6},{5,7},{6,4},{7,5},{8,10},{9,11},{10,... | collective-permute-start | bytes 73736 | tf_op jit(solution)/shard_map/ppermute | solution.py:387
  54.8 1.4 %jumped_coupling.1 = (bf16[256,2048]{1,0:T(8,128)(2,1)S(1)}, bf16[256,2048]{1,0:T(8,128)(2,1)S(1)}) custom-call(s32[1,128]{1,0:T(1,128)S(1)} %get-tuple-element.69.ints, f32[40,2048]{1,0:T(8,128)S(1)} %pad_maximum_fusion.both, f32[48,512]{1,0:T(8,128)S(1)} %collective-permute-done.i0, f32[48,512]{1,0:T(8,128)S(1)} %collective-permute-done.1.i1, ...), custom_call_target="tpu_custom_call" | custom-call | flops 1200000 | bytes 4200000 | tf_op jit(solution)/shard_map/jumped_coupling/pallas_call | solution.py:339
  56.2 1.5 %collective-permute-done.10.p2 = f32[16,384]{1,0:T(8,128)S(1)} collective-permute-done((f32[16,384]{1,0:T(8,128)S(1)}, f32[16,384]{1,0:T(8,128)S(1)}, u32[]{:S(2)}, u32[]{:S(2)}) %collective-permute-start.10) | collective-permute-done | bytes 24608 | tf_op jit(solution)/shard_map/ppermute | solution.py:387
  57.7 1.5 %next_vector.1 = (f32[16,2048]{1,0:T(8,128)S(1)}, f32[16,128]{1,0:T(8,128)S(1)}) custom-call(s32[1,128]{1,0:T(1,128)S(1)} %get-tuple-element.69.ints, f32[16,2048]{1,0:T(8,128)S(1)} %get-tuple-element.87.z0, f32[16,1152]{1,0:T(8,128)S(1)} %collective-permute-done.7.got, f32[16,512]{1,0:T(8,128)S(1)} %collective-permute-done.8.far, ...), custom_call_target="tpu_custom_call" | custom-call | flops 1600000 | bytes 5600000 | tf_op jit(solution)/shard_map/next_vector/pallas_call | solution.py:339
  59.2 2.5 %collective-permute-start.14 = (f32[16,128]{1,0:T(8,128)S(1)}, f32[16,128]{1,0:T(8,128)S(1)}, u32[]{:S(2)}, u32[]{:S(2)}) collective-permute-start(f32[16,128]{1,0:T(8,128)S(1)} %get-tuple-element.107), channel_id=1, source_target_pairs={{0,2},{1,3},{2,0},{3,1},{4,6},{5,7},{6,4},{7,5},{8,10},{9,11},{10,... | collective-permute-start | bytes 24584 | tf_op jit(solution)/shard_map/ppermute | solution.py:387
  62.1 1.3 %collective-permute-start.12 = (f32[16,128]{1,0:T(8,128)S(1)}, f32[16,128]{1,0:T(8,128)S(1)}, u32[]{:S(2)}, u32[]{:S(2)}) collective-permute-start(f32[16,128]{1,0:T(8,128)S(1)} %get-tuple-element.107), channel_id=1, source_target_pairs={{0,3},{1,2},{2,1},{3,0},{4,7},{5,6},{6,5},{7,4},{8,11},{9,10},{10,... | collective-permute-start | bytes 24584 | tf_op jit(solution)/shard_map/ppermute | solution.py:390
  63.4 2.1 %local_product.3 = (f32[16,2048]{1,0:T(8,128)S(1)}, f32[16,512]{1,0:T(8,128)S(1)}, f32[16,512]{1,0:T(8,128)S(1)}, f32[16,512]{1,0:T(8,128)S(1)}, f32[16,512]{1,0:T(8,128)S(1)}, /*index=5*/f32[16,128]{1,0:T(8,128)S(1)}) custom-call(s32[1,128]{1,0:T(1,128)S(1)} %get-tuple-element.69.ints, f32[16,2048]{1,0:T(8,128)S(1)} %get-tuple-element.108.v.v1, ...), custom_call_target="tpu_custom_call" | custom-call | flops 2000000 | bytes 7000000 | tf_op jit(solution)/shard_map/local_product/pallas_call | solution.py:339
  65.5 1.5 %collective-permute-done.12 = f32[16,128]{1,0:T(8,128)S(1)} collective-permute-done((f32[16,128]{1,0:T(8,128)S(1)}, f32[16,128]{1,0:T(8,128)S(1)}, u32[]{:S(2)}, u32[]{:S(2)}) %collective-permute-start.12) | collective-permute-done | bytes 8224 | tf_op jit(solution)/shard_map/ppermute | solution.py:390
  67.0 15.8 %all_to_all.11.t = f32[32,16,128]{2,1,0:T(8,128)S(1)} all-to-all(f32[32,16,128]{2,1,0:T(8,128)S(1)} %broadcast_in_dim.23), channel_id=1, replica_groups=mesh['z'=8,'x'=4,'c'=2,'y'=4] {'z','x'}, dimensions={0} | all-to-all | bytes 524288 | tf_op jit(solution)/shard_map/all_to_all | solution.py:394
  82.8 3.0 %coarse_half.3.own = f32[16,1152]{1,0:T(8,128)S(1)} custom-call(f32[32,16,128]{2,1,0:T(8,128)S(1)} %all_to_all.11.t, f32[16,512]{1,0:T(8,128)S(1)} %get-tuple-element.123.near, bf16[512,2048]{1,0:T(8,128)(2,1)S(1)} %get-tuple-element.98.f_hi.rest_0_, bf16[512,2048]{1,0:T(8,128)(2,1)S(1)} %get-tuple-element.99.f_lo.rest_1_, ...), custom_call_target="tpu_custom_call" | custom-call | flops 4000000 | bytes 14000000 | tf_op jit(solution)/shard_map/coarse_half/pallas_call | solution.py:339
  85.9 1.3 %collective-permute-done.15.got = f32[16,1152]{1,0:T(8,128)S(1)} collective-permute-done((f32[16,1152]{1,0:T(8,128)S(1)}, f32[16,1152]{1,0:T(8,128)S(1)}, u32[]{:S(2)}, u32[]{:S(2)}) %collective-permute-start.15) | collective-permute-done | bytes 73760 | tf_op jit(solution)/shard_map/ppermute | solution.py:378
  88.6 1.8 %collective-permute-start.19 = (f32[16,896]{1,0:T(8,128)S(1)}, f32[16,896]{1,0:T(8,128)S(1)}, u32[]{:S(2)}, u32[]{:S(2)}) collective-permute-start(f32[16,896]{1,0:T(8,128)S(1)} %get-tuple-element.131), channel_id=1, source_target_pairs={{0,3},{1,2},{2,1},{3,0},{4,7},{5,6},{6,5},{7,4},{8,11},{9,10},{10,... | collective-permute-start | bytes 172040 | tf_op jit(solution)/shard_map/ppermute | solution.py:390
  90.4 1.0 %collective-permute-start.16 = (f32[16,512]{1,0:T(8,128)S(1)}, f32[16,512]{1,0:T(8,128)S(1)}, u32[]{:S(2)}, u32[]{:S(2)}) collective-permute-start(f32[16,512]{1,0:T(8,128)S(1)} %get-tuple-element.126), channel_id=1, source_target_pairs={{4,8},{12,16},{20,24},{28,32},{36,40},{44,48},{52,56},{60,64},{68,... | collective-permute-start | bytes 98312 | tf_op jit(solution)/shard_map/ppermute | solution.py:381
  91.4 1.8 %collective-permute-start.18 = (f32[16,384]{1,0:T(8,128)S(1)}, f32[16,384]{1,0:T(8,128)S(1)}, u32[]{:S(2)}, u32[]{:S(2)}) collective-permute-start(f32[16,384]{1,0:T(8,128)S(1)} %get-tuple-element.129.p0), channel_id=1, source_target_pairs={{0,2},{1,3},{2,0},{3,1},{4,6},{5,7},{6,4},{7,5},{8,10},{9,11},{10,... | collective-permute-start | bytes 73736 | tf_op jit(solution)/shard_map/ppermute | solution.py:387
  93.2 2.6 %collective-permute-done.16.far = f32[16,512]{1,0:T(8,128)S(1)} collective-permute-done((f32[16,512]{1,0:T(8,128)S(1)}, f32[16,512]{1,0:T(8,128)S(1)}, u32[]{:S(2)}, u32[]{:S(2)}) %collective-permute-start.16) | collective-permute-done | bytes 32800 | tf_op jit(solution)/shard_map/ppermute | solution.py:381
  96.7 1.8 %finish.1 = (f32[16,2048]{1,0:T(8,128)}, f32[16,2048]{1,0:T(8,128)}) custom-call(s32[1,128]{1,0:T(1,128)S(1)} %get-tuple-element.69.ints, f32[16,2048]{1,0:T(8,128)S(1)} %get-tuple-element.116.z1, f32[16,1152]{1,0:T(8,128)S(1)} %collective-permute-done.15.got, f32[16,512]{1,0:T(8,128)S(1)} %collective-permute-done.16.far, ...), custom_call_target="tpu_custom_call" | custom-call | flops 1900000 | bytes 6650000 | tf_op jit(solution)/shard_map/finish/pallas_call | solution.py:339
  (32 shorter events, 5.7 us)
Async XLA Ops:
  3.1 10.0 %collective-permute-start = (f32[48,512]{1,0:T(8,128)S(1)}, f32[48,512]{1,0:T(8,128)S(1)}, u32[]{:S(2)}, u32[]{:S(2)}) collective-permute-start(f32[48,512]{1,0:T(8,128)S(1)} %get-tuple-element.70), channel_id=1, source_target_pairs={{0,4},{4,0},{1,5},{5,1},{2,6},{6,2},{3,7},{7,3},{8,12},{12,8},{9,1... | collective-permute-start | bytes 294920 | tf_op jit(solution)/shard_map/ppermute | solution.py:378
  3.2 9.9 %collective-permute-start.1 = (f32[48,512]{1,0:T(8,128)S(1)}, f32[48,512]{1,0:T(8,128)S(1)}, u32[]{:S(2)}, u32[]{:S(2)}) collective-permute-start(f32[48,512]{1,0:T(8,128)S(1)} %get-tuple-element.71), channel_id=1, source_target_pairs={{4,8},{12,16},{20,24},{28,32},{36,40},{44,48},{52,56},{60,64},{68,... | collective-permute-start | bytes 294920 | tf_op jit(solution)/shard_map/ppermute | solution.py:381
  5.6 7.5 %collective-permute-start.2 = (f32[40,512]{1,0:T(8,128)S(1)}, f32[40,512]{1,0:T(8,128)S(1)}, u32[]{:S(2)}, u32[]{:S(2)}) collective-permute-start(f32[40,512]{1,0:T(8,128)S(1)} %get-tuple-element.72), channel_id=1, source_target_pairs={{0,1},{1,0},{2,3},{3,2},{4,5},{5,4},{6,7},{7,6},{8,9},{9,8},{10,11... | collective-permute-start | bytes 245768 | tf_op jit(solution)/shard_map/ppermute | solution.py:384
  7.2 5.9 %collective-permute-start.3 = (f32[40,512]{1,0:T(8,128)S(1)}, f32[40,512]{1,0:T(8,128)S(1)}, u32[]{:S(2)}, u32[]{:S(2)}) collective-permute-start(f32[40,512]{1,0:T(8,128)S(1)} %get-tuple-element.73), channel_id=1, source_target_pairs={{0,3},{1,2},{2,1},{3,0},{4,7},{5,6},{6,5},{7,4},{8,11},{9,10},{10,... | collective-permute-start | bytes 245768 | tf_op jit(solution)/shard_map/ppermute | solution.py:390
  14.2 6.6 %collective-permute-start.6 = (f32[16,128]{1,0:T(8,128)S(1)}, f32[16,128]{1,0:T(8,128)S(1)}, u32[]{:S(2)}, u32[]{:S(2)}) collective-permute-start(f32[16,128]{1,0:T(8,128)S(1)} %get-tuple-element.78), channel_id=1, source_target_pairs={{0,2},{1,3},{2,0},{3,1},{4,6},{5,7},{6,4},{7,5},{8,10},{9,11},{10,... | collective-permute-start | bytes 24584 | tf_op jit(solution)/shard_map/ppermute | solution.py:387
  15.6 5.2 %collective-permute-start.5 = (f32[16,128]{1,0:T(8,128)S(1)}, f32[16,128]{1,0:T(8,128)S(1)}, u32[]{:S(2)}, u32[]{:S(2)}) collective-permute-start(f32[16,128]{1,0:T(8,128)S(1)} %get-tuple-element.78), channel_id=1, source_target_pairs={{0,1},{1,0},{2,3},{3,2},{4,5},{5,4},{6,7},{7,6},{8,9},{9,8},{10,11... | collective-permute-start | bytes 24584 | tf_op jit(solution)/shard_map/ppermute | solution.py:384
  17.0 4.9 %collective-permute-start.4 = (f32[16,128]{1,0:T(8,128)S(1)}, f32[16,128]{1,0:T(8,128)S(1)}, u32[]{:S(2)}, u32[]{:S(2)}) collective-permute-start(f32[16,128]{1,0:T(8,128)S(1)} %get-tuple-element.78), channel_id=1, source_target_pairs={{0,3},{1,2},{2,1},{3,0},{4,7},{5,6},{6,5},{7,4},{8,11},{9,10},{10,... | collective-permute-start | bytes 24584 | tf_op jit(solution)/shard_map/ppermute | solution.py:390
  18.3 24.0 %copy-start = (f32[512,2048]{1,0:T(8,128)S(1)}, f32[512,2048]{1,0:T(8,128)}, u32[]{:S(2)}) copy-start(f32[512,2048]{1,0:T(8,128)} %rest_0_.1) | copy-start | bytes 12582916
  45.8 2.6 %collective-permute-start.7 = (f32[16,1152]{1,0:T(8,128)S(1)}, f32[16,1152]{1,0:T(8,128)S(1)}, u32[]{:S(2)}, u32[]{:S(2)}) collective-permute-start(f32[16,1152]{1,0:T(8,128)S(1)} %get-tuple-element.94.own), channel_id=1, source_target_pairs={{0,4},{4,0},{1,5},{5,1},{2,6},{6,2},{3,7},{7,3},{8,12},{12,8},{9,1... | collective-permute-start | bytes 221192 | tf_op jit(solution)/shard_map/ppermute | solution.py:378
  49.1 8.6 %collective-permute-start.9 = (f32[16,896]{1,0:T(8,128)S(1)}, f32[16,896]{1,0:T(8,128)S(1)}, u32[]{:S(2)}, u32[]{:S(2)}) collective-permute-start(f32[16,896]{1,0:T(8,128)S(1)} %get-tuple-element.103), channel_id=1, source_target_pairs={{0,1},{1,0},{2,3},{3,2},{4,5},{5,4},{6,7},{7,6},{8,9},{9,8},{10,11... | collective-permute-start | bytes 172040 | tf_op jit(solution)/shard_map/ppermute | solution.py:384
  49.5 8.3 %collective-permute-start.11 = (f32[16,896]{1,0:T(8,128)S(1)}, f32[16,896]{1,0:T(8,128)S(1)}, u32[]{:S(2)}, u32[]{:S(2)}) collective-permute-start(f32[16,896]{1,0:T(8,128)S(1)} %get-tuple-element.104), channel_id=1, source_target_pairs={{0,3},{1,2},{2,1},{3,0},{4,7},{5,6},{6,5},{7,4},{8,11},{9,10},{10,... | collective-permute-start | bytes 172040 | tf_op jit(solution)/shard_map/ppermute | solution.py:390
  50.7 5.5 %collective-permute-start.8 = (f32[16,512]{1,0:T(8,128)S(1)}, f32[16,512]{1,0:T(8,128)S(1)}, u32[]{:S(2)}, u32[]{:S(2)}) collective-permute-start(f32[16,512]{1,0:T(8,128)S(1)} %get-tuple-element.95), channel_id=1, source_target_pairs={{4,8},{12,16},{20,24},{28,32},{36,40},{44,48},{52,56},{60,64},{68,... | collective-permute-start | bytes 98312 | tf_op jit(solution)/shard_map/ppermute | solution.py:381
  52.4 5.3 %collective-permute-start.10 = (f32[16,384]{1,0:T(8,128)S(1)}, f32[16,384]{1,0:T(8,128)S(1)}, u32[]{:S(2)}, u32[]{:S(2)}) collective-permute-start(f32[16,384]{1,0:T(8,128)S(1)} %get-tuple-element.102.p0), channel_id=1, source_target_pairs={{0,2},{1,3},{2,0},{3,1},{4,6},{5,7},{6,4},{7,5},{8,10},{9,11},{10,... | collective-permute-start | bytes 73736 | tf_op jit(solution)/shard_map/ppermute | solution.py:387
  59.2 6.2 %collective-permute-start.14 = (f32[16,128]{1,0:T(8,128)S(1)}, f32[16,128]{1,0:T(8,128)S(1)}, u32[]{:S(2)}, u32[]{:S(2)}) collective-permute-start(f32[16,128]{1,0:T(8,128)S(1)} %get-tuple-element.107), channel_id=1, source_target_pairs={{0,2},{1,3},{2,0},{3,1},{4,6},{5,7},{6,4},{7,5},{8,10},{9,11},{10,... | collective-permute-start | bytes 24584 | tf_op jit(solution)/shard_map/ppermute | solution.py:387
  61.7 3.8 %collective-permute-start.13 = (f32[16,128]{1,0:T(8,128)S(1)}, f32[16,128]{1,0:T(8,128)S(1)}, u32[]{:S(2)}, u32[]{:S(2)}) collective-permute-start(f32[16,128]{1,0:T(8,128)S(1)} %get-tuple-element.107), channel_id=1, source_target_pairs={{0,1},{1,0},{2,3},{3,2},{4,5},{5,4},{6,7},{7,6},{8,9},{9,8},{10,11... | collective-permute-start | bytes 24584 | tf_op jit(solution)/shard_map/ppermute | solution.py:384
  62.1 4.9 %collective-permute-start.12 = (f32[16,128]{1,0:T(8,128)S(1)}, f32[16,128]{1,0:T(8,128)S(1)}, u32[]{:S(2)}, u32[]{:S(2)}) collective-permute-start(f32[16,128]{1,0:T(8,128)S(1)} %get-tuple-element.107), channel_id=1, source_target_pairs={{0,3},{1,2},{2,1},{3,0},{4,7},{5,6},{6,5},{7,4},{8,11},{9,10},{10,... | collective-permute-start | bytes 24584 | tf_op jit(solution)/shard_map/ppermute | solution.py:390
  85.8 1.3 %collective-permute-start.15 = (f32[16,1152]{1,0:T(8,128)S(1)}, f32[16,1152]{1,0:T(8,128)S(1)}, u32[]{:S(2)}, u32[]{:S(2)}) collective-permute-start(f32[16,1152]{1,0:T(8,128)S(1)} %coarse_half.3.own), channel_id=1, source_target_pairs={{0,4},{4,0},{1,5},{5,1},{2,6},{6,2},{3,7},{7,3},{8,12},{12,8},{9,1... | collective-permute-start | bytes 221192 | tf_op jit(solution)/shard_map/ppermute | solution.py:378
  87.9 8.9 %collective-permute-start.17 = (f32[16,896]{1,0:T(8,128)S(1)}, f32[16,896]{1,0:T(8,128)S(1)}, u32[]{:S(2)}, u32[]{:S(2)}) collective-permute-start(f32[16,896]{1,0:T(8,128)S(1)} %get-tuple-element.130), channel_id=1, source_target_pairs={{0,1},{1,0},{2,3},{3,2},{4,5},{5,4},{6,7},{7,6},{8,9},{9,8},{10,11... | collective-permute-start | bytes 172040 | tf_op jit(solution)/shard_map/ppermute | solution.py:384
  88.6 8.1 %collective-permute-start.19 = (f32[16,896]{1,0:T(8,128)S(1)}, f32[16,896]{1,0:T(8,128)S(1)}, u32[]{:S(2)}, u32[]{:S(2)}) collective-permute-start(f32[16,896]{1,0:T(8,128)S(1)} %get-tuple-element.131), channel_id=1, source_target_pairs={{0,3},{1,2},{2,1},{3,0},{4,7},{5,6},{6,5},{7,4},{8,11},{9,10},{10,... | collective-permute-start | bytes 172040 | tf_op jit(solution)/shard_map/ppermute | solution.py:390
  90.4 5.4 %collective-permute-start.16 = (f32[16,512]{1,0:T(8,128)S(1)}, f32[16,512]{1,0:T(8,128)S(1)}, u32[]{:S(2)}, u32[]{:S(2)}) collective-permute-start(f32[16,512]{1,0:T(8,128)S(1)} %get-tuple-element.126), channel_id=1, source_target_pairs={{4,8},{12,16},{20,24},{28,32},{36,40},{44,48},{52,56},{60,64},{68,... | collective-permute-start | bytes 98312 | tf_op jit(solution)/shard_map/ppermute | solution.py:381
  91.4 5.3 %collective-permute-start.18 = (f32[16,384]{1,0:T(8,128)S(1)}, f32[16,384]{1,0:T(8,128)S(1)}, u32[]{:S(2)}, u32[]{:S(2)}) collective-permute-start(f32[16,384]{1,0:T(8,128)S(1)} %get-tuple-element.129.p0), channel_id=1, source_target_pairs={{0,2},{1,3},{2,0},{3,1},{4,6},{5,7},{6,4},{7,5},{8,10},{9,11},{10,... | collective-permute-start | bytes 73736 | tf_op jit(solution)/shard_map/ppermute | solution.py:387
